TPU v7x, 32 devices: a whole 2x2x4 slice. The times are simulated.
32 devices in a mesh: dp: 8 (over z, x), mp: 4 (over y, core).
Axes of the slice: x: 2, y: 2, z: 4, core: 2. Of those that a mesh axis runs over, the one named last changes fastest.
Arguments:
- blocks: bfloat16 [32, 512, 512], P('dp'), may hold values from -6 to 6
- block_segment: int32 [32, 512], P('dp'), may hold values from 0 to 7, never falling along the last dimension, each value on 1 to 128 neighbouring positions
- upstream: bfloat16 [32, 512, 512], P('dp'), may hold values from -6 to 6
- attend_master: float32 [3, 512, 512], P(None, 'dp', 'mp'), may hold values from -0.25 to 0.25
- attend_first: float32 [3, 512, 512], P(None, 'dp', 'mp'), may hold values from -768 to 768
- attend_second: float32 [3, 512, 512], P(None, 'dp', 'mp'), may hold values from 10928.128 to 43696.13
- mixing_master: float32 [512, 512], P('mp', 'dp'), may hold values from -2 to 2
- mixing_first: float32 [512, 512], P('mp', 'dp'), may hold values from -96 to 96
- mixing_second: float32 [512, 512], P('mp', 'dp'), may hold values from 170.752 to 682.752
- expand_master: float32 [512, 2048], P('dp', 'mp'), may hold values from -0.25 to 0.25
- expand_first: float32 [512, 2048], P('dp', 'mp'), may hold values from -256 to 256
- expand_second: float32 [512, 2048], P('dp', 'mp'), may hold values from 1359.872 to 5455.872
- shrink_master: float32 [2048, 512], P('mp', 'dp'), may hold values from -0.125 to 0.125
- shrink_first: float32 [2048, 512], P('mp', 'dp'), may hold values from -512 to 512
- shrink_second: float32 [2048, 512], P('mp', 'dp'), may hold values from 5455.872 to 21839.871
- gains_master: float32 [2, 512], P(None, 'dp'), may hold values from 0.5 to 1.5
- gains_first: float32 [2, 512], P(None, 'dp'), may hold values from -896 to 896
- gains_second: float32 [2, 512], P(None, 'dp'), may hold values from 16384 to 65536
Outputs:
- result: bfloat16 [32, 512, 512], P('dp')
- blocks_grad: float32 [32, 512, 512], P('dp')
- attend_weight: float32 [3, 512, 512], P(None, 'dp', 'mp')
- attend_moment: float32 [3, 512, 512], P(None, 'dp', 'mp')
- attend_square: float32 [3, 512, 512], P(None, 'dp', 'mp')
- attend_copy: bfloat16 [3, 512, 512], P(None, 'dp', 'mp')
- mixing_weight: float32 [512, 512], P('mp', 'dp')
- mixing_moment: float32 [512, 512], P('mp', 'dp')
- mixing_square: float32 [512, 512], P('mp', 'dp')
- mixing_copy: bfloat16 [512, 512], P('mp', 'dp')
- expand_weight: float32 [512, 2048], P('dp', 'mp')
- expand_moment: float32 [512, 2048], P('dp', 'mp')
- expand_square: float32 [512, 2048], P('dp', 'mp')
- expand_copy: bfloat16 [512, 2048], P('dp', 'mp')
- shrink_weight: float32 [2048, 512], P('mp', 'dp')
- shrink_moment: float32 [2048, 512], P('mp', 'dp')
- shrink_square: float32 [2048, 512], P('mp', 'dp')
- shrink_copy: bfloat16 [2048, 512], P('mp', 'dp')
- gains_weight: float32 [2, 512], P(None, 'dp')
- gains_moment: float32 [2, 512], P(None, 'dp')
- gains_square: float32 [2, 512], P(None, 'dp')
- gains_copy: bfloat16 [2, 512], P(None, 'dp')
Inputs may be any that keep to these rules, and one draw needn't show every extreme that they name: `block_segment`: in each row of 512 blocks the ids never fall and each id covers 1 to 128 consecutive blocks.
All inputs are finite; a program needn't handle non-finite values.
Results may differ from a plain program's by a relative error of at most 0.019.
Values may be sent and summed in bfloat16 or wider, within the bound.
No kernel may reach another device: no remote copies, remote signals or barrier semaphores. Data moves between devices by JAX's collectives and lax.ppermute only.
A program may use at most 128 MiB of HBM per device.

v0:
```python
import functools

import jax
import jax.numpy as jnp
from jax import lax
from jax.experimental import pallas as pl
from jax.experimental.pallas import tpu as pltpu
from jax.sharding import PartitionSpec as P

HD = 64
STEP = 5
TILE = 128
EPS = 1e-06
GELU = 0.79788456
CUBIC = 0.044715
BF = jnp.bfloat16
F32 = jnp.float32
VMEM_LIMIT = 56 * 1024 * 1024


def nn(a, b):
    return lax.dot_general(a, b, (((1,), (0,)), ((), ())), preferred_element_type=F32)


def nt(a, b):
    return lax.dot_general(a, b, (((1,), (1,)), ((), ())), preferred_element_type=F32)


def tn(a, b):
    return lax.dot_general(a, b, (((0,), (0,)), ((), ())), preferred_element_type=F32)


def root_scale(values):
    return lax.rsqrt(jnp.mean(values * values, axis=-1, keepdims=True) + EPS)


def call(body, outs, ins, scratch=(), prefetch=(), flops=0, moved=0, trans=0, maps=None, grid=(1,)):
    def whole(shape):
        return pl.BlockSpec(shape, lambda i, *s, n=len(shape): (0,) * n)

    maps = maps or {}
    in_specs = [maps.get(k) or whole(a.shape) for k, a in enumerate(ins)]
    out_specs = [maps.get(("out", k)) or whole(o.shape) for k, o in enumerate(outs)]
    return pl.pallas_call(
        body,
        out_shape=outs,
        grid_spec=pltpu.PrefetchScalarGridSpec(
            num_scalar_prefetch=len(prefetch),
            grid=grid,
            in_specs=in_specs,
            out_specs=out_specs,
            scratch_shapes=list(scratch),
        ),
        compiler_params=pltpu.CompilerParams(vmem_limit_bytes=VMEM_LIMIT),
        cost_estimate=pl.CostEstimate(flops=flops, bytes_accessed=moved, transcendentals=trans),
    )(*prefetch, *ins)


def pieces_of(refs, count, rows):
    half = count // 2
    for core in range(2):
        own, over_x, over_y, far_low, far_high = refs[5 * core : 5 * core + 5]
        yield core, 0, 0, count, own
        yield core, 1, 0, count, over_x
        yield 2 + core, 0, 0, count, over_y
        yield 2 + core, 1, 0, half, far_low
        yield 2 + core, 1, half, count - half, far_high


def place(refs, z, x, count, rows, store):
    for group, x_off, first, blocks, ref in pieces_of(refs, count, rows):
        x_at = lax.rem(x + x_off, 2)
        for k in range(blocks):
            z_at = lax.rem(z + (count - (first + k)), count)
            at = pl.multiple_of((z_at * 2 + x_at) * rows, rows)
            store(group, at, ref[k * rows : (k + 1) * rows, :])


def in_relative_rows(source, target, z, x, count, rows):
    half = count // 2
    for k in range(count):
        z_at = lax.rem(z + k, count)
        for x_off in range(2):
            x_at = lax.rem(x + x_off, 2)
            at = pl.multiple_of((z_at * 2 + x_at) * rows, rows)
            to = ((k // half) * 2 + x_off) * half * rows + (k % half) * rows
            target[to : to + rows, :] = source[pl.ds(at, rows), :]


def attention_kernel(count, rows, place_ref, x_ref, seg_col, seg_row, *refs):
    pieces, (h_ref, qkvo, p_ref, w_ref) = refs[:10], refs[10:]
    z, x = place_ref[0], place_ref[1]

    def store(group, at, block):
        for part in range(4):
            w_ref[pl.ds(at, rows), part * 512 + group * 128 : part * 512 + group * 128 + 128] = block[
                :, part * 128 : part * 128 + 128
            ]

    place(pieces, z, x, count, rows, store)
    states = x_ref[0].astype(F32)
    unit = (states * root_scale(states)).astype(BF)
    for part in range(3):
        qkvo[:, part * 512 : part * 512 + 512] = nn(unit, w_ref[:, part * 512 : part * 512 + 512]).astype(BF)
    lane = lax.broadcasted_iota(jnp.int32, (1, 128), 1)
    sides = [jnp.where(lane // HD == j, HD**-0.5, 0.0).astype(BF) for j in range(2)]
    tiles = qkvo.shape[0] // TILE
    for i in range(tiles):
        low = max(0, i - 1) * TILE
        wide = min(tiles, i + 2) * TILE - low
        mask = seg_col[i * TILE : (i + 1) * TILE, :] == seg_row[:, low : low + wide]
        for m in range(4):
            q = qkvo[i * TILE : (i + 1) * TILE, m * 128 : m * 128 + 128]
            k = qkvo[low : low + wide, 512 + m * 128 : 512 + m * 128 + 128]
            v = qkvo[low : low + wide, 1024 + m * 128 : 1024 + m * 128 + 128]
            o = []
            for j in range(2):
                s = jnp.where(mask, nt(q * sides[j], k), -1e30)
                e = jnp.exp(s - jnp.max(s, axis=-1, keepdims=True))
                p = (e * (1.0 / jnp.sum(e, axis=-1, keepdims=True))).astype(BF)
                p_ref[m * 2 + j, i, :, :wide] = p
                o.append(nn(p, v))
            qkvo[i * TILE : (i + 1) * TILE, 1536 + m * 128 : 1536 + m * 128 + 128] = jnp.where(
                lane < HD, o[0], o[1]
            ).astype(BF)
    h_ref[...] = states + nt(qkvo[:, 1536:2048], w_ref[:, 1536:2048])


def feed_kernel(count, rows, place_ref, h_ref, c_ref, *refs):
    pieces = refs[:10]
    res_ref, dh_ref, gain_ref, own_ref, sib_ref, w_e, w_s, u_flat, c_flat, u_rel, c_rel, acc_f, acc_d = refs[10:]
    z, x = place_ref[0], place_ref[1]
    cols = w_e.shape[2]

    def store(group, at, block):
        w_e[group, pl.ds(at, rows), :] = block[:, :cols]
        w_s[group, pl.ds(at, rows), :] = block[:, cols:]

    place(pieces, z, x, count, rows, store)
    h = h_ref[...]
    scale = root_scale(h)
    unit = h * scale
    low = unit.astype(BF)
    back = c_ref[0]
    u_flat[...] = low.T
    c_flat[...] = back.T
    in_relative_rows(u_flat, u_rel, z, x, count, rows)
    in_relative_rows(c_flat, c_rel, z, x, count, rows)
    for m in range(4):
        target = (own_ref, sib_ref)[m % 2]
        inner = nn(low, w_e[m])
        bent = jnp.tanh(GELU * (inner + CUBIC * inner * inner * inner))
        active = (0.5 * inner * (1.0 + bent)).astype(BF)
        slope = 0.5 * (1.0 + bent) + 0.5 * inner * (1.0 - bent * bent) * GELU * (
            1.0 + 3.0 * CUBIC * inner * inner
        )
        grad = (nn(back, w_s[m]) * slope).astype(BF)
        forward = nt(active, w_s[m])
        inward = nt(grad, w_e[m])
        if m == 0:
            acc_f[...] = forward
            acc_d[...] = inward
        else:
            acc_f[...] += forward
            acc_d[...] += inward
        shape = (2, 2, target.shape[3], cols)
        target[:, m // 2, :, :, :cols] = nn(u_rel[...], grad).astype(BF).reshape(shape)
        target[:, m // 2, :, :, cols:] = nn(c_rel[...], active).astype(BF).reshape(shape)
    res_ref[...] = (h + acc_f[...]).astype(BF)
    pushed = acc_d[...]
    both = pushed * unit
    gain_ref[...] = jnp.broadcast_to(jnp.sum(both, axis=0, keepdims=True), gain_ref.shape)
    dh_ref[...] = back.astype(F32) + scale * (pushed - unit * jnp.mean(both, axis=-1, keepdims=True))


def attention_back_kernel(count, rows, place_ref, dh_ref, x_ref, qkvo, p_ref, w_ref, *refs):
    bg_ref, bgl_ref, gain_ref, own_ref, sib_ref, flat, rel, do_ref, dqkv, acc_k, acc_v = refs
    z, x = place_ref[0], place_ref[1]
    low = dh_ref[...].astype(BF)
    do_ref[...] = nn(low, w_ref[:, 1536:2048]).astype(BF)
    flat[...] = low.T
    in_relative_rows(flat, rel, z, x, count, rows)
    shape = (2, 2, own_ref.shape[3], 128)

    def put(part, value):
        for m in range(4):
            target = (own_ref, sib_ref)[m % 2]
            target[:, m // 2, :, :, part * 128 : part * 128 + 128] = (
                value[:, m * 128 : m * 128 + 128].astype(BF).reshape(shape)
            )

    put(3, nn(rel[...], qkvo[:, 1536:2048]))
    lane = lax.broadcasted_iota(jnp.int32, (1, 128), 1)
    sides = [(lane // HD == j).astype(BF) for j in range(2)]
    halves = [(lane // HD == j).astype(F32) for j in range(2)]
    tiles = dqkv.shape[0] // TILE
    for m in range(4):
        acc_k[...] = jnp.zeros_like(acc_k)
        acc_v[...] = jnp.zeros_like(acc_v)
        for i in range(tiles):
            first = max(0, i - 1) * TILE
            wide = min(tiles, i + 2) * TILE - first
            here = slice(i * TILE, (i + 1) * TILE)
            there = slice(first, first + wide)
            at = slice(m * 128, m * 128 + 128)
            q = qkvo[here, at]
            k = qkvo[there, 512 + m * 128 : 512 + m * 128 + 128]
            v = qkvo[there, 1024 + m * 128 : 1024 + m * 128 + 128]
            do = do_ref[here, at]
            inside = do.astype(F32) * qkvo[here, 1536 + m * 128 : 1536 + m * 128 + 128].astype(F32)
            dq = 0.0
            for j in range(2):
                p = p_ref[m * 2 + j, i, :, :wide]
                do_j = do * sides[j]
                delta = jnp.sum(inside * halves[j], axis=-1, keepdims=True)
                ds = (p.astype(F32) * (nt(do_j, v) - delta)).astype(BF)
                dq = dq + nn(ds, k * sides[j])
                acc_k[there, :] += tn(ds, q * sides[j])
                acc_v[there, :] += tn(p, do_j)
            dqkv[here, at] = (dq * HD**-0.5).astype(BF)
        dqkv[:, 512 + m * 128 : 512 + m * 128 + 128] = (acc_k[...] * HD**-0.5).astype(BF)
        dqkv[:, 1024 + m * 128 : 1024 + m * 128 + 128] = acc_v[...].astype(BF)
    states = x_ref[0].astype(F32)
    scale = root_scale(states)
    unit = states * scale
    flat[...] = unit.astype(BF).T
    in_relative_rows(flat, rel, z, x, count, rows)
    for part in range(3):
        put(part, nn(rel[...], dqkv[:, part * 512 : part * 512 + 512]))
    pushed = nt(dqkv[...], w_ref[:, :1536])
    both = pushed * unit
    gain_ref[...] = jnp.broadcast_to(jnp.sum(both, axis=0, keepdims=True), gain_ref.shape)
    out = dh_ref[...] + scale * (pushed - unit * jnp.mean(both, axis=-1, keepdims=True))
    bg_ref[...] = out
    bgl_ref[...] = out.astype(BF)


def adam(master, moment, second, gradient, rate, decay):
    moment_new = 0.5 * moment + 0.5 * gradient
    second_new = 0.6 * second + 0.4 * gradient * gradient
    update = moment_new / (1.0 - 0.5**STEP) / (jnp.sqrt(second_new / (1.0 - 0.6**STEP)) + 1e-08)
    return master - rate * (update + decay * master), moment_new, second_new


def adam_into(outs, state, gradient, rate, decay):
    master, moment, second = adam(*state, gradient, rate, decay)
    outs[0][...] = master
    outs[1][...] = moment
    outs[2][...] = second
    outs[3][...] = master.astype(BF)


def total(refs):
    whole = refs[0][...].astype(F32)
    for ref in refs[1:]:
        whole = whole + ref[...].astype(F32)
    return whole


def feed_update_kernel(count, *refs):
    terms, gain, state, outs = refs[:count], refs[count], refs[count + 1 : count + 7], refs[count + 7 :]
    grad = total(terms)
    cols = state[0].shape[1]
    scaled = grad[:, :cols] * gain[:, 1:2].astype(BF).astype(F32)
    adam_into(outs[:4], [r[...] for r in state[:3]], scaled, 0.05, 0.1)
    adam_into(outs[4:], [r[...] for r in state[3:]], grad[:, cols:], 0.025, 0.1)


def attention_update_kernel(count, *refs):
    terms, gain, state, outs = refs[:count], refs[count], refs[count + 1 : count + 7], refs[count + 7 :]
    grad = total(terms)
    scale = gain[:, 0:1].astype(BF).astype(F32)
    for part in range(3):
        master, moment, second = adam(
            *[r[part] for r in state[:3]], grad[:, part * 128 : part * 128 + 128] * scale, 0.05, 0.1
        )
        outs[0][part] = master
        outs[1][part] = moment
        outs[2][part] = second
        outs[3][part] = master.astype(BF)
    adam_into(outs[4:], [r[...] for r in state[3:]], grad[:, 384:512], 0.3, 0.1)


def prepare_kernel(gain, attend, mixing, expand, shrink, first, second):
    gain_one = gain[:, 0:1].astype(BF).astype(F32)
    gain_two = gain[:, 1:2].astype(BF).astype(F32)
    cols = expand.shape[1]
    for part in range(3):
        first[:, part * 128 : part * 128 + 128] = (attend[part].astype(BF).astype(F32) * gain_one).astype(BF)
    first[:, 384:512] = mixing[...].astype(BF)
    second[:, :cols] = (expand[...].astype(BF).astype(F32) * gain_two).astype(BF)
    second[:, cols:] = shrink[...].astype(BF)


def rows_kernel(place_ref, own, sib, across, far, out_ref):
    step = pl.program_id(0)
    for k, ref in enumerate((own, sib, across, far)):

        @pl.when(step == k)
        def _(ref=ref):
            out_ref[0] = ref[...].astype(out_ref.dtype)


def struct(shape, dtype):
    return jax.ShapeDtypeStruct(shape, dtype)


def over_x(value):
    n = lax.axis_size("dp")
    return lax.ppermute(value, "dp", [(i, i ^ 1) for i in range(n)])


def over_z(value, k):
    n = lax.axis_size("dp")
    return lax.ppermute(value, "dp", [(i, (i + 2 * k) % n) for i in range(n)])


def over_y(value):
    return lax.ppermute(value, "mp", [(i, i ^ 2) for i in range(4)])


def over_core(value):
    return lax.ppermute(value, "mp", [(i, i ^ 1) for i in range(4)])


def gather_z(block, count):
    return jnp.concatenate([block] + [over_z(block, k) for k in range(1, count)], axis=0)


def gather_plane(column):
    half = column.shape[0] // 2
    near_x, near_y = over_x(column), over_y(column)
    far_low, far_high = over_x(near_y[:half]), over_y(near_x[half:])
    mine = [column, near_x, near_y, far_low, far_high]
    return mine + [over_core(v) for v in mine]


def add(a, b):
    return (a.astype(F32) + b.astype(F32)).astype(BF)


def scatter_plane(own, sib):
    got = over_core(sib)
    send_x, send_y = add(own[0, :, 1], got[0, :, 1]), add(own[1, 1], got[1, 1])
    got_x, got_y = over_x(send_x), over_y(send_y)
    low = [add(add(own[0, y, 0], got[0, y, 0]), got_x[y]) for y in range(2)]
    high = [add(add(own[1, 0, x], got[1, 0, x]), got_y[x]) for x in range(2)]
    return jnp.concatenate([add(low[0], over_y(low[1])), add(high[0], over_x(high[1]))], axis=0)


def scatter_z(column, count):
    rows = column.shape[0] // count
    return [column[:rows]] + [over_z(column[k * rows : (k + 1) * rows], k) for k in range(1, count)]


def to_rows(own, sib, dtype, row_at):
    across, far = over_y(own.astype(BF)), None
    far = over_core(across)
    return call(
        rows_kernel,
        [struct((4,) + own.shape, dtype)],
        [own, sib, across, far],
        prefetch=(row_at,),
        grid=(4,),
        maps={("out", 0): pl.BlockSpec((1,) + own.shape, lambda i, s: (s[2] ^ i, 0, 0))},
        moved=8 * own.size,
    )[0]


def on_device(
    blocks,
    block_segment,
    upstream,
    attend_master,
    attend_first,
    attend_second,
    mixing_master,
    mixing_first,
    mixing_second,
    expand_master,
    expand_first,
    expand_second,
    shrink_master,
    shrink_first,
    shrink_second,
    gains_master,
    gains_first,
    gains_second,
):
    dp_size = lax.axis_size("dp")
    count = dp_size // 2
    rows = attend_master.shape[1]
    length, width = blocks.shape[1:]
    cols = expand_master.shape[1]
    dp_at, mp_at = lax.axis_index("dp"), lax.axis_index("mp")
    where = jnp.stack([dp_at // 2, dp_at % 2, mp_at]).astype(jnp.int32)
    row_spec = pl.BlockSpec((1, length, width), lambda i, s: (s[2], 0, 0))
    gain_cols = gains_master.T

    first, second = call(
        prepare_kernel,
        [struct((rows, 512), BF), struct((rows, 2 * cols), BF)],
        [gain_cols, attend_master, mixing_master.T, expand_master, shrink_master.T],
        moved=2 << 20,
    )
    column_one = gather_z(first, count)
    second, column_one = lax.optimization_barrier((second, column_one))
    column_two = gather_z(second, count)
    pieces_one = gather_plane(column_one)
    pieces_two = gather_plane(column_two)

    segment = lax.dynamic_slice_in_dim(block_segment, mp_at, 1, 0)
    tiles = length // TILE
    h, qkvo, probs, weights = call(
        functools.partial(attention_kernel, count, rows),
        [
            struct((length, width), F32),
            struct((length, 2048), BF),
            struct((8, tiles, TILE, 3 * TILE), BF),
            struct((width, 2048), BF),
        ],
        [blocks, segment.reshape(length, 1), segment, *pieces_one],
        prefetch=(where,),
        maps={0: row_spec},
        flops=6 * 10**9,
        moved=12 << 20,
        trans=10**6,
    )
    res, dh, gain_two, own_two, sib_two = call(
        functools.partial(feed_kernel, count, rows),
        [
            struct((length, width), BF),
            struct((length, width), F32),
            struct((8, width), F32),
            struct((2, 2, 2, 128, 2 * cols), BF),
            struct((2, 2, 2, 128, 2 * cols), BF),
        ],
        [h, upstream, *pieces_two],
        scratch=[
            pltpu.VMEM((4, width, cols), BF),
            pltpu.VMEM((4, width, cols), BF),
            *[pltpu.VMEM((width, length), BF)] * 4,
            pltpu.VMEM((length, width), F32),
            pltpu.VMEM((length, width), F32),
        ],
        prefetch=(where,),
        maps={1: row_spec},
        flops=8 * 10**9,
        moved=12 << 20,
        trans=10**6,
    )
    result = to_rows(res, over_core(res), BF, where)
    bg, bg_low, gain_one, own_one, sib_one = call(
        functools.partial(attention_back_kernel, count, rows),
        [
            struct((length, width), F32),
            struct((length, width), BF),
            struct((8, width), F32),
            struct((2, 2, 2, 128, 512), BF),
            struct((2, 2, 2, 128, 512), BF),
        ],
        [dh, blocks, qkvo, probs, weights],
        scratch=[
            pltpu.VMEM((width, length), BF),
            pltpu.VMEM((width, length), BF),
            pltpu.VMEM((length, 512), BF),
            pltpu.VMEM((length, 1536), BF),
            pltpu.VMEM((length, 128), F32),
            pltpu.VMEM((length, 128), F32),
        ],
        prefetch=(where,),
        maps={1: row_spec},
        flops=8 * 10**9,
        moved=12 << 20,
    )
    blocks_grad = to_rows(bg, over_core(bg_low), F32, where)

    terms_two = scatter_z(scatter_plane(own_two, sib_two), count)
    terms_one = scatter_z(scatter_plane(own_one, sib_one), count)
    gain_sum = jnp.concatenate([gain_one[:1], gain_two[:1]], axis=0)
    for bit in (1, 2):
        gain_sum = gain_sum + lax.ppermute(gain_sum, "mp", [(i, i ^ bit) for i in range(4)])
    bit = 1
    while bit < dp_size:
        gain_sum = gain_sum + lax.ppermute(gain_sum, "dp", [(i, i ^ bit) for i in range(dp_size)])
        bit *= 2

    def quad(shape):
        return [struct(shape, F32)] * 3 + [struct(shape, BF)]

    feed_new = call(
        functools.partial(feed_update_kernel, count),
        quad((rows, cols)) * 2,
        [
            *terms_two,
            gain_cols,
            expand_master,
            expand_first,
            expand_second,
            shrink_master.T,
            shrink_first.T,
            shrink_second.T,
        ],
        moved=3 << 20,
    )
    attention_new = call(
        functools.partial(attention_update_kernel, count),
        quad(attend_master.shape) + quad((rows, 128)),
        [
            *terms_one,
            gain_cols,
            attend_master,
            attend_first,
            attend_second,
            mixing_master.T,
            mixing_first.T,
            mixing_second.T,
        ],
        moved=3 << 20,
    )
    gain_grad = lax.dynamic_slice_in_dim(gain_sum, dp_at * rows, rows, 1) / gains_master.astype(BF).astype(F32)
    gains_new = adam(gains_master, gains_first, gains_second, gain_grad, 0.25, 0.0)
    return (
        result,
        blocks_grad,
        *attention_new[:4],
        *[a.T for a in attention_new[4:]],
        *feed_new[:4],
        *[a.T for a in feed_new[4:]],
        *gains_new,
        gains_new[0].astype(BF),
    )


def solution(mesh):
    rows = P("dp", None, None)
    attend, mixing, expand, gains = P(None, "dp", "mp"), P("mp", "dp"), P("dp", "mp"), P(None, "dp")
    kinds = (attend, mixing, expand, mixing, gains)
    in_specs = (rows, P("dp", None), rows) + tuple(k for k in kinds for _ in range(3))
    out_specs = (rows, rows) + tuple(k for k in kinds for _ in range(4))
    return jax.shard_map(on_device, mesh=mesh, in_specs=in_specs, out_specs=out_specs, check_vma=False)
```

profile of v0, /device:TPU:0, one launch (start us, length us, event | category | flops | bytes accessed | tf_op | source)
XLA Modules:
  0.0 199.4 jit_solution(6024950350909981207)
XLA Ops:
  0.7 1.4 copy.45
  2.1 1.8 shard_map.345
  3.9 5.0 %collective-permute-start.2 = (bf16[64,512]{1,0:T(8,128)(2,1)}, bf16[64,512]{1,0:T(8,128)(2,1)S(1)}, u32[]{:S(2)}, u32[]{:S(2)}) collective-permute-start(bf16[64,512]{1,0:T(8,128)(2,1)} %get-tuple-element.57), channel_id=1, source_target_pairs={{0,24},{4,28},{8,0},{12,4},{16,8},{20,12},{24,16},{28,20},{1,25},{... | collective-permute-start | bytes 196616 | tf_op jit(solution)/shard_map/ppermute | solution.py:315
  9.9 1.8 collective-permute-done.2
  11.7 3.9 %collective-permute-done.1 = bf16[64,512]{1,0:T(8,128)(2,1)S(1)} collective-permute-done((bf16[64,512]{1,0:T(8,128)(2,1)}, bf16[64,512]{1,0:T(8,128)(2,1)S(1)}, u32[]{:S(2)}, u32[]{:S(2)}) %collective-permute-start.1) | collective-permute-done | bytes 65568 | tf_op jit(solution)/shard_map/ppermute | solution.py:315
  16.7 3.7 %collective-permute-start.14 = (bf16[64,1024]{1,0:T(8,128)(2,1)}, bf16[64,1024]{1,0:T(8,128)(2,1)S(1)}, u32[]{:S(2)}, u32[]{:S(2)}) collective-permute-start(bf16[64,1024]{1,0:T(8,128)(2,1)} %get-tuple-element.60), channel_id=1, source_target_pairs={{0,24},{4,28},{8,0},{12,4},{16,8},{20,12},{24,16},{28,20},{1,25},{... | collective-permute-start | bytes 393224 | tf_op jit(solution)/shard_map/ppermute | solution.py:315
  21.3 3.6 %collective-permute-done.12 = bf16[64,1024]{1,0:T(8,128)(2,1)S(1)} collective-permute-done((bf16[64,1024]{1,0:T(8,128)(2,1)}, bf16[64,1024]{1,0:T(8,128)(2,1)S(1)}, u32[]{:S(2)}, u32[]{:S(2)}) %collective-permute-start.12) | collective-permute-done | bytes 131104 | tf_op jit(solution)/shard_map/ppermute | solution.py:315
  24.9 6.6 %collective-permute-done.13 = bf16[64,1024]{1,0:T(8,128)(2,1)S(1)} collective-permute-done((bf16[64,1024]{1,0:T(8,128)(2,1)}, bf16[64,1024]{1,0:T(8,128)(2,1)S(1)}, u32[]{:S(2)}, u32[]{:S(2)}) %collective-permute-start.13) | collective-permute-done | bytes 131104 | tf_op jit(solution)/shard_map/ppermute | solution.py:315
  31.6 1.6 collective-permute-start.16
  33.2 1.5 collective-permute-start.15
  35.7 14.7 %collective-permute-done.4.refs_2_ = bf16[256,512]{1,0:T(8,128)(2,1)S(1)} collective-permute-done((bf16[256,512]{1,0:T(8,128)(2,1)S(1)}, bf16[256,512]{1,0:T(8,128)(2,1)S(1)}, u32[]{:S(2)}, u32[]{:S(2)}) %collective-permute-start.4) | collective-permute-done | bytes 262176 | tf_op jit(solution)/shard_map/ppermute | solution.py:319
  50.4 1.2 collective-permute-done.3.refs_1_
  51.6 1.5 collective-permute-start.5
  54.5 2.1 %collective-permute-done.5.refs_3_ = bf16[128,512]{1,0:T(8,128)(2,1)S(1)} collective-permute-done((bf16[128,512]{1,0:T(8,128)(2,1)S(1)}, bf16[128,512]{1,0:T(8,128)(2,1)S(1)}, u32[]{:S(2)}, u32[]{:S(2)}) %collective-permute-start.5) | collective-permute-done | bytes 131104 | tf_op jit(solution)/shard_map/ppermute | solution.py:310
  56.6 1.3 collective-permute-start.18
  61.5 1.3 collective-permute-done.17.refs_3_
  62.8 1.4 collective-permute-done.18.refs_4_
  64.2 14.6 %shard_map.346 = (f32[512,512]{1,0:T(8,128)}, bf16[512,2048]{1,0:T(8,128)(2,1)}, bf16[8,4,128,384]{3,2,1,0:T(8,128)(2,1)}, bf16[512,2048]{1,0:T(8,128)(2,1)}) custom-call(s32[3]{0:T(128)} %pad_add_fusion.place_ref, bf16[4,512,512]{2,1,0:T(8,128)(2,1)} %x_ref.3, s32[512,1]{1,0:T(8,128)} %copy.46.seg_col, s32[1,512]{1,0:T(1,128)} %constant_dynamic-slice_fusion.seg_row, ...), custom_call_target="tpu_custom_call" | custom-call | flops 6000000000 | bytes 12582912 | tf_op jit(solution)/shard_map/pallas_call | solution.py:44
  80.2 13.9 %shard_map.347 = (bf16[512,512]{1,0:T(8,128)(2,1)}, f32[512,512]{1,0:T(8,128)}, f32[8,512]{1,0:T(8,128)}, bf16[2,2,2,128,1024]{4,3,2,1,0:T(8,128)(2,1)}, bf16[2,2,2,128,1024]{4,3,2,1,0:T(8,128)(2,1)}) custom-call(s32[3]{0:T(128)} %pad_add_fusion.place_ref, f32[512,512]{1,0:T(8,128)} %get-tuple-element.59.h_ref, bf16[4,512,512]{2,1,0:T(8,128)(2,1)} %c_ref.1, ...), custom_call_target="tpu_custom_call" | custom-call | flops 8000000000 | bytes 12582912 | tf_op jit(solution)/shard_map/pallas_call | solution.py:44
  94.6 15.0 %shard_map.349 = (f32[512,512]{1,0:T(8,128)}, bf16[512,512]{1,0:T(8,128)(2,1)}, f32[8,512]{1,0:T(8,128)}, bf16[2,2,2,128,512]{4,3,2,1,0:T(8,128)(2,1)}, bf16[2,2,2,128,512]{4,3,2,1,0:T(8,128)(2,1)}) custom-call(s32[3]{0:T(128)} %pad_add_fusion.place_ref, f32[512,512]{1,0:T(8,128)} %get-tuple-element.62.dh_ref, bf16[4,512,512]{2,1,0:T(8,128)(2,1)} %x_ref.3, ...), custom_call_target="tpu_custom_call" | custom-call | flops 8000000000 | bytes 12582912 | tf_op jit(solution)/shard_map/pallas_call | solution.py:44
  112.9 1.8 collective-permute-start.47
  117.0 1.6 collective-permute-start.48
  118.6 2.1 %collective-permute-done.48 = f32[2,512]{1,0:T(2,128)S(1)} collective-permute-done((f32[2,512]{1,0:T(2,128)S(1)}, f32[2,512]{1,0:T(2,128)S(1)}, u32[]{:S(2)}, u32[]{:S(2)}) %collective-permute-start.48) | collective-permute-done | bytes 4128 | tf_op jit(solution)/shard_map/ppermute | solution.py:485
  120.8 1.3 convert_element_type.320
  122.1 1.8 collective-permute-start.28
  124.3 1.7 collective-permute-start.50
  126.0 1.1 fusion.6
  127.1 1.6 collective-permute-start.31
  130.3 1.4 fusion.1
  131.8 1.8 collective-permute-start.42
  134.8 1.4 collective-permute-done.35
  136.2 1.1 add_convert_fusion.10
  137.4 1.7 collective-permute-start.32
  139.1 1.2 fusion
  140.3 1.6 collective-permute-start.39
  141.9 17.7 %collective-permute-done.42 = bf16[2,128,1024]{2,1,0:T(8,128)(2,1)S(1)} collective-permute-done((bf16[2,128,1024]{2,1,0:T(8,128)(2,1)S(1)}, bf16[2,128,1024]{2,1,0:T(8,128)(2,1)S(1)}, u32[]{:S(2)}, u32[]{:S(2)}) %collective-permute-start.42) | collective-permute-done | bytes 524320 | tf_op jit(solution)/shard_map/ppermute | solution.py:319
  159.6 1.1 fusion.2
  160.7 1.6 collective-permute-start.43
  164.5 2.9 %collective-permute-done.43 = bf16[128,1024]{1,0:T(8,128)(2,1)S(1)} collective-permute-done((bf16[128,1024]{1,0:T(8,128)(2,1)S(1)}, bf16[128,1024]{1,0:T(8,128)(2,1)S(1)}, u32[]{:S(2)}, u32[]{:S(2)}) %collective-permute-start.43) | collective-permute-done | bytes 262176 | tf_op jit(solution)/shard_map/ppermute | solution.py:310
  167.3 1.3 add_convert_fusion.2
  170.2 4.9 %collective-permute-done.40 = bf16[128,1024]{1,0:T(8,128)(2,1)S(1)} collective-permute-done((bf16[128,1024]{1,0:T(8,128)(2,1)S(1)}, bf16[128,1024]{1,0:T(8,128)(2,1)S(1)}, u32[]{:S(2)}, u32[]{:S(2)}) %collective-permute-start.40) | collective-permute-done | bytes 262176 | tf_op jit(solution)/shard_map/ppermute | solution.py:319
  175.1 1.2 collective-permute-start.37
  176.3 1.1 add_convert_fusion.5
  179.6 3.5 %collective-permute-start.45 = (bf16[64,1024]{1,0:T(8,128)(2,1)S(1)}, bf16[64,1024]{1,0:T(8,128)(2,1)S(1)}, u32[]{:S(2)}, u32[]{:S(2)}) collective-permute-start(bf16[64,1024]{1,0:T(8,128)(2,1)S(1)} %get-tuple-element.98), channel_id=1, source_target_pairs={{0,24},{4,28},{8,0},{12,4},{16,8},{20,12},{24,16},{28,20},{1,25},{... | collective-permute-start | bytes 393224 | tf_op jit(solution)/shard_map/ppermute | solution.py:315
  184.5 4.1 %shard_map.348 = bf16[4,512,512]{2,1,0:T(8,128)(2,1)} custom-call(s32[3]{0:T(128)} %pad_add_fusion.place_ref, bf16[512,512]{1,0:T(8,128)(2,1)} %get-tuple-element.61.own, bf16[512,512]{1,0:T(8,128)(2,1)} %copy-done.6, bf16[512,512]{1,0:T(8,128)(2,1)} %copy-done.5, bf16[512,512]{1,0:T(8,128)(2,1)} %copy-done.7), custom_call_target="tpu_custom_call" | custom-call | bytes 2097152 | tf_op jit(solution)/shard_map/pallas_call | solution.py:44
  188.5 4.8 %shard_map.350 = f32[4,512,512]{2,1,0:T(8,128)} custom-call(s32[3]{0:T(128)} %pad_add_fusion.place_ref, f32[512,512]{1,0:T(8,128)} %get-tuple-element.66.own, bf16[512,512]{1,0:T(8,128)(2,1)} %copy-done.9, bf16[512,512]{1,0:T(8,128)(2,1)} %copy-done.8, bf16[512,512]{1,0:T(8,128)(2,1)} %copy-done.10), custom_call_target="tpu_custom_call" | custom-call | bytes 2097152 | tf_op jit(solution)/shard_map/pallas_call | solution.py:44
  194.0 2.0 shard_map.351
  196.8 2.5 %shard_map.352 = (f32[64,512]{1,0:T(8,128)}, f32[64,512]{1,0:T(8,128)}, f32[64,512]{1,0:T(8,128)}, bf16[64,512]{1,0:T(8,128)(2,1)}, f32[64,512]{1,0:T(8,128)}, /...) custom-call(bf16[64,1024]{1,0:T(8,128)(2,1)} %get-tuple-element.101.refs_0_, ...), custom_call_target="tpu_custom_call" | custom-call | bytes 3145728 | tf_op jit(solution)/shard_map/pallas_call | solution.py:44
  (170 shorter events, 28.3 us)
Async XLA Ops:
  3.9 7.9 %collective-permute-start.2 = (bf16[64,512]{1,0:T(8,128)(2,1)}, bf16[64,512]{1,0:T(8,128)(2,1)S(1)}, u32[]{:S(2)}, u32[]{:S(2)}) collective-permute-start(bf16[64,512]{1,0:T(8,128)(2,1)} %get-tuple-element.57), channel_id=1, source_target_pairs={{0,24},{4,28},{8,0},{12,4},{16,8},{20,12},{24,16},{28,20},{1,25},{... | collective-permute-start | bytes 196616 | tf_op jit(solution)/shard_map/ppermute | solution.py:315
  8.9 6.7 %collective-permute-start.1 = (bf16[64,512]{1,0:T(8,128)(2,1)}, bf16[64,512]{1,0:T(8,128)(2,1)S(1)}, u32[]{:S(2)}, u32[]{:S(2)}) collective-permute-start(bf16[64,512]{1,0:T(8,128)(2,1)} %get-tuple-element.57), channel_id=1, source_target_pairs={{0,16},{4,20},{8,24},{12,28},{16,0},{20,4},{24,8},{28,12},{1,17},{... | collective-permute-start | bytes 196616 | tf_op jit(solution)/shard_map/ppermute | solution.py:315
  8.9 6.7 %collective-permute-start = (bf16[64,512]{1,0:T(8,128)(2,1)}, bf16[64,512]{1,0:T(8,128)(2,1)S(1)}, u32[]{:S(2)}, u32[]{:S(2)}) collective-permute-start(bf16[64,512]{1,0:T(8,128)(2,1)} %get-tuple-element.57), channel_id=1, source_target_pairs={{0,8},{4,12},{8,16},{12,20},{16,24},{20,28},{24,0},{28,4},{1,9},{5... | collective-permute-start | bytes 196616 | tf_op jit(solution)/shard_map/ppermute | solution.py:315
  16.5 8.4 %collective-permute-start.12 = (bf16[64,1024]{1,0:T(8,128)(2,1)}, bf16[64,1024]{1,0:T(8,128)(2,1)S(1)}, u32[]{:S(2)}, u32[]{:S(2)}) collective-permute-start(bf16[64,1024]{1,0:T(8,128)(2,1)} %get-tuple-element.60), channel_id=1, source_target_pairs={{0,8},{4,12},{8,16},{12,20},{16,24},{20,28},{24,0},{28,4},{1,9},{5... | collective-permute-start | bytes 393224 | tf_op jit(solution)/shard_map/ppermute | solution.py:315
  16.7 14.9 %collective-permute-start.14 = (bf16[64,1024]{1,0:T(8,128)(2,1)}, bf16[64,1024]{1,0:T(8,128)(2,1)S(1)}, u32[]{:S(2)}, u32[]{:S(2)}) collective-permute-start(bf16[64,1024]{1,0:T(8,128)(2,1)} %get-tuple-element.60), channel_id=1, source_target_pairs={{0,24},{4,28},{8,0},{12,4},{16,8},{20,12},{24,16},{28,20},{1,25},{... | collective-permute-start | bytes 393224 | tf_op jit(solution)/shard_map/ppermute | solution.py:315
  20.3 11.2 %collective-permute-start.13 = (bf16[64,1024]{1,0:T(8,128)(2,1)}, bf16[64,1024]{1,0:T(8,128)(2,1)S(1)}, u32[]{:S(2)}, u32[]{:S(2)}) collective-permute-start(bf16[64,1024]{1,0:T(8,128)(2,1)} %get-tuple-element.60), channel_id=1, source_target_pairs={{0,16},{4,20},{8,24},{12,28},{16,0},{20,4},{24,8},{28,12},{1,17},{... | collective-permute-start | bytes 393224 | tf_op jit(solution)/shard_map/ppermute | solution.py:315
  31.6 21.6 %collective-permute-start.16 = (bf16[256,1024]{1,0:T(8,128)(2,1)S(1)}, bf16[256,1024]{1,0:T(8,128)(2,1)S(1)}, u32[]{:S(2)}, u32[]{:S(2)}) collective-permute-start(bf16[256,1024]{1,0:T(8,128)(2,1)S(1)} %constant_dynamic-update-slice_fusion.refs_0_), channel_id=1, source_target_pairs={{0,2},{1,3},{2,0},{3,1},{4,6},{5,7},{6,4},{7,5},{8,10},{9,11},{10,... | collective-permute-start | bytes 1572872 | tf_op jit(solution)/shard_map/ppermute | solution.py:319
  33.2 20.6 %collective-permute-start.15 = (bf16[256,1024]{1,0:T(8,128)(2,1)S(1)}, bf16[256,1024]{1,0:T(8,128)(2,1)S(1)}, u32[]{:S(2)}, u32[]{:S(2)}) collective-permute-start(bf16[256,1024]{1,0:T(8,128)(2,1)S(1)} %constant_dynamic-update-slice_fusion.refs_0_), channel_id=1, source_target_pairs={{0,4},{4,0},{8,12},{12,8},{16,20},{20,16},{24,28},{28,24},{1,5},{5... | collective-permute-start | bytes 1572872 | tf_op jit(solution)/shard_map/ppermute | solution.py:310
  34.7 15.7 %collective-permute-start.4 = (bf16[256,512]{1,0:T(8,128)(2,1)S(1)}, bf16[256,512]{1,0:T(8,128)(2,1)S(1)}, u32[]{:S(2)}, u32[]{:S(2)}) collective-permute-start(bf16[256,512]{1,0:T(8,128)(2,1)S(1)} %pad_maximum_fusion.refs_0_), channel_id=1, source_target_pairs={{0,2},{1,3},{2,0},{3,1},{4,6},{5,7},{6,4},{7,5},{8,10},{9,11},{10,... | collective-permute-start | bytes 786440 | tf_op jit(solution)/shard_map/ppermute | solution.py:319
  35.2 16.5 %collective-permute-start.3 = (bf16[256,512]{1,0:T(8,128)(2,1)S(1)}, bf16[256,512]{1,0:T(8,128)(2,1)S(1)}, u32[]{:S(2)}, u32[]{:S(2)}) collective-permute-start(bf16[256,512]{1,0:T(8,128)(2,1)S(1)} %pad_maximum_fusion.refs_0_), channel_id=1, source_target_pairs={{0,4},{4,0},{8,12},{12,8},{16,20},{20,16},{24,28},{28,24},{1,5},{5... | collective-permute-start | bytes 786440 | tf_op jit(solution)/shard_map/ppermute | solution.py:310
  35.7 18.2 %collective-permute-start.7 = (bf16[256,512]{1,0:T(8,128)(2,1)S(1)}, bf16[256,512]{1,0:T(8,128)(2,1)S(1)}, u32[]{:S(2)}, u32[]{:S(2)}) collective-permute-start(bf16[256,512]{1,0:T(8,128)(2,1)S(1)} %pad_maximum_fusion.refs_0_), channel_id=1, source_target_pairs={{0,1},{1,0},{2,3},{3,2},{4,5},{5,4},{6,7},{7,6},{8,9},{9,8},{10,11... | collective-permute-start | bytes 786440 | tf_op jit(solution)/shard_map/ppermute | solution.py:323
  50.4 7.9 %collective-permute-start.9 = (bf16[256,512]{1,0:T(8,128)(2,1)S(1)}, bf16[256,512]{1,0:T(8,128)(2,1)}, u32[]{:S(2)}, u32[]{:S(2)}) collective-permute-start(bf16[256,512]{1,0:T(8,128)(2,1)S(1)} %collective-permute-done.4.refs_2_), channel_id=1, source_target_pairs={{0,1},{1,0},{2,3},{3,2},{4,5},{5,4},{6,7},{7,6},{8,9},{9,8},{10,11... | collective-permute-start | bytes 786440 | tf_op jit(solution)/shard_map/ppermute | solution.py:323
  51.6 5.0 %collective-permute-start.5 = (bf16[128,512]{1,0:T(8,128)(2,1)S(1)}, bf16[128,512]{1,0:T(8,128)(2,1)S(1)}, u32[]{:S(2)}, u32[]{:S(2)}) collective-permute-start(bf16[128,512]{1,0:T(8,128)(2,1)S(1)} %slice.184), channel_id=1, source_target_pairs={{0,4},{4,0},{8,12},{12,8},{16,20},{20,16},{24,28},{28,24},{1,5},{5... | collective-permute-start | bytes 393224 | tf_op jit(solution)/shard_map/ppermute | solution.py:310
  53.2 5.1 %collective-permute-start.6 = (bf16[128,512]{1,0:T(8,128)(2,1)S(1)}, bf16[128,512]{1,0:T(8,128)(2,1)}, u32[]{:S(2)}, u32[]{:S(2)}) collective-permute-start(bf16[128,512]{1,0:T(8,128)(2,1)S(1)} %slice.185), channel_id=1, source_target_pairs={{0,2},{1,3},{2,0},{3,1},{4,6},{5,7},{6,4},{7,5},{8,10},{9,11},{10,... | collective-permute-start | bytes 393224 | tf_op jit(solution)/shard_map/ppermute | solution.py:319
  53.8 7.1 %collective-permute-start.8 = (bf16[256,512]{1,0:T(8,128)(2,1)S(1)}, bf16[256,512]{1,0:T(8,128)(2,1)}, u32[]{:S(2)}, u32[]{:S(2)}) collective-permute-start(bf16[256,512]{1,0:T(8,128)(2,1)S(1)} %collective-permute-done.3.refs_1_), channel_id=1, source_target_pairs={{0,1},{1,0},{2,3},{3,2},{4,5},{5,4},{6,7},{7,6},{8,9},{9,8},{10,11... | collective-permute-start | bytes 786440 | tf_op jit(solution)/shard_map/ppermute | solution.py:323
  53.9 8.9 %collective-permute-start.17 = (bf16[128,1024]{1,0:T(8,128)(2,1)S(1)}, bf16[128,1024]{1,0:T(8,128)(2,1)}, u32[]{:S(2)}, u32[]{:S(2)}) collective-permute-start(bf16[128,1024]{1,0:T(8,128)(2,1)S(1)} %slice.186), channel_id=1, source_target_pairs={{0,4},{4,0},{8,12},{12,8},{16,20},{20,16},{24,28},{28,24},{1,5},{5... | collective-permute-start | bytes 786440 | tf_op jit(solution)/shard_map/ppermute | solution.py:310
  56.6 7.6 %collective-permute-start.18 = (bf16[128,1024]{1,0:T(8,128)(2,1)S(1)}, bf16[128,1024]{1,0:T(8,128)(2,1)}, u32[]{:S(2)}, u32[]{:S(2)}) collective-permute-start(bf16[128,1024]{1,0:T(8,128)(2,1)S(1)} %slice.187), channel_id=1, source_target_pairs={{0,2},{1,3},{2,0},{3,1},{4,6},{5,7},{6,4},{7,5},{8,10},{9,11},{10,... | collective-permute-start | bytes 786440 | tf_op jit(solution)/shard_map/ppermute | solution.py:319
  60.9 18.0 %collective-permute-start.19 = (bf16[256,1024]{1,0:T(8,128)(2,1)S(1)}, bf16[256,1024]{1,0:T(8,128)(2,1)S(1)}, u32[]{:S(2)}, u32[]{:S(2)}) collective-permute-start(bf16[256,1024]{1,0:T(8,128)(2,1)S(1)} %constant_dynamic-update-slice_fusion.refs_0_), channel_id=1, source_target_pairs={{0,1},{1,0},{2,3},{3,2},{4,5},{5,4},{6,7},{7,6},{8,9},{9,8},{10,11... | collective-permute-start | bytes 1572872 | tf_op jit(solution)/shard_map/ppermute | solution.py:323
  60.9 18.0 %collective-permute-start.21 = (bf16[256,1024]{1,0:T(8,128)(2,1)S(1)}, bf16[256,1024]{1,0:T(8,128)(2,1)S(1)}, u32[]{:S(2)}, u32[]{:S(2)}) collective-permute-start(bf16[256,1024]{1,0:T(8,128)(2,1)S(1)} %collective-permute-done.16.refs_2_), channel_id=1, source_target_pairs={{0,1},{1,0},{2,3},{3,2},{4,5},{5,4},{6,7},{7,6},{8,9},{9,8},{10,11... | collective-permute-start | bytes 1572872 | tf_op jit(solution)/shard_map/ppermute | solution.py:323
  61.4 17.6 %collective-permute-start.20 = (bf16[256,1024]{1,0:T(8,128)(2,1)S(1)}, bf16[256,1024]{1,0:T(8,128)(2,1)S(1)}, u32[]{:S(2)}, u32[]{:S(2)}) collective-permute-start(bf16[256,1024]{1,0:T(8,128)(2,1)S(1)} %collective-permute-done.15.refs_1_), channel_id=1, source_target_pairs={{0,1},{1,0},{2,3},{3,2},{4,5},{5,4},{6,7},{7,6},{8,9},{9,8},{10,11... | collective-permute-start | bytes 1572872 | tf_op jit(solution)/shard_map/ppermute | solution.py:323
  62.8 16.1 %collective-permute-start.22 = (bf16[128,1024]{1,0:T(8,128)(2,1)}, bf16[128,1024]{1,0:T(8,128)(2,1)S(1)}, u32[]{:S(2)}, u32[]{:S(2)}) collective-permute-start(bf16[128,1024]{1,0:T(8,128)(2,1)} %collective-permute-done.17.refs_3_), channel_id=1, source_target_pairs={{0,1},{1,0},{2,3},{3,2},{4,5},{5,4},{6,7},{7,6},{8,9},{9,8},{10,11... | collective-permute-start | bytes 786440 | tf_op jit(solution)/shard_map/ppermute | solution.py:323
  64.2 14.7 %collective-permute-start.23 = (bf16[128,1024]{1,0:T(8,128)(2,1)}, bf16[128,1024]{1,0:T(8,128)(2,1)S(1)}, u32[]{:S(2)}, u32[]{:S(2)}) collective-permute-start(bf16[128,1024]{1,0:T(8,128)(2,1)} %collective-permute-done.18.refs_4_), channel_id=1, source_target_pairs={{0,1},{1,0},{2,3},{3,2},{4,5},{5,4},{6,7},{7,6},{8,9},{9,8},{10,11... | collective-permute-start | bytes 786440 | tf_op jit(solution)/shard_map/ppermute | solution.py:323
  94.1 35.6 %collective-permute-start.38 = (bf16[2,2,2,128,1024]{4,3,2,1,0:T(8,128)(2,1)}, bf16[2,2,2,128,1024]{4,3,2,1,0:T(8,128)(2,1)}, u32[]{:S(2)}, u32[]{:S(2)}) collective-permute-start(bf16[2,2,2,128,1024]{4,3,2,1,0:T(8,128)(2,1)} %get-tuple-element.79), channel_id=1, source_target_pairs={{0,1},{1,0},{2,3},{3,2},{4,5},{5,4},{6,7},{7,6},{8,9},{9,8},{10,11... | collective-permute-start | bytes 6291464 | tf_op jit(solution)/shard_map/ppermute | solution.py:323
  109.7 5.0 %collective-permute-start.30 = (bf16[2,2,2,128,512]{4,3,2,1,0:T(8,128)(2,1)}, bf16[2,2,2,128,512]{4,3,2,1,0:T(8,128)(2,1)S(1)}, u32[]{:S(2)}, u32[]{:S(2)}) collective-permute-start(bf16[2,2,2,128,512]{4,3,2,1,0:T(8,128)(2,1)} %get-tuple-element.69), channel_id=1, source_target_pairs={{0,1},{1,0},{2,3},{3,2},{4,5},{5,4},{6,7},{7,6},{8,9},{9,8},{10,11... | collective-permute-start | bytes 3145736 | tf_op jit(solution)/shard_map/ppermute | solution.py:323
  112.9 4.1 %collective-permute-start.47 = (f32[2,512]{1,0:T(2,128)S(1)}, f32[2,512]{1,0:T(2,128)S(1)}, u32[]{:S(2)}, u32[]{:S(2)}) collective-permute-start(f32[2,512]{1,0:T(2,128)S(1)} %fusion.22), channel_id=1, source_target_pairs={{0,2},{1,3},{2,0},{3,1},{4,6},{5,7},{6,4},{7,5},{8,10},{9,11},{10,... | collective-permute-start | bytes 12296 | tf_op jit(solution)/shard_map/ppermute | solution.py:482
  116.7 10.5 %collective-permute-start.34 = (bf16[2,128,512]{2,1,0:T(8,128)(2,1)S(1)}, bf16[2,128,512]{2,1,0:T(8,128)(2,1)}, u32[]{:S(2)}, u32[]{:S(2)}) collective-permute-start(bf16[2,128,512]{2,1,0:T(8,128)(2,1)S(1)} %fusion.7), channel_id=1, source_target_pairs={{0,2},{1,3},{2,0},{3,1},{4,6},{5,7},{6,4},{7,5},{8,10},{9,11},{10,... | collective-permute-start | bytes 786440 | tf_op jit(solution)/shard_map/ppermute | solution.py:319
  117.0 3.7 %collective-permute-start.48 = (f32[2,512]{1,0:T(2,128)S(1)}, f32[2,512]{1,0:T(2,128)S(1)}, u32[]{:S(2)}, u32[]{:S(2)}) collective-permute-start(f32[2,512]{1,0:T(2,128)S(1)} %fusion.30), channel_id=1, source_target_pairs={{0,4},{4,0},{8,12},{12,8},{16,20},{20,16},{24,28},{28,24},{1,5},{5... | collective-permute-start | bytes 12296 | tf_op jit(solution)/shard_map/ppermute | solution.py:485
  120.7 3.6 %collective-permute-start.49 = (f32[2,512]{1,0:T(2,128)S(1)}, f32[2,512]{1,0:T(2,128)S(1)}, u32[]{:S(2)}, u32[]{:S(2)}) collective-permute-start(f32[2,512]{1,0:T(2,128)S(1)} %add.154), channel_id=1, source_target_pairs={{0,8},{4,12},{8,0},{12,4},{16,24},{20,28},{24,16},{28,20},{1,9},{5... | collective-permute-start | bytes 12296 | tf_op jit(solution)/shard_map/ppermute | solution.py:485
  122.1 41.3 %collective-permute-start.28 = (bf16[512,512]{1,0:T(8,128)(2,1)S(1)}, bf16[512,512]{1,0:T(8,128)(2,1)S(1)}, u32[]{:S(2)}, u32[]{:S(2)}) collective-permute-start(bf16[512,512]{1,0:T(8,128)(2,1)S(1)} %convert_element_type.320), channel_id=1, source_target_pairs={{0,2},{1,3},{2,0},{3,1},{4,6},{5,7},{6,4},{7,5},{8,10},{9,11},{10,... | collective-permute-start | bytes 1572872 | tf_op jit(solution)/shard_map/ppermute | solution.py:319
  123.9 40.1 %collective-permute-start.25 = (bf16[512,512]{1,0:T(8,128)(2,1)}, bf16[512,512]{1,0:T(8,128)(2,1)S(1)}, u32[]{:S(2)}, u32[]{:S(2)}) collective-permute-start(bf16[512,512]{1,0:T(8,128)(2,1)} %get-tuple-element.61.own), channel_id=1, source_target_pairs={{0,2},{1,3},{2,0},{3,1},{4,6},{5,7},{6,4},{7,5},{8,10},{9,11},{10,... | collective-permute-start | bytes 1572872 | tf_op jit(solution)/shard_map/ppermute | solution.py:319
  124.3 7.5 %collective-permute-start.50 = (f32[2,512]{1,0:T(2,128)S(1)}, f32[2,512]{1,0:T(2,128)S(1)}, u32[]{:S(2)}, u32[]{:S(2)}) collective-permute-start(f32[2,512]{1,0:T(2,128)S(1)} %add.155), channel_id=1, source_target_pairs={{0,16},{4,20},{8,24},{12,28},{16,0},{20,4},{24,8},{28,12},{1,17},{... | collective-permute-start | bytes 12296 | tf_op jit(solution)/shard_map/ppermute | solution.py:485
  127.1 7.7 %collective-permute-start.31 = (bf16[2,128,512]{2,1,0:T(8,128)(2,1)S(1)}, bf16[2,128,512]{2,1,0:T(8,128)(2,1)S(1)}, u32[]{:S(2)}, u32[]{:S(2)}) collective-permute-start(bf16[2,128,512]{2,1,0:T(8,128)(2,1)S(1)} %fusion.6), channel_id=1, source_target_pairs={{0,4},{4,0},{8,12},{12,8},{16,20},{20,16},{24,28},{28,24},{1,5},{5... | collective-permute-start | bytes 786440 | tf_op jit(solution)/shard_map/ppermute | solution.py:310
  129.7 6.5 %collective-permute-start.35 = (bf16[128,512]{1,0:T(8,128)(2,1)S(1)}, bf16[128,512]{1,0:T(8,128)(2,1)S(1)}, u32[]{:S(2)}, u32[]{:S(2)}) collective-permute-start(bf16[128,512]{1,0:T(8,128)(2,1)S(1)} %fusion.12), channel_id=1, source_target_pairs={{0,4},{4,0},{8,12},{12,8},{16,20},{20,16},{24,28},{28,24},{1,5},{5... | collective-permute-start | bytes 393224 | tf_op jit(solution)/shard_map/ppermute | solution.py:310
  131.8 27.8 %collective-permute-start.42 = (bf16[2,128,1024]{2,1,0:T(8,128)(2,1)S(1)}, bf16[2,128,1024]{2,1,0:T(8,128)(2,1)S(1)}, u32[]{:S(2)}, u32[]{:S(2)}) collective-permute-start(bf16[2,128,1024]{2,1,0:T(8,128)(2,1)S(1)} %fusion.1), channel_id=1, source_target_pairs={{0,2},{1,3},{2,0},{3,1},{4,6},{5,7},{6,4},{7,5},{8,10},{9,11},{10,... | collective-permute-start | bytes 1572872 | tf_op jit(solution)/shard_map/ppermute | solution.py:319
  137.4 24.9 %collective-permute-start.32 = (bf16[128,512]{1,0:T(8,128)(2,1)S(1)}, bf16[128,512]{1,0:T(8,128)(2,1)S(1)}, u32[]{:S(2)}, u32[]{:S(2)}) collective-permute-start(bf16[128,512]{1,0:T(8,128)(2,1)S(1)} %get-tuple-element.97), channel_id=1, source_target_pairs={{0,2},{1,3},{2,0},{3,1},{4,6},{5,7},{6,4},{7,5},{8,10},{9,11},{10,... | collective-permute-start | bytes 393224 | tf_op jit(solution)/shard_map/ppermute | solution.py:319
  140.3 23.7 %collective-permute-start.39 = (bf16[2,128,1024]{2,1,0:T(8,128)(2,1)S(1)}, bf16[2,128,1024]{2,1,0:T(8,128)(2,1)S(1)}, u32[]{:S(2)}, u32[]{:S(2)}) collective-permute-start(bf16[2,128,1024]{2,1,0:T(8,128)(2,1)S(1)} %fusion), channel_id=1, source_target_pairs={{0,4},{4,0},{8,12},{12,8},{16,20},{20,16},{24,28},{28,24},{1,5},{5... | collective-permute-start | bytes 1572872 | tf_op jit(solution)/shard_map/ppermute | solution.py:310
  160.7 6.6 %collective-permute-start.43 = (bf16[128,1024]{1,0:T(8,128)(2,1)S(1)}, bf16[128,1024]{1,0:T(8,128)(2,1)S(1)}, u32[]{:S(2)}, u32[]{:S(2)}) collective-permute-start(bf16[128,1024]{1,0:T(8,128)(2,1)S(1)} %fusion.2), channel_id=1, source_target_pairs={{0,4},{4,0},{8,12},{12,8},{16,20},{20,16},{24,28},{28,24},{1,5},{5... | collective-permute-start | bytes 786440 | tf_op jit(solution)/shard_map/ppermute | solution.py:310
  162.3 16.9 %collective-permute-start.24 = (bf16[512,512]{1,0:T(8,128)(2,1)S(1)}, bf16[512,512]{1,0:T(8,128)(2,1)S(1)}, u32[]{:S(2)}, u32[]{:S(2)}) collective-permute-start(bf16[512,512]{1,0:T(8,128)(2,1)S(1)} %copy-done.4), channel_id=1, source_target_pairs={{0,1},{1,0},{2,3},{3,2},{4,5},{5,4},{6,7},{7,6},{8,9},{9,8},{10,11... | collective-permute-start | bytes 1572872 | tf_op jit(solution)/shard_map/ppermute | solution.py:323
  163.4 14.8 %collective-permute-start.27 = (bf16[512,512]{1,0:T(8,128)(2,1)S(1)}, bf16[512,512]{1,0:T(8,128)(2,1)S(1)}, u32[]{:S(2)}, u32[]{:S(2)}) collective-permute-start(bf16[512,512]{1,0:T(8,128)(2,1)S(1)} %copy-done.26), channel_id=1, source_target_pairs={{0,1},{1,0},{2,3},{3,2},{4,5},{5,4},{6,7},{7,6},{8,9},{9,8},{10,11... | collective-permute-start | bytes 1572872 | tf_op jit(solution)/shard_map/ppermute | solution.py:323
  163.9 15.6 %collective-permute-start.29 = (bf16[512,512]{1,0:T(8,128)(2,1)S(1)}, bf16[512,512]{1,0:T(8,128)(2,1)S(1)}, u32[]{:S(2)}, u32[]{:S(2)}) collective-permute-start(bf16[512,512]{1,0:T(8,128)(2,1)S(1)} %collective-permute-done.28.across), channel_id=1, source_target_pairs={{0,1},{1,0},{2,3},{3,2},{4,5},{5,4},{6,7},{7,6},{8,9},{9,8},{10,11... | collective-permute-start | bytes 1572872 | tf_op jit(solution)/shard_map/ppermute | solution.py:323
  164.0 19.0 %collective-permute-start.26 = (bf16[512,512]{1,0:T(8,128)(2,1)S(1)}, bf16[512,512]{1,0:T(8,128)(2,1)S(1)}, u32[]{:S(2)}, u32[]{:S(2)}) collective-permute-start(bf16[512,512]{1,0:T(8,128)(2,1)S(1)} %collective-permute-done.25.across), channel_id=1, source_target_pairs={{0,1},{1,0},{2,3},{3,2},{4,5},{5,4},{6,7},{7,6},{8,9},{9,8},{10,11... | collective-permute-start | bytes 1572872 | tf_op jit(solution)/shard_map/ppermute | solution.py:323
  168.7 6.4 %collective-permute-start.40 = (bf16[128,1024]{1,0:T(8,128)(2,1)S(1)}, bf16[128,1024]{1,0:T(8,128)(2,1)S(1)}, u32[]{:S(2)}, u32[]{:S(2)}) collective-permute-start(bf16[128,1024]{1,0:T(8,128)(2,1)S(1)} %get-tuple-element.95), channel_id=1, source_target_pairs={{0,2},{1,3},{2,0},{3,1},{4,6},{5,7},{6,4},{7,5},{8,10},{9,11},{10,... | collective-permute-start | bytes 786440 | tf_op jit(solution)/shard_map/ppermute | solution.py:319
  175.1 8.0 %collective-permute-start.37 = (bf16[64,512]{1,0:T(8,128)(2,1)S(1)}, bf16[64,512]{1,0:T(8,128)(2,1)S(1)}, u32[]{:S(2)}, u32[]{:S(2)}) collective-permute-start(bf16[64,512]{1,0:T(8,128)(2,1)S(1)} %get-tuple-element.102), channel_id=1, source_target_pairs={{0,24},{4,28},{8,0},{12,4},{16,8},{20,12},{24,16},{28,20},{1,25},{... | collective-permute-start | bytes 196616 | tf_op jit(solution)/shard_map/ppermute | solution.py:315
  178.2 15.2 %collective-permute-start.36 = (bf16[64,512]{1,0:T(8,128)(2,1)S(1)}, bf16[64,512]{1,0:T(8,128)(2,1)S(1)}, u32[]{:S(2)}, u32[]{:S(2)}) collective-permute-start(bf16[64,512]{1,0:T(8,128)(2,1)S(1)} %get-tuple-element.103), channel_id=1, source_target_pairs={{0,16},{4,20},{8,24},{12,28},{16,0},{20,4},{24,8},{28,12},{1,17},{... | collective-permute-start | bytes 196616 | tf_op jit(solution)/shard_map/ppermute | solution.py:315
  179.2 14.2 %collective-permute-start.33 = (bf16[64,512]{1,0:T(8,128)(2,1)S(1)}, bf16[64,512]{1,0:T(8,128)(2,1)S(1)}, u32[]{:S(2)}, u32[]{:S(2)}) collective-permute-start(bf16[64,512]{1,0:T(8,128)(2,1)S(1)} %get-tuple-element.104), channel_id=1, source_target_pairs={{0,8},{4,12},{8,16},{12,20},{16,24},{20,28},{24,0},{28,4},{1,9},{5... | collective-permute-start | bytes 196616 | tf_op jit(solution)/shard_map/ppermute | solution.py:315
  179.6 16.4 %collective-permute-start.45 = (bf16[64,1024]{1,0:T(8,128)(2,1)S(1)}, bf16[64,1024]{1,0:T(8,128)(2,1)S(1)}, u32[]{:S(2)}, u32[]{:S(2)}) collective-permute-start(bf16[64,1024]{1,0:T(8,128)(2,1)S(1)} %get-tuple-element.98), channel_id=1, source_target_pairs={{0,24},{4,28},{8,0},{12,4},{16,8},{20,12},{24,16},{28,20},{1,25},{... | collective-permute-start | bytes 393224 | tf_op jit(solution)/shard_map/ppermute | solution.py:315
  183.0 13.0 %collective-permute-start.44 = (bf16[64,1024]{1,0:T(8,128)(2,1)S(1)}, bf16[64,1024]{1,0:T(8,128)(2,1)S(1)}, u32[]{:S(2)}, u32[]{:S(2)}) collective-permute-start(bf16[64,1024]{1,0:T(8,128)(2,1)S(1)} %get-tuple-element.99), channel_id=1, source_target_pairs={{0,16},{4,20},{8,24},{12,28},{16,0},{20,4},{24,8},{28,12},{1,17},{... | collective-permute-start | bytes 393224 | tf_op jit(solution)/shard_map/ppermute | solution.py:315
  183.1 12.9 %collective-permute-start.41 = (bf16[64,1024]{1,0:T(8,128)(2,1)S(1)}, bf16[64,1024]{1,0:T(8,128)(2,1)S(1)}, u32[]{:S(2)}, u32[]{:S(2)}) collective-permute-start(bf16[64,1024]{1,0:T(8,128)(2,1)S(1)} %get-tuple-element.100), channel_id=1, source_target_pairs={{0,8},{4,12},{8,16},{12,20},{16,24},{20,28},{24,0},{28,4},{1,9},{5... | collective-permute-start | bytes 393224 | tf_op jit(solution)/shard_map/ppermute | solution.py:315
  (38 other events, 464.2 us)
where the time goes:
time: 200 us; the launch traced here: 199 us
  waiting for transfers between devices  67.4 us (34%)
  Pallas kernels  58.7 us (29%)
  starting transfers between devices  45.8 us (23%)
  other arithmetic  15.5 us (8%)
  local copies, waits for them, and re-layouts  10.6 us (5%)
    pallas_call x8, Pallas kernels, call(): pl.pallas_call(body, out_shape=outs, grid_spec=pltpu.PrefetchScalarGridSp...  58.7 us
    ppermute x10, waiting for transfers between devices, over_y(): return lax.ppermute(value, 'mp', [(i, i ^ 2) for i in range(4)])  39 us
    ppermute x12, starting transfers between devices, over_z(): return lax.ppermute(value, 'dp', [(i, (i + 2 * k) % n) for i in range(n)])  16.9 us
    ppermute x12, waiting for transfers between devices, over_z(): return lax.ppermute(value, 'dp', [(i, (i + 2 * k) % n) for i in range(n)])  15.9 us
    convert_element_type x10, other arithmetic, add(): return (a.astype(F32) + b.astype(F32)).astype(BF)  11.5 us
    ppermute x10, starting transfers between devices, over_y(): return lax.ppermute(value, 'mp', [(i, i ^ 2) for i in range(4)])  10.9 us
    ppermute x8, waiting for transfers between devices, over_x(): return lax.ppermute(value, 'dp', [(i, i ^ 1) for i in range(n)])  9.42 us
    ppermute x8, starting transfers between devices, over_x(): return lax.ppermute(value, 'dp', [(i, i ^ 1) for i in range(n)])  9.39 us
  transfers between devices with their start and end apart: 51, of which 18 were waited for; matrix products, arithmetic and copies ran while one was open for 10% of the time, Pallas kernels for 20%

commit v1 on v0

v1 whole, which is shorter than its diff:
```python
import functools

import jax
import jax.numpy as jnp
from jax import lax
from jax.experimental import pallas as pl
from jax.experimental.pallas import tpu as pltpu
from jax.sharding import PartitionSpec as P

HD = 64
STEP = 5
TILE = 128
EPS = 1e-06
GELU = 0.79788456
CUBIC = 0.044715
BF = jnp.bfloat16
F32 = jnp.float32


def nn(a, b):
    return lax.dot_general(a, b, (((1,), (0,)), ((), ())), preferred_element_type=F32)


def nt(a, b):
    return lax.dot_general(a, b, (((1,), (1,)), ((), ())), preferred_element_type=F32)


def tn(a, b):
    return lax.dot_general(a, b, (((0,), (0,)), ((), ())), preferred_element_type=F32)


def root_scale(values):
    return lax.rsqrt(jnp.mean(values * values, axis=-1, keepdims=True) + EPS)


def call(body, outs, ins, where, scratch=(), outside=(), limit=24, flops=0, moved=0, trans=0):
    vmem = pl.BlockSpec(memory_space=pltpu.VMEM)
    specs = [pl.BlockSpec(memory_space=pltpu.HBM) if k in outside else vmem for k in range(len(ins))]
    return pl.pallas_call(
        body,
        out_shape=outs,
        in_specs=[pl.BlockSpec(memory_space=pltpu.SMEM)] + specs,
        out_specs=[vmem] * len(outs),
        scratch_shapes=list(scratch),
        compiler_params=pltpu.CompilerParams(vmem_limit_bytes=limit * 1024 * 1024),
        cost_estimate=pl.CostEstimate(flops=flops, bytes_accessed=moved, transcendentals=trans),
    )(where, *ins)


def row_copy(array, row, target, sem):
    return pltpu.make_async_copy(array.at[row], target, sem)


def order_of_blocks(count):
    steps = range(1, count // 2)
    first = [(0, 0), (1, 0), (0, count // 2)] + [(c, k) for k in steps for c in (0, 1)]
    return first + [(1, count // 2)] + [(1 - c, -k) for k in steps for c in (0, 1)]


def place(pieces, core, z, x, count, rows, store):
    own, near, near_too, far, far_too = pieces
    half = far.shape[1]
    for ref, flip, x_off, y_off, at_column in (
        (own, 0, 0, 0, 0),
        (near, 0, 1 - core, core, 0),
        (near_too, 1, core, 1 - core, 0),
        (far, 0, 1, 1, core * half),
        (far_too, 1, 1, 1, (1 - core) * half),
    ):
        step = (2 * core - 1) * (1 - 2 * flip)
        x_at = lax.rem(x + x_off, 2)
        for number, (distance, k) in enumerate(order_of_blocks(count)):
            z_at = lax.rem(z + count + step * k, count)
            at = pl.multiple_of((z_at * 2 + x_at) * rows, rows)
            group = (distance ^ flip) + 2 * y_off
            for c in range(0, ref.shape[1], 128):
                store(group, at, at_column + c, ref[number * rows : (number + 1) * rows, c : c + 128])


def in_relative_rows(source, target, z, x, count, rows, x_off):
    x_at = lax.rem(x + x_off, 2)
    for k in range(count):
        z_at = lax.rem(z + k, count)
        at = pl.multiple_of((z_at * 2 + x_at) * rows, rows)
        target[k * rows : (k + 1) * rows, :] = source[pl.ds(at, rows), :]


def attention_kernel(count, rows, place_ref, x_any, seg_ref, *refs):
    h_ref, q_ref, k_ref, v_ref, o_ref, p_ref, w_ref, x_row, flat, o_flat, sem = refs[5:]
    z, x = place_ref[0], place_ref[1]
    copy = row_copy(x_any, place_ref[2], x_row, sem)
    copy.start()

    def store(group, at, c, block):
        w_ref[pl.ds(at, rows), pl.ds(pl.multiple_of(c * 4 + group * 128, 128), 128)] = block

    place(refs[:5], lax.rem(place_ref[2], 2), z, x, count, rows, store)
    copy.wait()
    states = x_row[...].astype(F32)
    unit = (states * root_scale(states)).astype(BF)
    v = nn(unit, w_ref[:, 1024:1536]).astype(BF)
    v_ref[...] = v
    flat[...] = v.T
    q_ref[...] = (nn(unit, w_ref[:, :512]) * HD**-0.5).astype(BF)
    k_ref[...] = nn(unit, w_ref[:, 512:1024]).astype(BF)
    lane = lax.broadcasted_iota(jnp.int32, (1, 128), 1)
    sides = [(lane // HD == j).astype(BF) for j in range(2)]
    tiles = q_ref.shape[0] // TILE
    segment = seg_ref[pl.ds(place_ref[2], 1), :]
    down = [column(segment[:, i * TILE : (i + 1) * TILE]) for i in range(tiles)]
    for i in range(tiles):
        first, last = max(0, i - 1), min(tiles, i + 2)
        window = slice(first * TILE, last * TILE)
        here = slice(i * TILE, (i + 1) * TILE)
        mask = jnp.concatenate(down[first:last], axis=0) == segment[:, here]
        for m in range(4):
            at = slice(m * 128, m * 128 + 128)
            q, k = q_ref[here, at], k_ref[window, at]
            for j in range(2):
                s = jnp.where(mask, nt(k, q * sides[j]), -1e30)
                e = jnp.exp(s - jnp.max(s, axis=0, keepdims=True))
                p = (e * (1.0 / jnp.sum(e, axis=0, keepdims=True))).astype(BF)
                p_ref[m * 2 + j, i, : s.shape[0], :] = p
                head = slice(m * 128 + j * HD, m * 128 + (j + 1) * HD)
                o_flat[head, here] = nn(flat[head, window], p).astype(BF)
    o = o_flat[...].T
    o_ref[...] = o
    h_ref[...] = states + nt(o, w_ref[:, 1536:2048])


def feed_kernel(count, rows, place_ref, h_ref, c_any, *refs):
    far_own, far_sib, g_ref, dz_ref, w_ref, u_near, c_near = refs[5:12]
    c_row, u_flat, c_flat, u_far, c_far, sem = refs[12:]
    z, x = place_ref[0], place_ref[1]
    width = w_ref.shape[1] // 2
    cols = width // 4
    copy = row_copy(c_any, place_ref[2], c_row, sem)
    copy.start()

    def store(group, at, c, block):
        to = c // cols * width + group * cols + c % cols if isinstance(c, int) else None
        if to is None:
            to = lax.div(c, cols) * width + group * cols + lax.rem(c, cols)
        w_ref[pl.ds(at, rows), pl.ds(pl.multiple_of(to, 128), 128)] = block

    place(refs[:5], lax.rem(place_ref[2], 2), z, x, count, rows, store)
    h = h_ref[...]
    low = (h * root_scale(h)).astype(BF)
    u_flat[...] = low.T
    copy.wait()
    back = c_row[...]
    c_flat[...] = back.T
    for source, near, far in ((u_flat, u_near, u_far), (c_flat, c_near, c_far)):
        in_relative_rows(source, near, z, x, count, rows, 0)
        in_relative_rows(source, far, z, x, count, rows, 1)
    for m in range(4):
        at = slice(m * cols, (m + 1) * cols)
        inner = nn(low, w_ref[:, at])
        square = inner * inner
        bent = jnp.tanh(inner * (GELU + GELU * CUBIC * square))
        half = 0.5 + 0.5 * bent
        g_ref[:, at] = (inner * half).astype(BF)
        slope = half + (inner * half) * (1.0 - bent) * (GELU + 3.0 * GELU * CUBIC * square)
        dz_ref[:, at] = (nn(back, w_ref[:, width + m * cols : width + (m + 1) * cols]) * slope).astype(BF)
        target = (far_own, far_sib)[m % 2]
        target[0, m // 2] = nn(u_far[...], dz_ref[:, at]).astype(BF)
        target[1, m // 2] = nn(c_far[...], g_ref[:, at]).astype(BF)


def feed_rest_kernel(place_ref, h_ref, g_ref, dz_ref, w_ref, u_near, c_near, c_any, *refs):
    near_own, near_sib, row_ref, dh_ref, gain_ref, c_row, sem = refs
    width = w_ref.shape[1] // 2
    cols = width // 4
    copy = row_copy(c_any, place_ref[2], c_row, sem)
    copy.start()
    h = h_ref[...]
    row_ref[...] = (h + nt(g_ref[...], w_ref[:, width:])).astype(BF)
    pushed = nt(dz_ref[...], w_ref[:, :width])
    for m in range(4):
        at = slice(m * cols, (m + 1) * cols)
        target = (near_own, near_sib)[m % 2]
        target[0, m // 2] = nn(u_near[...], dz_ref[:, at]).astype(BF)
        target[1, m // 2] = nn(c_near[...], g_ref[:, at]).astype(BF)
    scale = root_scale(h)
    unit = h * scale
    both = pushed * unit
    gain_ref[...] = jnp.broadcast_to(jnp.sum(both, axis=0, keepdims=True), gain_ref.shape)
    copy.wait()
    back = c_row[...].astype(F32)
    dh_ref[...] = back + scale * (pushed - unit * jnp.mean(both, axis=-1, keepdims=True))


def attention_back_kernel(count, rows, place_ref, x_any, dh_ref, q_ref, k_ref, v_ref, o_ref, p_ref, w_ref, *refs):
    gain_in, bg_ref, row_ref, near_own, far_own, near_sib, far_sib = refs[:7]
    x_row, flat_d, flat_u, near, far, do_ref, k_flat, dq_flat, ds_ref, dqkv, sem = refs[7:]
    z, x = place_ref[0], place_ref[1]
    copy = row_copy(x_any, place_ref[2], x_row, sem)
    copy.start()
    low = dh_ref[...].astype(BF)
    do_ref[...] = nn(low, w_ref[:, 1536:2048]).astype(BF)
    k_flat[...] = k_ref[...].T
    flat_d[...] = low.T

    def products(part, right):
        at = slice(part * 128, part * 128 + 128)
        for left, targets in ((near, (near_own, near_sib)), (far, (far_own, far_sib))):
            value = nn(left[...], right)
            for m in range(4):
                targets[m % 2][m // 2, : left.shape[0], at] = value[:, m * 128 : m * 128 + 128].astype(BF)

    in_relative_rows(flat_d, near, z, x, count, rows, 0)
    in_relative_rows(flat_d, far, z, x, count, rows, 1)
    products(3, o_ref[...])
    copy.wait()
    states = x_row[...].astype(F32)
    scale = root_scale(states)
    unit = states * scale
    flat_u[...] = unit.astype(BF).T
    in_relative_rows(flat_u, near, z, x, count, rows, 0)
    in_relative_rows(flat_u, far, z, x, count, rows, 1)
    lane = lax.broadcasted_iota(jnp.int32, (1, 128), 1)
    sides = [(lane // HD == j).astype(BF) for j in range(2)]
    select = (lax.broadcasted_iota(jnp.int32, (8, 128), 1) // HD == lax.broadcasted_iota(jnp.int32, (8, 128), 0)).astype(BF)
    tiles = do_ref.shape[0] // TILE
    for m in range(4):
        at = slice(m * 128, m * 128 + 128)
        for i in range(tiles):
            first, last = max(0, i - 1), min(tiles, i + 2)
            window = slice(first * TILE, last * TILE)
            here = slice(i * TILE, (i + 1) * TILE)
            v, do = v_ref[window, at], do_ref[here, at]
            delta = nt(select, do * o_ref[here, at])
            for j in range(2):
                p = p_ref[m * 2 + j, i, : v.shape[0], :].astype(F32)
                ds = (p * (nt(v, do * sides[j]) - delta[j : j + 1, :])).astype(BF)
                ds_ref[j, i, : v.shape[0], :] = ds
                head = slice(m * 128 + j * HD, m * 128 + (j + 1) * HD)
                dq_flat[head, here] = (nn(k_flat[head, window], ds) * HD**-0.5).astype(BF)
        for t in range(tiles):
            blocks = [(i, j) for i in range(max(0, t - 1), min(tiles, t + 2)) for j in range(2)]
            there = slice(t * TILE, (t + 1) * TILE)

            def rows_of(i):
                return slice((t - max(0, i - 1)) * TILE, (t - max(0, i - 1) + 1) * TILE)

            left = jnp.concatenate([ds_ref[j, i, rows_of(i), :] for i, j in blocks], axis=1)
            right = jnp.concatenate([q_ref[i * TILE : (i + 1) * TILE, at] * sides[j] for i, j in blocks], axis=0)
            dqkv[there, 512 + m * 128 : 640 + m * 128] = nn(left, right).astype(BF)
            left = jnp.concatenate([p_ref[m * 2 + j, i, rows_of(i), :] for i, j in blocks], axis=1)
            right = jnp.concatenate([do_ref[i * TILE : (i + 1) * TILE, at] * sides[j] for i, j in blocks], axis=0)
            dqkv[there, 1024 + m * 128 : 1152 + m * 128] = nn(left, right).astype(BF)
    dqkv[:, :512] = dq_flat[...].T
    for part in range(3):
        products(part, dqkv[:, part * 512 : part * 512 + 512])
    pushed = nt(dqkv[...], w_ref[:, :1536])
    both = pushed * unit
    out = dh_ref[...] + scale * (pushed - unit * jnp.mean(both, axis=-1, keepdims=True))
    bg_ref[...] = out
    row_ref[...] = out.astype(BF)
    gains = jnp.concatenate(
        [jnp.sum(both, axis=0, keepdims=True), gain_in[0:1, :], jnp.zeros((14, out.shape[1]), F32)], axis=0
    )
    width, group = out.shape[1], 2 * rows
    gains = pltpu.roll(gains, lax.rem(width - z * group, width), 1)
    lane = lax.broadcasted_iota(jnp.int32, gains.shape, 1)
    swapped = jnp.where(lax.rem(lane, group) < rows, pltpu.roll(gains, width - rows, 1), pltpu.roll(gains, rows, 1))
    here, there = jnp.where(x == 0, gains, swapped), jnp.where(x == 0, swapped, gains)
    for targets, value in (((near_own, near_sib), here), ((far_own, far_sib), there)):
        for target in targets:
            for y in range(2):
                target[y, near.shape[0] :, :] = value.astype(BF)


def column(row):
    n = row.shape[1]
    here = lax.broadcasted_iota(jnp.int32, (n, n), 0) == lax.broadcasted_iota(jnp.int32, (n, n), 1)
    return jnp.sum(jnp.where(here, row, jnp.zeros_like(row)), axis=1, keepdims=True)


def gain_column(gain, k):
    return column(gain[k : k + 1, :].astype(BF).astype(F32))


def adam(master, moment, second, gradient, rate, decay):
    moment_new = 0.5 * moment + 0.5 * gradient
    second_new = 0.6 * second + 0.4 * gradient * gradient
    update = moment_new / (1.0 - 0.5**STEP) / (jnp.sqrt(second_new / (1.0 - 0.6**STEP)) + 1e-08)
    return master - rate * (update + decay * master), moment_new, second_new


def adam_into(outs, state, gradient, rate, decay):
    master, moment, second = adam(*state, gradient, rate, decay)
    outs[0][...] = master
    outs[1][...] = moment
    outs[2][...] = second
    outs[3][...] = master.astype(BF)


def total(refs):
    whole = refs[0][...].astype(F32)
    for ref in refs[1:]:
        whole = whole + ref[...].astype(F32)
    return whole


def feed_update_kernel(count, place_ref, *refs):
    count += 1
    terms, gain, state, outs = refs[:count], refs[count], refs[count + 1 : count + 7], refs[count + 7 :]
    grad = total(terms)
    scaled = grad[0] * gain_column(gain, 1)
    adam_into(outs[:4], [r[...] for r in state[:3]], scaled, 0.05, 0.1)
    adam_into(outs[4:], [r[...] for r in state[3:]], grad[1], 0.025, 0.1)


def attention_update_kernel(count, place_ref, *refs):
    terms, state, outs = refs[:count], refs[count : count + 9], refs[count + 9 :]
    whole = total(terms)
    gain, size = state[0], state[0].shape[1]
    grad = whole[:size]
    gains = []
    for k in range(2):
        at = size + k
        parts = [ref[at : at + 1, 2 * size * n : 2 * size * n + size].astype(F32) for n, ref in enumerate(terms)]
        gains.append(sum(parts[1:], parts[0]))
    gains = jnp.concatenate(gains, axis=0) / gain[...].astype(BF).astype(F32)
    adam_into(outs[8:], [r[...] for r in state[:3]], gains, 0.25, 0.0)
    scale = gain_column(gain, 0)
    state = state[3:]
    for part in range(3):
        master, moment, second = adam(
            *[r[part] for r in state[:3]], grad[:, part * 128 : part * 128 + 128] * scale, 0.05, 0.1
        )
        outs[0][part] = master
        outs[1][part] = moment
        outs[2][part] = second
        outs[3][part] = master.astype(BF)
    adam_into(outs[4:8], [r[...] for r in state[3:]], grad[:, 384:512], 0.3, 0.1)


def prepare_kernel(place_ref, *refs):
    whole, first, second = refs[5:8]
    local, sems = refs[8:13], refs[13]
    copies = [pltpu.make_async_copy(refs[k], local[k], sems.at[k]) for k in range(5)]
    for copy in copies:
        copy.start()
    for copy in copies:
        copy.wait()
    gain, attend, mixing, expand, shrink = local
    gain_one = gain_column(gain, 0)
    gain_two = gain_column(gain, 1)
    cols = expand.shape[1]
    for part in range(3):
        first[:, part * 128 : part * 128 + 128] = (attend[part].astype(BF).astype(F32) * gain_one).astype(BF)
    first[:, 384:512] = mixing[...].astype(BF)
    second[:, :cols] = (expand[...].astype(BF).astype(F32) * gain_two).astype(BF)
    second[:, cols:] = shrink[...].astype(BF)
    whole[:, :512] = first[...]
    whole[:, 512:] = second[...]


def put_kernel(messages, place_ref, *refs):
    step = pl.program_id(0)
    for k, ref in enumerate(refs[-1 - messages : -1]):

        @pl.when(step == k)
        def _(ref=ref):
            refs[-1][0] = ref[...].astype(refs[-1].dtype)


def struct(shape, dtype):
    return jax.ShapeDtypeStruct(shape, dtype)


def over_x(value):
    n = lax.axis_size("dp")
    return lax.ppermute(value, "dp", [(i, i ^ 1) for i in range(n)])


def over_z(value, k):
    n = lax.axis_size("dp")
    return lax.ppermute(value, "dp", [(i, (i + 2 * k) % n) for i in range(n)])


def over_y(value):
    return lax.ppermute(value, "mp", [(i, i ^ 2) for i in range(4)])


def over_core(value):
    return lax.ppermute(value, "mp", [(i, i ^ 1) for i in range(4)])


def two_ways(value, first, second):
    n = lax.axis_size("dp")
    pairs = [(dp * 4 + mp, (first, second)[mp % 2](dp, mp)) for dp in range(n) for mp in range(4)]
    return lax.ppermute(value, ("dp", "mp"), [(source, dp * 4 + mp) for source, (dp, mp) in pairs])


def gather_column(block, sibling, count):
    n = 2 * count
    chip = jnp.concatenate([block, sibling], axis=0)
    got = [over_z(block, count // 2)]
    for k in range(1, count // 2):
        got.append(two_ways(chip, lambda d, m, k=k: ((d + 2 * k) % n, m), lambda d, m, k=k: ((d - 2 * k) % n, m)))
    got = jnp.concatenate(got, axis=0)
    return jnp.concatenate([chip, got, over_core(got)], axis=0)


def gather_near(column):
    return two_ways(column, lambda d, m: (d ^ 1, m), lambda d, m: (d, m ^ 2))


def gather_far(near, core):
    half = near.shape[1] // 2
    part = lax.dynamic_slice_in_dim(near, core * half, half, 1)
    return two_ways(part, lambda d, m: (d, m ^ 2), lambda d, m: (d ^ 1, m))


def after(values, *others):
    return lax.optimization_barrier((values, others))[0]


def add(*terms):
    whole = terms[0].astype(F32)
    for term in terms[1:]:
        whole = whole + term.astype(F32)
    return whole.astype(BF)


def scatter_start(grads):
    return add(grads[1], over_core(grads[3]))


def scatter_next(grads, far):
    near, got = grads[0], over_core(grads[2])
    return add(near[0], got[0], far[0]), add(near[1], got[1], far[1])


def put(array, messages, offset, where):
    size = (messages[0].shape[0] // TILE * TILE, messages[0].shape[1])
    kept = [] if offset == 0 else [array]
    return pl.pallas_call(
        functools.partial(put_kernel, len(messages)),
        out_shape=struct((4,) + size, array if offset == 0 else array.dtype),
        grid_spec=pltpu.PrefetchScalarGridSpec(
            num_scalar_prefetch=1,
            grid=(len(messages),),
            in_specs=[pl.BlockSpec(memory_space=pl.ANY)] * len(kept)
            + [pl.BlockSpec(size, lambda i, s: (0, 0))] * len(messages),
            out_specs=pl.BlockSpec((1,) + size, lambda i, s: (s[2] ^ (offset + i), 0, 0)),
        ),
        input_output_aliases={1: 0} if kept else {},
        compiler_params=pltpu.CompilerParams(vmem_limit_bytes=16 * 1024 * 1024),
        cost_estimate=pl.CostEstimate(flops=0, bytes_accessed=16 * messages[0].size, transcendentals=0),
    )(where, *kept, *messages)


def on_device(
    blocks,
    block_segment,
    upstream,
    attend_master,
    attend_first,
    attend_second,
    mixing_master,
    mixing_first,
    mixing_second,
    expand_master,
    expand_first,
    expand_second,
    shrink_master,
    shrink_first,
    shrink_second,
    gains_master,
    gains_first,
    gains_second,
):
    dp_size = lax.axis_size("dp")
    count = dp_size // 2
    rows = attend_master.shape[1]
    length, width = blocks.shape[1:]
    cols = expand_master.shape[1]
    dp_at, mp_at = lax.axis_index("dp"), lax.axis_index("mp")
    where = jnp.stack([dp_at // 2, dp_at % 2, mp_at]).astype(jnp.int32)

    masters = [gains_master, attend_master, mixing_master.T, expand_master, shrink_master.T]
    whole, first, second = call(
        prepare_kernel,
        [struct((rows, 512 + 2 * cols), BF), struct((rows, 512), BF), struct((rows, 2 * cols), BF)],
        masters,
        where,
        scratch=[pltpu.VMEM(a.shape, F32) for a in masters] + [pltpu.SemaphoreType.DMA((5,))],
        outside=range(5),
        limit=60,
        moved=2 << 20,
    )
    core = mp_at % 2
    sibling = over_core(whole)
    column_one = gather_column(first, sibling[:, :512], count)
    column_two = gather_column(second, sibling[:, 512:], count)
    near_one, near_two = gather_near(column_one), gather_near(column_two)
    far_one = gather_far(after(near_one, column_two), core)
    sib_far_one = over_core(far_one)
    tiles = length // TILE
    half = count * rows
    h, q, k, v, o, probs, weights = call(
        functools.partial(attention_kernel, count, rows),
        [
            struct((length, width), F32),
            *[struct((length, 512), BF)] * 4,
            struct((8, tiles, 3 * TILE, TILE), BF),
            struct((width, 2048), BF),
        ],
        [blocks, block_segment, column_one, near_one, over_core(near_one), far_one, sib_far_one],
        where,
        scratch=[pltpu.VMEM((length, width), BF), *[pltpu.VMEM((512, length), BF)] * 2, pltpu.SemaphoreType.DMA],
        outside=(0,),
        flops=6 * 10**9,
        moved=12 << 20,
        trans=10**6,
    )
    far_two = gather_far(after(near_two, h), core)
    pair = struct((2, 2, half, cols), BF)
    far_own, far_sib, g, dz, w_feed, u_near, c_near = call(
        functools.partial(feed_kernel, count, rows),
        [
            pair,
            pair,
            *[struct((length, 4 * cols), BF)] * 2,
            struct((width, 8 * cols), BF),
            *[struct((half, length), BF)] * 2,
        ],
        [h, upstream, column_two, near_two, over_core(near_two), far_two, over_core(far_two)],
        where,
        scratch=[
            pltpu.VMEM((length, width), BF),
            *[pltpu.VMEM((width, length), BF)] * 2,
            *[pltpu.VMEM((half, length), BF)] * 2,
            pltpu.SemaphoreType.DMA,
        ],
        outside=(1,),
        flops=4 * 10**9,
        moved=12 << 20,
        trans=10**6,
    )
    send = add(far_own, over_core(far_sib))
    g = after(g, send)
    near_own, near_sib, row, dh, gain_two = call(
        feed_rest_kernel,
        [
            pair,
            pair,
            struct((length, width), BF),
            struct((length, width), F32),
            struct((8, width), F32),
        ],
        [h, g, dz, w_feed, u_near, c_near, upstream],
        where,
        scratch=[pltpu.VMEM((length, width), BF), pltpu.SemaphoreType.DMA],
        outside=(6,),
        flops=4 * 10**9,
        moved=12 << 20,
    )
    far = over_x(send)
    row_sib, row_across = over_core(row), over_y(row)
    one = struct((2, half + 16, 512), BF)
    bg, row_low, *grads_one = call(
        functools.partial(attention_back_kernel, count, rows),
        [struct((length, width), F32), struct((length, width), BF), one, one, one, one],
        [blocks, dh, q, k, v, o, probs, weights, gain_two],
        where,
        scratch=[
            pltpu.VMEM((length, width), BF),
            *[pltpu.VMEM((width, length), BF)] * 2,
            *[pltpu.VMEM((half, length), BF)] * 2,
            pltpu.VMEM((length, 512), BF),
            *[pltpu.VMEM((512, length), BF)] * 2,
            pltpu.VMEM((2, tiles, 3 * TILE, TILE), BF),
            pltpu.VMEM((length, 1536), BF),
            pltpu.SemaphoreType.DMA,
        ],
        outside=(0,),
        flops=8 * 10**9,
        moved=12 << 20,
    )
    bg, row_low, grads_one = after((bg, row_low, grads_one), row_across)
    result = put(BF, [row, row_sib], 0, where)
    result = put(result, [row_across, over_core(row_across)], 2, where)
    send_one = scatter_start(grads_one)
    far_one = over_x(send_one)
    low_sib, low_across = over_core(row_low), over_y(row_low)
    low_far = over_core(after(low_across, far_one))
    bg = put(F32, [bg, low_sib], 0, where)
    blocks_grad = put(bg, [low_across, low_far], 2, where)

    got = over_core(near_sib)
    units = [
        add(*[part[:, :, k * rows : (k + 1) * rows] for part in (near_own, got, far)]) for k in range(count)
    ]
    units = [over_z(unit, k) if k else unit for k, unit in enumerate(units)]
    kept_one, send_one_y = scatter_next(grads_one, far_one)
    units = after(units, far_one, result)
    send = add(*[unit[:, 1] for unit in units])
    terms_two = [unit[:, 0] for unit in units] + [over_y(send)]
    sum_one = add(kept_one, over_y(send_one_y))
    parts = [jnp.concatenate([sum_one[k * rows : (k + 1) * rows], sum_one[half:]], axis=0) for k in range(count)]
    terms_one = [over_z(part, k) if k else part for k, part in enumerate(parts)]

    def quad(shape):
        return [struct(shape, F32)] * 3 + [struct(shape, BF)]

    feed_new = call(
        functools.partial(feed_update_kernel, count),
        quad((rows, cols)) * 2,
        [
            *terms_two,
            gains_master,
            expand_master,
            expand_first,
            expand_second,
            shrink_master.T,
            shrink_first.T,
            shrink_second.T,
        ],
        where,
        moved=3 << 20,
    )
    terms_one = after(terms_one, feed_new[0], blocks_grad)
    attention_new = call(
        functools.partial(attention_update_kernel, count),
        quad(attend_master.shape) + quad((rows, 128)) + quad((2, rows)),
        [
            *terms_one,
            gains_master,
            gains_first,
            gains_second,
            attend_master,
            attend_first,
            attend_second,
            mixing_master.T,
            mixing_first.T,
            mixing_second.T,
        ],
        where,
        moved=3 << 20,
    )
    return (
        result,
        blocks_grad,
        *attention_new[:4],
        *[a.T for a in attention_new[4:8]],
        *feed_new[:4],
        *[a.T for a in feed_new[4:]],
        *attention_new[8:],
    )


def solution(mesh):
    rows = P("dp", None, None)
    attend, mixing, expand, gains = P(None, "dp", "mp"), P("mp", "dp"), P("dp", "mp"), P(None, "dp")
    kinds = (attend, mixing, expand, mixing, gains)
    in_specs = (rows, P("dp", None), rows) + tuple(k for k in kinds for _ in range(3))
    out_specs = (rows, rows) + tuple(k for k in kinds for _ in range(4))
    return jax.shard_map(on_device, mesh=mesh, in_specs=in_specs, out_specs=out_specs, check_vma=False)
```

time: 200 us -> 153 us (0.77)
  Pallas kernels: 58.7 us -> 42 us
  other arithmetic: 15.5 us -> 3.7 us
  waiting for transfers between devices: 67.4 us -> 60.1 us
  local copies, waits for them, and re-layouts: 10.6 us -> 3.84 us
  starting transfers between devices: 45.8 us -> 41.3 us
    ppermute x10 -> x4, waiting for transfers between devices: 39 us -> 13.7 us  [over_y(): return lax.ppermute(value, 'mp', [(i, i ^ 2) for i in range(4)])]
    ppermute x5 -> x6, waiting for transfers between devices: 3.11 us -> 21.5 us  [two_ways(): lax.ppermute(value, ('dp', 'mp'), [(source, dp * 4 + mp) for source, (dp,...]
    pallas_call x8 -> x11, Pallas kernels: 58.7 us -> 42 us  [the longest x7 35 us: call(): pl.pallas_call(body, out_shape=outs, in_specs=[pl.BlockSpec(memory_space=...]
    convert_element_type x12 -> x5, other arithmetic: 13.5 us -> 1.21 us  [add(): return whole.astype(BF)]
    ppermute x16 -> x15, waiting for transfers between devices: 0.04 us -> 10.4 us  [over_core(): return lax.ppermute(value, 'mp', [(i, i ^ 1) for i in range(4)])]
    ppermute x8 -> x2, waiting for transfers between devices: 9.42 us -> 0.6 us  [over_x(): return lax.ppermute(value, 'dp', [(i, i ^ 1) for i in range(n)])]
    ppermute x8 -> x2, starting transfers between devices: 9.39 us -> 2.14 us  [over_x(): return lax.ppermute(value, 'dp', [(i, i ^ 1) for i in range(n)])]
    ppermute x5 -> x6, starting transfers between devices: 5.72 us -> 11.6 us  [two_ways(): lax.ppermute(value, ('dp', 'mp'), [(source, dp * 4 + mp) for source, (dp,...]
  transfers between devices with their start and end apart: 51 -> 35, of which waited for: 18 -> 15; matrix products, arithmetic and copies ran while one was open for 10% -> 3% of each run, Pallas kernels for 20% -> 21%
where the time goes in v1:
time: 153 us; the launch traced here: 152 us
  waiting for transfers between devices  60.1 us (39%)
  Pallas kernels  42 us (27%)
  starting transfers between devices  41.3 us (27%)
  local copies, waits for them, and re-layouts  3.84 us (3%)
  other arithmetic  3.7 us (2%)
    pallas_call x7, Pallas kernels, call(): pl.pallas_call(body, out_shape=outs, in_specs=[pl.BlockSpec(memory_space=...  35 us
    ppermute x6, waiting for transfers between devices, two_ways(): lax.ppermute(value, ('dp', 'mp'), [(source, dp * 4 + mp) for source, (dp,...  21.5 us
    ppermute x8, starting transfers between devices, over_z(): return lax.ppermute(value, 'dp', [(i, (i + 2 * k) % n) for i in range(n)])  18.7 us
    ppermute x8, waiting for transfers between devices, over_z(): return lax.ppermute(value, 'dp', [(i, (i + 2 * k) % n) for i in range(n)])  13.9 us
    ppermute x4, waiting for transfers between devices, over_y(): return lax.ppermute(value, 'mp', [(i, i ^ 2) for i in range(4)])  13.7 us
    ppermute x6, starting transfers between devices, two_ways(): lax.ppermute(value, ('dp', 'mp'), [(source, dp * 4 + mp) for source, (dp,...  11.6 us
    ppermute x15, waiting for transfers between devices, over_core(): return lax.ppermute(value, 'mp', [(i, i ^ 1) for i in range(4)])  10.4 us
    ppermute x4, starting transfers between devices, over_y(): return lax.ppermute(value, 'mp', [(i, i ^ 2) for i in range(4)])  7.44 us
  transfers between devices with their start and end apart: 35, of which 15 were waited for; matrix products, arithmetic and copies ran while one was open for 3% of the time, Pallas kernels for 21%

profile of v1, /device:TPU:0, one launch (start us, length us, event | category | flops | bytes accessed | tf_op | source)
XLA Modules:
  0.0 152.3 jit_solution(3333180988252741148)
XLA Ops:
  1.3 2.6 %shard_map.345 = (bf16[64,1536]{1,0:T(8,128)(2,1)}, bf16[64,512]{1,0:T(8,128)(2,1)}, bf16[64,1024]{1,0:T(8,128)(2,1)}) custom-call(s32[3]{0:T(128)} %pad_add_fusion.place_ref, f32[2,64]{1,0:T(2,128)} %refs_4_.1, f32[3,64,128]{2,1,0:T(8,128)} %refs_7_.3, f32[64,128]{1,0:T(8,128)} %bitcast.38, f32[64,512]{1,0:T(8,128)} %refs_6_.2, f32[64,512]{1,0:T(8,128)} %bitcast.34), custom_call_target="tpu_custom_call" | custom-call | bytes 2097152 | tf_op jit(solution)/shard_map/pallas_call | solution.py:39
  3.9 4.1 %collective-permute-start.1 = (bf16[64,512]{1,0:T(8,128)(2,1)}, bf16[64,512]{1,0:T(8,128)(2,1)S(1)}, u32[]{:S(2)}, u32[]{:S(2)}) collective-permute-start(bf16[64,512]{1,0:T(8,128)(2,1)} %get-tuple-element.88), channel_id=1, source_target_pairs={{0,16},{4,20},{8,24},{12,28},{16,0},{20,4},{24,8},{28,12},{1,17},{... | collective-permute-start | bytes 196616 | tf_op jit(solution)/shard_map/ppermute | solution.py:381
  8.0 0.8 constant_dynamic-update-slice_fusion.4
  8.9 0.9 constant_dynamic-update-slice_fusion.9
  9.8 0.9 pad_maximum_fusion.3
  10.7 1.9 %collective-permute-start.2 = (bf16[128,512]{1,0:T(8,128)(2,1)S(1)}, bf16[128,512]{1,0:T(8,128)(2,1)S(1)}, u32[]{:S(2)}, u32[]{:S(2)}) collective-permute-start(bf16[128,512]{1,0:T(8,128)(2,1)S(1)} %pad_maximum_fusion.3), channel_id=1, source_target_pairs={{0,8},{1,25},{2,10},{3,27},{4,12},{5,29},{6,14},{7,31},{8,16},{9,1... | collective-permute-start | bytes 393224 | tf_op jit(solution)/shard_map/ppermute | solution.py:395
  12.6 0.9 pad_maximum_fusion.1
  13.6 1.6 %collective-permute-start.7 = (bf16[128,1024]{1,0:T(8,128)(2,1)S(1)}, bf16[128,1024]{1,0:T(8,128)(2,1)S(1)}, u32[]{:S(2)}, u32[]{:S(2)}) collective-permute-start(bf16[128,1024]{1,0:T(8,128)(2,1)S(1)} %pad_maximum_fusion.1), channel_id=1, source_target_pairs={{0,8},{1,25},{2,10},{3,27},{4,12},{5,29},{6,14},{7,31},{8,16},{9,1... | collective-permute-start | bytes 786440 | tf_op jit(solution)/shard_map/ppermute | solution.py:395
  15.2 3.8 %collective-permute-done.2 = bf16[128,512]{1,0:T(8,128)(2,1)S(1)} collective-permute-done((bf16[128,512]{1,0:T(8,128)(2,1)S(1)}, bf16[128,512]{1,0:T(8,128)(2,1)S(1)}, u32[]{:S(2)}, u32[]{:S(2)}) %collective-permute-start.2) | collective-permute-done | bytes 131104 | tf_op jit(solution)/shard_map/ppermute | solution.py:395
  19.1 1.4 collective-permute-done.3
  20.5 2.0 %collective-permute-start.4 = (bf16[512,512]{1,0:T(8,128)(2,1)S(1)}, bf16[512,512]{1,0:T(8,128)(2,1)S(1)}, u32[]{:S(2)}, u32[]{:S(2)}) collective-permute-start(bf16[512,512]{1,0:T(8,128)(2,1)S(1)} %constant_dynamic-update-slice_fusion.refs_0_), channel_id=1, source_target_pairs={{0,4},{1,3},{2,6},{3,1},{4,0},{5,7},{6,2},{7,5},{8,12},{9,11},{10,... | collective-permute-start | bytes 1572872 | tf_op jit(solution)/shard_map/ppermute | solution.py:395
  22.5 2.1 %collective-permute-done.7 = bf16[128,1024]{1,0:T(8,128)(2,1)S(1)} collective-permute-done((bf16[128,1024]{1,0:T(8,128)(2,1)S(1)}, bf16[128,1024]{1,0:T(8,128)(2,1)S(1)}, u32[]{:S(2)}, u32[]{:S(2)}) %collective-permute-start.7) | collective-permute-done | bytes 262176 | tf_op jit(solution)/shard_map/ppermute | solution.py:395
  24.9 1.4 collective-permute-done.8
  26.4 3.3 %collective-permute-done.4.refs_1_ = bf16[512,512]{1,0:T(8,128)(2,1)S(1)} collective-permute-done((bf16[512,512]{1,0:T(8,128)(2,1)S(1)}, bf16[512,512]{1,0:T(8,128)(2,1)S(1)}, u32[]{:S(2)}, u32[]{:S(2)}) %collective-permute-start.4) | collective-permute-done | bytes 524320 | tf_op jit(solution)/shard_map/ppermute | solution.py:395
  29.8 2.0 %collective-permute-start.9 = (bf16[512,256]{1,0:T(8,128)(2,1)S(1)}, bf16[512,256]{1,0:T(8,128)(2,1)S(1)}, u32[]{:S(2)}, u32[]{:S(2)}) collective-permute-start(bf16[512,256]{1,0:T(8,128)(2,1)S(1)} %constant_dynamic-slice_fusion.1), channel_id=1, source_target_pairs={{0,2},{1,5},{2,0},{3,7},{4,6},{5,1},{6,4},{7,3},{8,10},{9,13},{10,... | collective-permute-start | bytes 786440 | tf_op jit(solution)/shard_map/ppermute | solution.py:395
  31.8 1.5 collective-permute-start.11
  33.3 5.2 %collective-permute-done.9.refs_3_ = bf16[512,256]{1,0:T(8,128)(2,1)S(1)} collective-permute-done((bf16[512,256]{1,0:T(8,128)(2,1)S(1)}, bf16[512,256]{1,0:T(8,128)(2,1)S(1)}, u32[]{:S(2)}, u32[]{:S(2)}) %collective-permute-start.9) | collective-permute-done | bytes 262176 | tf_op jit(solution)/shard_map/ppermute | solution.py:395
  38.5 1.7 %collective-permute-done.10.refs_4_ = bf16[512,256]{1,0:T(8,128)(2,1)} collective-permute-done((bf16[512,256]{1,0:T(8,128)(2,1)S(1)}, bf16[512,256]{1,0:T(8,128)(2,1)}, u32[]{:S(2)}, u32[]{:S(2)}) %collective-permute-start.10) | collective-permute-done | bytes 262176 | tf_op jit(solution)/shard_map/ppermute | solution.py:389
  40.2 1.6 %copy-done.17 = bf16[4,512,512]{2,1,0:T(8,128)(2,1)S(1)} copy-done((bf16[4,512,512]{2,1,0:T(8,128)(2,1)S(1)}, bf16[4,512,512]{2,1,0:T(8,128)(2,1)}, u32[]{:S(2)}) %copy-start.17) | copy-done | bytes 2097176
  41.8 8.7 %shard_map.346 = (f32[512,512]{1,0:T(8,128)S(1)}, bf16[512,512]{1,0:T(8,128)(2,1)S(1)}, bf16[512,512]{1,0:T(8,128)(2,1)S(1)}, bf16[512,512]{1,0:T(8,128)(2,1)S(1...) custom-call(s32[3]{0:T(128)S(1)} %copy-done.12, ...), custom_call_target="tpu_custom_call" | custom-call | flops 6000000000 | bytes 12582912 | tf_op jit(solution)/shard_map/pallas_call | solution.py:39
  50.5 2.6 %collective-permute-start.13 = (bf16[512,512]{1,0:T(8,128)(2,1)S(1)}, bf16[512,512]{1,0:T(8,128)(2,1)S(1)}, u32[]{:S(2)}, u32[]{:S(2)}) collective-permute-start(bf16[512,512]{1,0:T(8,128)(2,1)S(1)} %constant_dynamic-slice_fusion), channel_id=1, source_target_pairs={{0,2},{1,5},{2,0},{3,7},{4,6},{5,1},{6,4},{7,3},{8,10},{9,13},{10,... | collective-permute-start | bytes 1572872 | tf_op jit(solution)/shard_map/ppermute | solution.py:395
  53.1 7.2 %collective-permute-done.13.refs_3_ = bf16[512,512]{1,0:T(8,128)(2,1)S(1)} collective-permute-done((bf16[512,512]{1,0:T(8,128)(2,1)S(1)}, bf16[512,512]{1,0:T(8,128)(2,1)S(1)}, u32[]{:S(2)}, u32[]{:S(2)}) %collective-permute-start.13) | collective-permute-done | bytes 524320 | tf_op jit(solution)/shard_map/ppermute | solution.py:395
  60.2 1.9 %collective-permute-done.14.refs_4_ = bf16[512,512]{1,0:T(8,128)(2,1)S(1)} collective-permute-done((bf16[512,512]{1,0:T(8,128)(2,1)S(1)}, bf16[512,512]{1,0:T(8,128)(2,1)S(1)}, u32[]{:S(2)}, u32[]{:S(2)}) %collective-permute-start.14) | collective-permute-done | bytes 524320 | tf_op jit(solution)/shard_map/ppermute | solution.py:389
  62.1 6.6 %shard_map.347 = (bf16[2,2,256,512]{3,2,1,0:T(8,128)(2,1)S(1)}, bf16[2,2,256,512]{3,2,1,0:T(8,128)(2,1)S(1)}, bf16[512,2048]{1,0:T(8,128)(2,1)S(1)}, bf16[512,20...) custom-call(s32[3]{0:T(128)S(1)} %copy-done.12, ...), custom_call_target="tpu_custom_call" | custom-call | flops 4000000000 | bytes 12582912 | tf_op jit(solution)/shard_map/pallas_call | solution.py:39
  69.0 2.5 %collective-permute-done.15 = bf16[2,2,256,512]{3,2,0,1:T(8,128)(2,1)S(1)} collective-permute-done((bf16[2,2,256,512]{3,2,0,1:T(8,128)(2,1)S(1)}, bf16[2,2,256,512]{3,2,0,1:T(8,128)(2,1)S(1)}, u32[]{:S(2)}, u32[]{:S(2)}) %collective-permute-start.15) | collective-permute-done | bytes 1048608 | tf_op jit(solution)/shard_map/ppermute | solution.py:389
  71.8 1.5 collective-permute-start.30
  73.3 4.5 %shard_map.348 = (bf16[2,2,256,512]{3,2,1,0:T(8,128)(2,1)S(1)}, bf16[2,2,256,512]{3,2,1,0:T(8,128)(2,1)S(1)}, bf16[512,512]{1,0:T(8,128)(2,1)S(1)}, f32[512,512]{1,0:T(8,128)S(1)}, f32[8,512]{1,0:T(8,128)S(1)}) custom-call(s32[3]{0:T(128)S(1)} %copy-done.12, f32[512,512]{1,0:T(8,128)S(1)} %get-tuple-element.92.h_ref, ...), custom_call_target="tpu_custom_call" | custom-call | flops 4000000000 | bytes 12582912 | tf_op jit(solution)/shard_map/pallas_call | solution.py:39
  77.9 2.1 %collective-permute-start.17 = (bf16[512,512]{1,0:T(8,128)(2,1)S(1)}, bf16[512,512]{1,0:T(8,128)(2,1)S(1)}, u32[]{:S(2)}, u32[]{:S(2)}) collective-permute-start(bf16[512,512]{1,0:T(8,128)(2,1)S(1)} %get-tuple-element.102.refs_0_), channel_id=1, source_target_pairs={{0,2},{1,3},{2,0},{3,1},{4,6},{5,7},{6,4},{7,5},{8,10},{9,11},{10,... | collective-permute-start | bytes 1572872 | tf_op jit(solution)/shard_map/ppermute | solution.py:385
  80.2 9.4 %shard_map.351 = (f32[512,512]{1,0:T(8,128)S(1)}, bf16[512,512]{1,0:T(8,128)(2,1)S(1)}, bf16[2,272,512]{2,1,0:T(8,128)(2,1)S(1)}, bf16[2,272,512]{2,1,0:T(8,128)...) custom-call(s32[3]{0:T(128)S(1)} %copy-done.12, bf16[4,512,512]{2,1,0:T(8,128)(2,1)S(1)} %copy-done.18, ...), custom_call_target="tpu_custom_call" | custom-call | flops 8000000000 | bytes 12582912 | tf_op jit(solution)/shard_map/pallas_call | solution.py:39
  89.6 2.4 %collective-permute-done.17.refs_1_ = bf16[512,512]{1,0:T(8,128)(2,1)S(1)} collective-permute-done((bf16[512,512]{1,0:T(8,128)(2,1)S(1)}, bf16[512,512]{1,0:T(8,128)(2,1)S(1)}, u32[]{:S(2)}, u32[]{:S(2)}) %collective-permute-start.17) | collective-permute-done | bytes 524320 | tf_op jit(solution)/shard_map/ppermute | solution.py:385
  92.5 1.4 collective-permute-done.21
  94.1 0.6 collective-permute-start.22
  94.7 1.7 %collective-permute-start.20 = (bf16[512,512]{1,0:T(8,128)(2,1)S(1)}, bf16[512,512]{1,0:T(8,128)(2,1)S(1)}, u32[]{:S(2)}, u32[]{:S(2)}) collective-permute-start(bf16[512,512]{1,0:T(8,128)(2,1)S(1)} %get-tuple-element.118), channel_id=1, source_target_pairs={{0,2},{1,3},{2,0},{3,1},{4,6},{5,7},{6,4},{7,5},{8,10},{9,11},{10,... | collective-permute-start | bytes 1572872 | tf_op jit(solution)/shard_map/ppermute | solution.py:385
  96.7 0.6 collective-permute-done.30
  97.8 11.3 %collective-permute-done.20.refs_1_ = bf16[512,512]{1,0:T(8,128)(2,1)S(1)} collective-permute-done((bf16[512,512]{1,0:T(8,128)(2,1)S(1)}, bf16[512,512]{1,0:T(8,128)(2,1)S(1)}, u32[]{:S(2)}, u32[]{:S(2)}) %collective-permute-start.20) | collective-permute-done | bytes 524320 | tf_op jit(solution)/shard_map/ppermute | solution.py:385
  109.0 6.5 %collective-permute-start.33 = (bf16[2,2,64,512]{3,2,0,1:T(8,128)(2,1)S(1)}, bf16[2,2,64,512]{3,2,0,1:T(8,128)(2,1)S(1)}, u32[]{:S(2)}, u32[]{:S(2)}) collective-permute-start(bf16[2,2,64,512]{3,2,0,1:T(8,128)(2,1)S(1)} %get-tuple-element.154), channel_id=1, source_target_pairs={{0,24},{4,28},{8,0},{12,4},{16,8},{20,12},{24,16},{28,20},{1,25},{... | collective-permute-start | bytes 786440 | tf_op jit(solution)/shard_map/ppermute | solution.py:381
  115.5 1.2 collective-permute-start.31
  116.7 1.6 %shard_map.349.refs_0_ = bf16[4,512,512]{2,1,0:T(8,128)(2,1)} custom-call(s32[3]{0:T(128)S(1)} %copy-done.12, bf16[512,512]{1,0:T(8,128)(2,1)S(1)} %get-tuple-element.102.refs_0_, bf16[512,512]{1,0:T(8,128)(2,1)S(1)} %collective-permute-done.16.refs_1_), custom_call_target="tpu_custom_call" | custom-call | bytes 4194304 | tf_op jit(solution)/shard_map/pallas_call | solution.py:441
  118.3 1.6 %shard_map.350 = bf16[4,512,512]{2,1,0:T(8,128)(2,1)} custom-call(s32[3]{0:T(128)S(1)} %copy-done.12, bf16[4,512,512]{2,1,0:T(8,128)(2,1)} %shard_map.349.refs_0_, bf16[512,512]{1,0:T(8,128)(2,1)S(1)} %collective-permute-done.17.refs_1_, bf16[512,512]{1,0:T(8,128)(2,1)S(1)} %collective-permute-done.18.refs_2_), custom_call_target="tpu_custom_call", output_to_operand_aliasing={{}: (1, {})} | custom-call | bytes 4194304 | tf_op jit(solution)/shard_map/pallas_call | solution.py:441
  119.9 2.0 %shard_map.352.refs_0_ = f32[4,512,512]{2,1,0:T(8,128)} custom-call(s32[3]{0:T(128)S(1)} %copy-done.12, f32[512,512]{1,0:T(8,128)S(1)} %get-tuple-element.117.refs_0_, bf16[512,512]{1,0:T(8,128)(2,1)S(1)} %collective-permute-done.19.refs_1_), custom_call_target="tpu_custom_call" | custom-call | bytes 4194304 | tf_op jit(solution)/shard_map/pallas_call | solution.py:441
  122.1 1.8 %collective-permute-start.25 = (bf16[272,512]{1,0:T(8,128)(2,1)S(1)}, bf16[272,512]{1,0:T(8,128)(2,1)S(1)}, u32[]{:S(2)}, u32[]{:S(2)}) collective-permute-start(bf16[272,512]{1,0:T(8,128)(2,1)S(1)} %fusion.2), channel_id=1, source_target_pairs={{0,2},{1,3},{2,0},{3,1},{4,6},{5,7},{6,4},{7,5},{8,10},{9,11},{10,... | collective-permute-start | bytes 835592 | tf_op jit(solution)/shard_map/ppermute | solution.py:385
  123.9 13.9 %collective-permute-done.32 = bf16[2,2,64,512]{3,2,0,1:T(8,128)(2,1)S(1)} collective-permute-done((bf16[2,2,64,512]{3,2,0,1:T(8,128)(2,1)S(1)}, bf16[2,2,64,512]{3,2,0,1:T(8,128)(2,1)S(1)}, u32[]{:S(2)}, u32[]{:S(2)}) %collective-permute-start.32) | collective-permute-done | bytes 262176 | tf_op jit(solution)/shard_map/ppermute | solution.py:381
  137.8 1.8 %collective-permute-start.34 = (bf16[2,64,512]{2,1,0:T(8,128)(2,1)S(1)}, bf16[2,64,512]{2,1,0:T(8,128)(2,1)S(1)}, u32[]{:S(2)}, u32[]{:S(2)}) collective-permute-start(bf16[2,64,512]{2,1,0:T(8,128)(2,1)S(1)} %fusion.3), channel_id=1, source_target_pairs={{0,2},{1,3},{2,0},{3,1},{4,6},{5,7},{6,4},{7,5},{8,10},{9,11},{10,... | collective-permute-start | bytes 393224 | tf_op jit(solution)/shard_map/ppermute | solution.py:385
  139.9 3.0 %collective-permute-start.27 = (bf16[80,512]{1,0:T(8,128)(2,1)S(1)}, bf16[80,512]{1,0:T(8,128)(2,1)S(1)}, u32[]{:S(2)}, u32[]{:S(2)}) collective-permute-start(bf16[80,512]{1,0:T(8,128)(2,1)S(1)} %get-tuple-element.165), channel_id=1, source_target_pairs={{0,16},{4,20},{8,24},{12,28},{16,0},{20,4},{24,8},{28,12},{1,17},{... | collective-permute-start | bytes 245768 | tf_op jit(solution)/shard_map/ppermute | solution.py:381
  142.9 3.8 %collective-permute-start.28 = (bf16[80,512]{1,0:T(8,128)(2,1)S(1)}, bf16[80,512]{1,0:T(8,128)(2,1)S(1)}, u32[]{:S(2)}, u32[]{:S(2)}) collective-permute-start(bf16[80,512]{1,0:T(8,128)(2,1)S(1)} %concatenate.42), channel_id=1, source_target_pairs={{0,24},{4,28},{8,0},{12,4},{16,8},{20,12},{24,16},{28,20},{1,25},{... | collective-permute-start | bytes 245768 | tf_op jit(solution)/shard_map/ppermute | solution.py:381
  146.8 1.7 %shard_map.354 = (f32[64,512]{1,0:T(8,128)}, f32[64,512]{1,0:T(8,128)}, f32[64,512]{1,0:T(8,128)}, bf16[64,512]{1,0:T(8,128)(2,1)}, f32[64,512]{1,0:T(8,128)}, /...) custom-call(s32[3]{0:T(128)S(1)} %copy-done.12, bf16[2,64,512]{2,1,0:T(8,128)(2,1)S(1)} %get-tuple-element.171.refs_0_, ...), custom_call_target="tpu_custom_call" | custom-call | bytes 3145728 | tf_op jit(solution)/shard_map/pallas_call | solution.py:39
  148.6 2.0 %shard_map.353 = f32[4,512,512]{2,1,0:T(8,128)} custom-call(s32[3]{0:T(128)S(1)} %copy-done.12, f32[4,512,512]{2,1,0:T(8,128)} %shard_map.352.refs_0_, bf16[512,512]{1,0:T(8,128)(2,1)S(1)} %collective-permute-done.20.refs_1_, bf16[512,512]{1,0:T(8,128)(2,1)S(1)} %collective-permute-done.23.refs_2_), custom_call_target="tpu_custom_call", output_to_operand_aliasing={{}: (1, {})} | custom-call | bytes 4194304 | tf_op jit(solution)/shard_map/pallas_call | solution.py:441
  150.7 1.5 shard_map.355
  (104 shorter events, 4.0 us)
Async XLA Ops:
  3.9 11.3 %collective-permute-start.1 = (bf16[64,512]{1,0:T(8,128)(2,1)}, bf16[64,512]{1,0:T(8,128)(2,1)S(1)}, u32[]{:S(2)}, u32[]{:S(2)}) collective-permute-start(bf16[64,512]{1,0:T(8,128)(2,1)} %get-tuple-element.88), channel_id=1, source_target_pairs={{0,16},{4,20},{8,24},{12,28},{16,0},{20,4},{24,8},{28,12},{1,17},{... | collective-permute-start | bytes 196616 | tf_op jit(solution)/shard_map/ppermute | solution.py:381
  8.0 14.5 %collective-permute-start.6 = (bf16[64,1024]{1,0:T(8,128)(2,1)}, bf16[64,1024]{1,0:T(8,128)(2,1)S(1)}, u32[]{:S(2)}, u32[]{:S(2)}) collective-permute-start(bf16[64,1024]{1,0:T(8,128)(2,1)} %get-tuple-element.90), channel_id=1, source_target_pairs={{0,16},{4,20},{8,24},{12,28},{16,0},{20,4},{24,8},{28,12},{1,17},{... | collective-permute-start | bytes 393224 | tf_op jit(solution)/shard_map/ppermute | solution.py:381
  8.0 1.8 %collective-permute-start = (bf16[64,1536]{1,0:T(8,128)(2,1)}, bf16[64,1536]{1,0:T(8,128)(2,1)S(1)}, u32[]{:S(2)}, u32[]{:S(2)}) collective-permute-start(bf16[64,1536]{1,0:T(8,128)(2,1)} %get-tuple-element.89), channel_id=1, source_target_pairs={{0,1},{1,0},{2,3},{3,2},{4,5},{5,4},{6,7},{7,6},{8,9},{9,8},{10,11... | collective-permute-start | bytes 589832 | tf_op jit(solution)/shard_map/ppermute | solution.py:389
  10.7 8.3 %collective-permute-start.2 = (bf16[128,512]{1,0:T(8,128)(2,1)S(1)}, bf16[128,512]{1,0:T(8,128)(2,1)S(1)}, u32[]{:S(2)}, u32[]{:S(2)}) collective-permute-start(bf16[128,512]{1,0:T(8,128)(2,1)S(1)} %pad_maximum_fusion.3), channel_id=1, source_target_pairs={{0,8},{1,25},{2,10},{3,27},{4,12},{5,29},{6,14},{7,31},{8,16},{9,1... | collective-permute-start | bytes 393224 | tf_op jit(solution)/shard_map/ppermute | solution.py:395
  13.5 26.6 %copy-start.12 = (s32[3]{0:T(128)S(1)}, s32[3]{0:T(128)}, u32[]{:S(2)}) copy-start(s32[3]{0:T(128)} %pad_add_fusion.place_ref) | copy-start | bytes 40
  13.5 26.6 %copy-start.19 = (s32[4,512]{1,0:T(4,128)S(1)}, s32[4,512]{1,0:T(4,128)}, u32[]{:S(2)}) copy-start(s32[4,512]{1,0:T(4,128)} %seg_ref.1) | copy-start | bytes 24580
  13.6 11.0 %collective-permute-start.7 = (bf16[128,1024]{1,0:T(8,128)(2,1)S(1)}, bf16[128,1024]{1,0:T(8,128)(2,1)S(1)}, u32[]{:S(2)}, u32[]{:S(2)}) collective-permute-start(bf16[128,1024]{1,0:T(8,128)(2,1)S(1)} %pad_maximum_fusion.1), channel_id=1, source_target_pairs={{0,8},{1,25},{2,10},{3,27},{4,12},{5,29},{6,14},{7,31},{8,16},{9,1... | collective-permute-start | bytes 786440 | tf_op jit(solution)/shard_map/ppermute | solution.py:395
  19.0 1.5 collective-permute-start.3
  20.5 9.2 %collective-permute-start.4 = (bf16[512,512]{1,0:T(8,128)(2,1)S(1)}, bf16[512,512]{1,0:T(8,128)(2,1)S(1)}, u32[]{:S(2)}, u32[]{:S(2)}) collective-permute-start(bf16[512,512]{1,0:T(8,128)(2,1)S(1)} %constant_dynamic-update-slice_fusion.refs_0_), channel_id=1, source_target_pairs={{0,4},{1,3},{2,6},{3,1},{4,0},{5,7},{6,2},{7,5},{8,12},{9,11},{10,... | collective-permute-start | bytes 1572872 | tf_op jit(solution)/shard_map/ppermute | solution.py:395
  24.6 1.8 %collective-permute-start.8 = (bf16[192,1024]{1,0:T(8,128)(2,1)S(1)}, bf16[192,1024]{1,0:T(8,128)(2,1)S(1)}, u32[]{:S(2)}, u32[]{:S(2)}) collective-permute-start(bf16[192,1024]{1,0:T(8,128)(2,1)S(1)} %pad_maximum_fusion), channel_id=1, source_target_pairs={{0,1},{1,0},{2,3},{3,2},{4,5},{5,4},{6,7},{7,6},{8,9},{9,8},{10,11... | collective-permute-start | bytes 1179656 | tf_op jit(solution)/shard_map/ppermute | solution.py:389
  29.8 8.7 %collective-permute-start.9 = (bf16[512,256]{1,0:T(8,128)(2,1)S(1)}, bf16[512,256]{1,0:T(8,128)(2,1)S(1)}, u32[]{:S(2)}, u32[]{:S(2)}) collective-permute-start(bf16[512,256]{1,0:T(8,128)(2,1)S(1)} %constant_dynamic-slice_fusion.1), channel_id=1, source_target_pairs={{0,2},{1,5},{2,0},{3,7},{4,6},{5,1},{6,4},{7,3},{8,10},{9,13},{10,... | collective-permute-start | bytes 786440 | tf_op jit(solution)/shard_map/ppermute | solution.py:395
  31.8 6.7 %collective-permute-start.5 = (bf16[512,512]{1,0:T(8,128)(2,1)S(1)}, bf16[512,512]{1,0:T(8,128)(2,1)}, u32[]{:S(2)}, u32[]{:S(2)}) collective-permute-start(bf16[512,512]{1,0:T(8,128)(2,1)S(1)} %collective-permute-done.4.refs_1_), channel_id=1, source_target_pairs={{0,1},{1,0},{2,3},{3,2},{4,5},{5,4},{6,7},{7,6},{8,9},{9,8},{10,11... | collective-permute-start | bytes 1572872 | tf_op jit(solution)/shard_map/ppermute | solution.py:389
  31.8 18.6 %collective-permute-start.11 = (bf16[512,1024]{1,0:T(8,128)(2,1)S(1)}, bf16[512,1024]{1,0:T(8,128)(2,1)S(1)}, u32[]{:S(2)}, u32[]{:S(2)}) collective-permute-start(bf16[512,1024]{1,0:T(8,128)(2,1)S(1)} %constant_dynamic-update-slice_fusion.5.refs_0_), channel_id=1, source_target_pairs={{0,4},{1,3},{2,6},{3,1},{4,0},{5,7},{6,2},{7,5},{8,12},{9,11},{10,... | collective-permute-start | bytes 3145736 | tf_op jit(solution)/shard_map/ppermute | solution.py:395
  38.5 1.7 %collective-permute-start.10 = (bf16[512,256]{1,0:T(8,128)(2,1)S(1)}, bf16[512,256]{1,0:T(8,128)(2,1)}, u32[]{:S(2)}, u32[]{:S(2)}) collective-permute-start(bf16[512,256]{1,0:T(8,128)(2,1)S(1)} %collective-permute-done.9.refs_3_), channel_id=1, source_target_pairs={{0,1},{1,0},{2,3},{3,2},{4,5},{5,4},{6,7},{7,6},{8,9},{9,8},{10,11... | collective-permute-start | bytes 786440 | tf_op jit(solution)/shard_map/ppermute | solution.py:389
  38.5 23.6 %copy-start.16 = (bf16[4,512,512]{2,1,0:T(8,128)(2,1)S(1)}, bf16[4,512,512]{2,1,0:T(8,128)(2,1)}, u32[]{:S(2)}) copy-start(bf16[4,512,512]{2,1,0:T(8,128)(2,1)} %c_any.3) | copy-start | bytes 6291460
  50.5 9.7 %collective-permute-start.13 = (bf16[512,512]{1,0:T(8,128)(2,1)S(1)}, bf16[512,512]{1,0:T(8,128)(2,1)S(1)}, u32[]{:S(2)}, u32[]{:S(2)}) collective-permute-start(bf16[512,512]{1,0:T(8,128)(2,1)S(1)} %constant_dynamic-slice_fusion), channel_id=1, source_target_pairs={{0,2},{1,5},{2,0},{3,7},{4,6},{5,1},{6,4},{7,3},{8,10},{9,13},{10,... | collective-permute-start | bytes 1572872 | tf_op jit(solution)/shard_map/ppermute | solution.py:395
  53.1 7.2 %collective-permute-start.12 = (bf16[512,1024]{1,0:T(8,128)(2,1)S(1)}, bf16[512,1024]{1,0:T(8,128)(2,1)S(1)}, u32[]{:S(2)}, u32[]{:S(2)}) collective-permute-start(bf16[512,1024]{1,0:T(8,128)(2,1)S(1)} %collective-permute-done.11.refs_1_), channel_id=1, source_target_pairs={{0,1},{1,0},{2,3},{3,2},{4,5},{5,4},{6,7},{7,6},{8,9},{9,8},{10,11... | collective-permute-start | bytes 3145736 | tf_op jit(solution)/shard_map/ppermute | solution.py:389
  60.2 1.9 %collective-permute-start.14 = (bf16[512,512]{1,0:T(8,128)(2,1)S(1)}, bf16[512,512]{1,0:T(8,128)(2,1)S(1)}, u32[]{:S(2)}, u32[]{:S(2)}) collective-permute-start(bf16[512,512]{1,0:T(8,128)(2,1)S(1)} %collective-permute-done.13.refs_3_), channel_id=1, source_target_pairs={{0,1},{1,0},{2,3},{3,2},{4,5},{5,4},{6,7},{7,6},{8,9},{9,8},{10,11... | collective-permute-start | bytes 1572872 | tf_op jit(solution)/shard_map/ppermute | solution.py:389
  68.8 2.7 %collective-permute-start.15 = (bf16[2,2,256,512]{3,2,0,1:T(8,128)(2,1)S(1)}, bf16[2,2,256,512]{3,2,0,1:T(8,128)(2,1)S(1)}, u32[]{:S(2)}, u32[]{:S(2)}) collective-permute-start(bf16[2,2,256,512]{3,2,0,1:T(8,128)(2,1)S(1)} %copy.43), channel_id=1, source_target_pairs={{0,1},{1,0},{2,3},{3,2},{4,5},{5,4},{6,7},{7,6},{8,9},{9,8},{10,11... | collective-permute-start | bytes 3145736 | tf_op jit(solution)/shard_map/ppermute | solution.py:389
  71.8 25.4 %collective-permute-start.30 = (bf16[2,2,256,512]{3,2,0,1:T(8,128)(2,1)S(1)}, bf16[2,2,256,512]{3,2,0,1:T(8,128)(2,1)S(1)}, u32[]{:S(2)}, u32[]{:S(2)}) collective-permute-start(bf16[2,2,256,512]{3,2,0,1:T(8,128)(2,1)S(1)} %add_convert_fusion), channel_id=1, source_target_pairs={{0,4},{4,0},{8,12},{12,8},{16,20},{20,16},{24,28},{28,24},{1,5},{5... | collective-permute-start | bytes 3145736 | tf_op jit(solution)/shard_map/ppermute | solution.py:376
  77.9 2.3 %copy-start.18 = (bf16[4,512,512]{2,1,0:T(8,128)(2,1)S(1)}, bf16[4,512,512]{2,1,0:T(8,128)(2,1)}, u32[]{:S(2)}) copy-start(bf16[4,512,512]{2,1,0:T(8,128)(2,1)} %x_any.3) | copy-start | bytes 6291460
  77.9 14.0 %collective-permute-start.17 = (bf16[512,512]{1,0:T(8,128)(2,1)S(1)}, bf16[512,512]{1,0:T(8,128)(2,1)S(1)}, u32[]{:S(2)}, u32[]{:S(2)}) collective-permute-start(bf16[512,512]{1,0:T(8,128)(2,1)S(1)} %get-tuple-element.102.refs_0_), channel_id=1, source_target_pairs={{0,2},{1,3},{2,0},{3,1},{4,6},{5,7},{6,4},{7,5},{8,10},{9,11},{10,... | collective-permute-start | bytes 1572872 | tf_op jit(solution)/shard_map/ppermute | solution.py:385
  80.1 16.4 %collective-permute-start.29 = (bf16[2,2,256,512]{3,2,0,1:T(8,128)(2,1)S(1)}, bf16[2,2,256,512]{3,2,0,1:T(8,128)(2,1)S(1)}, u32[]{:S(2)}, u32[]{:S(2)}) collective-permute-start(bf16[2,2,256,512]{3,2,0,1:T(8,128)(2,1)S(1)} %copy.45), channel_id=1, source_target_pairs={{0,1},{1,0},{2,3},{3,2},{4,5},{5,4},{6,7},{7,6},{8,9},{9,8},{10,11... | collective-permute-start | bytes 3145736 | tf_op jit(solution)/shard_map/ppermute | solution.py:389
  92.0 2.0 %collective-permute-start.21 = (bf16[2,272,512]{2,1,0:T(8,128)(2,1)S(1)}, bf16[2,272,512]{2,1,0:T(8,128)(2,1)S(1)}, u32[]{:S(2)}, u32[]{:S(2)}) collective-permute-start(bf16[2,272,512]{2,1,0:T(8,128)(2,1)S(1)} %get-tuple-element.120), channel_id=1, source_target_pairs={{0,1},{1,0},{2,3},{3,2},{4,5},{5,4},{6,7},{7,6},{8,9},{9,8},{10,11... | collective-permute-start | bytes 1671176 | tf_op jit(solution)/shard_map/ppermute | solution.py:389
  92.0 2.8 %collective-permute-start.16 = (bf16[512,512]{1,0:T(8,128)(2,1)S(1)}, bf16[512,512]{1,0:T(8,128)(2,1)S(1)}, u32[]{:S(2)}, u32[]{:S(2)}) collective-permute-start(bf16[512,512]{1,0:T(8,128)(2,1)S(1)} %get-tuple-element.102.refs_0_), channel_id=1, source_target_pairs={{0,1},{1,0},{2,3},{3,2},{4,5},{5,4},{6,7},{7,6},{8,9},{9,8},{10,11... | collective-permute-start | bytes 1572872 | tf_op jit(solution)/shard_map/ppermute | solution.py:389
  94.1 27.8 %collective-permute-start.22 = (bf16[2,272,512]{2,1,0:T(8,128)(2,1)S(1)}, bf16[2,272,512]{2,1,0:T(8,128)(2,1)S(1)}, u32[]{:S(2)}, u32[]{:S(2)}) collective-permute-start(bf16[2,272,512]{2,1,0:T(8,128)(2,1)S(1)} %add_convert_fusion.1), channel_id=1, source_target_pairs={{0,4},{4,0},{8,12},{12,8},{16,20},{20,16},{24,28},{28,24},{1,5},{5... | collective-permute-start | bytes 1671176 | tf_op jit(solution)/shard_map/ppermute | solution.py:376
  94.7 27.1 %collective-permute-start.24 = (bf16[2,272,512]{2,1,0:T(8,128)(2,1)S(1)}, bf16[2,272,512]{2,1,0:T(8,128)(2,1)S(1)}, u32[]{:S(2)}, u32[]{:S(2)}) collective-permute-start(bf16[2,272,512]{2,1,0:T(8,128)(2,1)S(1)} %get-tuple-element.123), channel_id=1, source_target_pairs={{0,1},{1,0},{2,3},{3,2},{4,5},{5,4},{6,7},{7,6},{8,9},{9,8},{10,11... | collective-permute-start | bytes 1671176 | tf_op jit(solution)/shard_map/ppermute | solution.py:389
  94.7 14.3 %collective-permute-start.20 = (bf16[512,512]{1,0:T(8,128)(2,1)S(1)}, bf16[512,512]{1,0:T(8,128)(2,1)S(1)}, u32[]{:S(2)}, u32[]{:S(2)}) collective-permute-start(bf16[512,512]{1,0:T(8,128)(2,1)S(1)} %get-tuple-element.118), channel_id=1, source_target_pairs={{0,2},{1,3},{2,0},{3,1},{4,6},{5,7},{6,4},{7,5},{8,10},{9,11},{10,... | collective-permute-start | bytes 1572872 | tf_op jit(solution)/shard_map/ppermute | solution.py:385
  96.4 19.1 %collective-permute-start.19 = (bf16[512,512]{1,0:T(8,128)(2,1)S(1)}, bf16[512,512]{1,0:T(8,128)(2,1)S(1)}, u32[]{:S(2)}, u32[]{:S(2)}) collective-permute-start(bf16[512,512]{1,0:T(8,128)(2,1)S(1)} %get-tuple-element.118), channel_id=1, source_target_pairs={{0,1},{1,0},{2,3},{3,2},{4,5},{5,4},{6,7},{7,6},{8,9},{9,8},{10,11... | collective-permute-start | bytes 1572872 | tf_op jit(solution)/shard_map/ppermute | solution.py:389
  97.3 18.2 %collective-permute-start.18 = (bf16[512,512]{1,0:T(8,128)(2,1)S(1)}, bf16[512,512]{1,0:T(8,128)(2,1)S(1)}, u32[]{:S(2)}, u32[]{:S(2)}) collective-permute-start(bf16[512,512]{1,0:T(8,128)(2,1)S(1)} %collective-permute-done.17.refs_1_), channel_id=1, source_target_pairs={{0,1},{1,0},{2,3},{3,2},{4,5},{5,4},{6,7},{7,6},{8,9},{9,8},{10,11... | collective-permute-start | bytes 1572872 | tf_op jit(solution)/shard_map/ppermute | solution.py:389
  109.0 14.8 %collective-permute-start.33 = (bf16[2,2,64,512]{3,2,0,1:T(8,128)(2,1)S(1)}, bf16[2,2,64,512]{3,2,0,1:T(8,128)(2,1)S(1)}, u32[]{:S(2)}, u32[]{:S(2)}) collective-permute-start(bf16[2,2,64,512]{3,2,0,1:T(8,128)(2,1)S(1)} %get-tuple-element.154), channel_id=1, source_target_pairs={{0,24},{4,28},{8,0},{12,4},{16,8},{20,12},{24,16},{28,20},{1,25},{... | collective-permute-start | bytes 786440 | tf_op jit(solution)/shard_map/ppermute | solution.py:381
  115.5 22.2 %collective-permute-start.32 = (bf16[2,2,64,512]{3,2,0,1:T(8,128)(2,1)S(1)}, bf16[2,2,64,512]{3,2,0,1:T(8,128)(2,1)S(1)}, u32[]{:S(2)}, u32[]{:S(2)}) collective-permute-start(bf16[2,2,64,512]{3,2,0,1:T(8,128)(2,1)S(1)} %get-tuple-element.155), channel_id=1, source_target_pairs={{0,16},{4,20},{8,24},{12,28},{16,0},{20,4},{24,8},{28,12},{1,17},{... | collective-permute-start | bytes 786440 | tf_op jit(solution)/shard_map/ppermute | solution.py:381
  115.5 22.2 %collective-permute-start.31 = (bf16[2,2,64,512]{3,2,0,1:T(8,128)(2,1)S(1)}, bf16[2,2,64,512]{3,2,0,1:T(8,128)(2,1)S(1)}, u32[]{:S(2)}, u32[]{:S(2)}) collective-permute-start(bf16[2,2,64,512]{3,2,0,1:T(8,128)(2,1)S(1)} %get-tuple-element.156), channel_id=1, source_target_pairs={{0,8},{4,12},{8,16},{12,20},{16,24},{20,28},{24,0},{28,4},{1,9},{5... | collective-permute-start | bytes 786440 | tf_op jit(solution)/shard_map/ppermute | solution.py:381
  121.8 26.8 %collective-permute-start.23 = (bf16[512,512]{1,0:T(8,128)(2,1)S(1)}, bf16[512,512]{1,0:T(8,128)(2,1)S(1)}, u32[]{:S(2)}, u32[]{:S(2)}) collective-permute-start(bf16[512,512]{1,0:T(8,128)(2,1)S(1)} %collective-permute-done.20.refs_1_), channel_id=1, source_target_pairs={{0,1},{1,0},{2,3},{3,2},{4,5},{5,4},{6,7},{7,6},{8,9},{9,8},{10,11... | collective-permute-start | bytes 1572872 | tf_op jit(solution)/shard_map/ppermute | solution.py:389
  122.0 24.8 %copy-start = (f32[64,512]{1,0:T(8,128)S(1)}, f32[64,512]{1,0:T(8,128)}, u32[]{:S(2)}) copy-start(f32[64,512]{1,0:T(8,128)} %refs_6_.2) | copy-start | bytes 393220
  122.0 24.8 %copy-start.1 = (f32[512,64]{0,1:T(8,128)S(1)}, f32[512,64]{0,1:T(8,128)}, u32[]{:S(2)}) copy-start(f32[512,64]{0,1:T(8,128)} %param.30) | copy-start | bytes 393220
  122.0 24.8 %copy-start.3 = (f32[64,512]{1,0:T(8,128)S(1)}, f32[64,512]{1,0:T(8,128)}, u32[]{:S(2)}) copy-start(f32[64,512]{1,0:T(8,128)} %refs_7_.2) | copy-start | bytes 393220
  122.0 24.8 %copy-start.4 = (f32[64,512]{1,0:T(8,128)S(1)}, f32[64,512]{1,0:T(8,128)}, u32[]{:S(2)}) copy-start(f32[64,512]{1,0:T(8,128)} %refs_8_.2) | copy-start | bytes 393220
  122.0 24.8 %copy-start.5 = (f32[512,64]{0,1:T(8,128)S(1)}, f32[512,64]{0,1:T(8,128)}, u32[]{:S(2)}) copy-start(f32[512,64]{0,1:T(8,128)} %param.31) | copy-start | bytes 393220
  122.0 24.8 %copy-start.6 = (f32[512,64]{0,1:T(8,128)S(1)}, f32[512,64]{0,1:T(8,128)}, u32[]{:S(2)}) copy-start(f32[512,64]{0,1:T(8,128)} %param.32) | copy-start | bytes 393220
  122.0 24.8 %copy-start.13 = (f32[2,64]{1,0:T(2,128)S(1)}, f32[2,64]{1,0:T(2,128)}, u32[]{:S(2)}) copy-start(f32[2,64]{1,0:T(2,128)} %refs_4_.1) | copy-start | bytes 1540
  122.1 17.6 %collective-permute-start.25 = (bf16[272,512]{1,0:T(8,128)(2,1)S(1)}, bf16[272,512]{1,0:T(8,128)(2,1)S(1)}, u32[]{:S(2)}, u32[]{:S(2)}) collective-permute-start(bf16[272,512]{1,0:T(8,128)(2,1)S(1)} %fusion.2), channel_id=1, source_target_pairs={{0,2},{1,3},{2,0},{3,1},{4,6},{5,7},{6,4},{7,5},{8,10},{9,11},{10,... | collective-permute-start | bytes 835592 | tf_op jit(solution)/shard_map/ppermute | solution.py:385
  137.8 8.9 %collective-permute-start.34 = (bf16[2,64,512]{2,1,0:T(8,128)(2,1)S(1)}, bf16[2,64,512]{2,1,0:T(8,128)(2,1)S(1)}, u32[]{:S(2)}, u32[]{:S(2)}) collective-permute-start(bf16[2,64,512]{2,1,0:T(8,128)(2,1)S(1)} %fusion.3), channel_id=1, source_target_pairs={{0,2},{1,3},{2,0},{3,1},{4,6},{5,7},{6,4},{7,5},{8,10},{9,11},{10,... | collective-permute-start | bytes 393224 | tf_op jit(solution)/shard_map/ppermute | solution.py:385
  139.9 10.7 %collective-permute-start.27 = (bf16[80,512]{1,0:T(8,128)(2,1)S(1)}, bf16[80,512]{1,0:T(8,128)(2,1)S(1)}, u32[]{:S(2)}, u32[]{:S(2)}) collective-permute-start(bf16[80,512]{1,0:T(8,128)(2,1)S(1)} %get-tuple-element.165), channel_id=1, source_target_pairs={{0,16},{4,20},{8,24},{12,28},{16,0},{20,4},{24,8},{28,12},{1,17},{... | collective-permute-start | bytes 245768 | tf_op jit(solution)/shard_map/ppermute | solution.py:381
  142.9 7.7 %collective-permute-start.26 = (bf16[80,512]{1,0:T(8,128)(2,1)S(1)}, bf16[80,512]{1,0:T(8,128)(2,1)S(1)}, u32[]{:S(2)}, u32[]{:S(2)}) collective-permute-start(bf16[80,512]{1,0:T(8,128)(2,1)S(1)} %get-tuple-element.166), channel_id=1, source_target_pairs={{0,8},{4,12},{8,16},{12,20},{16,24},{20,28},{24,0},{28,4},{1,9},{5... | collective-permute-start | bytes 245768 | tf_op jit(solution)/shard_map/ppermute | solution.py:381
  142.9 7.7 %collective-permute-start.28 = (bf16[80,512]{1,0:T(8,128)(2,1)S(1)}, bf16[80,512]{1,0:T(8,128)(2,1)S(1)}, u32[]{:S(2)}, u32[]{:S(2)}) collective-permute-start(bf16[80,512]{1,0:T(8,128)(2,1)S(1)} %concatenate.42), channel_id=1, source_target_pairs={{0,24},{4,28},{8,0},{12,4},{16,8},{20,12},{24,16},{28,20},{1,25},{... | collective-permute-start | bytes 245768 | tf_op jit(solution)/shard_map/ppermute | solution.py:381
  148.6 2.1 %copy-start.9 = (f32[3,64,128]{2,1,0:T(8,128)S(1)}, f32[3,64,128]{2,1,0:T(8,128)}, u32[]{:S(2)}) copy-start(f32[3,64,128]{2,1,0:T(8,128)} %refs_9_.1) | copy-start | bytes 294916
  148.6 2.1 %copy-start.10 = (f32[128,64]{0,1:T(8,128)S(1)}, f32[128,64]{0,1:T(8,128)}, u32[]{:S(2)}) copy-start(f32[128,64]{0,1:T(8,128)} %param.25) | copy-start | bytes 98308
  (7 other events, 14.0 us)

commit v2 on v1

--- a/solution.py
+++ b/solution.py
@@ -33,22 +33,18 @@
     return lax.rsqrt(jnp.mean(values * values, axis=-1, keepdims=True) + EPS)
 
 
-def call(body, outs, ins, where, scratch=(), outside=(), limit=24, flops=0, moved=0, trans=0):
+def call(body, outs, ins, where, scratch=(), outside=(), out_there=(), limit=24, flops=0, moved=0, trans=0):
     vmem = pl.BlockSpec(memory_space=pltpu.VMEM)
     specs = [pl.BlockSpec(memory_space=pltpu.HBM) if k in outside else vmem for k in range(len(ins))]
     return pl.pallas_call(
         body,
         out_shape=outs,
         in_specs=[pl.BlockSpec(memory_space=pltpu.SMEM)] + specs,
-        out_specs=[vmem] * len(outs),
+        out_specs=[pl.BlockSpec(memory_space=pltpu.HBM) if k in out_there else vmem for k in range(len(outs))],
         scratch_shapes=list(scratch),
         compiler_params=pltpu.CompilerParams(vmem_limit_bytes=limit * 1024 * 1024),
         cost_estimate=pl.CostEstimate(flops=flops, bytes_accessed=moved, transcendentals=trans),
     )(where, *ins)
-
-
-def row_copy(array, row, target, sem):
-    return pltpu.make_async_copy(array.at[row], target, sem)
 
 
 def order_of_blocks(count):
@@ -85,17 +81,14 @@
         target[k * rows : (k + 1) * rows, :] = source[pl.ds(at, rows), :]
 
 
-def attention_kernel(count, rows, place_ref, x_any, seg_ref, *refs):
-    h_ref, q_ref, k_ref, v_ref, o_ref, p_ref, w_ref, x_row, flat, o_flat, sem = refs[5:]
+def attention_kernel(count, rows, place_ref, x_row, seg_ref, *refs):
+    h_ref, q_ref, k_ref, v_ref, o_ref, p_ref, w_ref, flat, o_flat = refs[5:]
     z, x = place_ref[0], place_ref[1]
-    copy = row_copy(x_any, place_ref[2], x_row, sem)
-    copy.start()
 
     def store(group, at, c, block):
         w_ref[pl.ds(at, rows), pl.ds(pl.multiple_of(c * 4 + group * 128, 128), 128)] = block
 
     place(refs[:5], lax.rem(place_ref[2], 2), z, x, count, rows, store)
-    copy.wait()
     states = x_row[...].astype(F32)
     unit = (states * root_scale(states)).astype(BF)
     v = nn(unit, w_ref[:, 1024:1536]).astype(BF)
@@ -128,14 +121,12 @@
     h_ref[...] = states + nt(o, w_ref[:, 1536:2048])
 
 
-def feed_kernel(count, rows, place_ref, h_ref, c_any, *refs):
-    far_own, far_sib, g_ref, dz_ref, w_ref, u_near, c_near = refs[5:12]
-    c_row, u_flat, c_flat, u_far, c_far, sem = refs[12:]
+def feed_kernel(count, rows, place_ref, h_ref, c_row, *refs):
+    far_refs, (g_ref, dz_ref, w_ref, u_near, c_near, row_ref) = refs[5:9], refs[9:15]
+    u_flat, c_flat, u_far, c_far = refs[15:]
     z, x = place_ref[0], place_ref[1]
     width = w_ref.shape[1] // 2
     cols = width // 4
-    copy = row_copy(c_any, place_ref[2], c_row, sem)
-    copy.start()
 
     def store(group, at, c, block):
         to = c // cols * width + group * cols + c % cols if isinstance(c, int) else None
@@ -147,7 +138,6 @@
     h = h_ref[...]
     low = (h * root_scale(h)).astype(BF)
     u_flat[...] = low.T
-    copy.wait()
     back = c_row[...]
     c_flat[...] = back.T
     for source, near, far in ((u_flat, u_near, u_far), (c_flat, c_near, c_far)):
@@ -162,19 +152,16 @@
         g_ref[:, at] = (inner * half).astype(BF)
         slope = half + (inner * half) * (1.0 - bent) * (GELU + 3.0 * GELU * CUBIC * square)
         dz_ref[:, at] = (nn(back, w_ref[:, width + m * cols : width + (m + 1) * cols]) * slope).astype(BF)
-        target = (far_own, far_sib)[m % 2]
-        target[0, m // 2] = nn(u_far[...], dz_ref[:, at]).astype(BF)
-        target[1, m // 2] = nn(c_far[...], g_ref[:, at]).astype(BF)
-
-
-def feed_rest_kernel(place_ref, h_ref, g_ref, dz_ref, w_ref, u_near, c_near, c_any, *refs):
-    near_own, near_sib, row_ref, dh_ref, gain_ref, c_row, sem = refs
+        far_refs[m % 2][m // 2] = nn(u_far[...], dz_ref[:, at]).astype(BF)
+        far_refs[2 + m % 2][m // 2] = nn(c_far[...], g_ref[:, at]).astype(BF)
+    row_ref[...] = (h + nt(g_ref[...], w_ref[:, width:])).astype(BF)
+
+
+def feed_rest_kernel(place_ref, h_ref, g_ref, dz_ref, w_ref, u_near, c_near, c_row, *refs):
+    near_own, near_sib, dh_ref, gain_ref = refs
     width = w_ref.shape[1] // 2
     cols = width // 4
-    copy = row_copy(c_any, place_ref[2], c_row, sem)
-    copy.start()
     h = h_ref[...]
-    row_ref[...] = (h + nt(g_ref[...], w_ref[:, width:])).astype(BF)
     pushed = nt(dz_ref[...], w_ref[:, :width])
     for m in range(4):
         at = slice(m * cols, (m + 1) * cols)
@@ -185,17 +172,14 @@
     unit = h * scale
     both = pushed * unit
     gain_ref[...] = jnp.broadcast_to(jnp.sum(both, axis=0, keepdims=True), gain_ref.shape)
-    copy.wait()
     back = c_row[...].astype(F32)
     dh_ref[...] = back + scale * (pushed - unit * jnp.mean(both, axis=-1, keepdims=True))
 
 
-def attention_back_kernel(count, rows, place_ref, x_any, dh_ref, q_ref, k_ref, v_ref, o_ref, p_ref, w_ref, *refs):
+def attention_back_kernel(count, rows, place_ref, x_row, dh_ref, q_ref, k_ref, v_ref, o_ref, p_ref, w_ref, *refs):
     gain_in, bg_ref, row_ref, near_own, far_own, near_sib, far_sib = refs[:7]
-    x_row, flat_d, flat_u, near, far, do_ref, k_flat, dq_flat, ds_ref, dqkv, sem = refs[7:]
+    flat_d, flat_u, near, far, do_ref, k_flat, dq_flat, ds_ref, dqkv = refs[7:]
     z, x = place_ref[0], place_ref[1]
-    copy = row_copy(x_any, place_ref[2], x_row, sem)
-    copy.start()
     low = dh_ref[...].astype(BF)
     do_ref[...] = nn(low, w_ref[:, 1536:2048]).astype(BF)
     k_flat[...] = k_ref[...].T
@@ -211,7 +195,6 @@
     in_relative_rows(flat_d, near, z, x, count, rows, 0)
     in_relative_rows(flat_d, far, z, x, count, rows, 1)
     products(3, o_ref[...])
-    copy.wait()
     states = x_row[...].astype(F32)
     scale = root_scale(states)
     unit = states * scale
@@ -304,12 +287,11 @@
 
 
 def feed_update_kernel(count, place_ref, *refs):
-    count += 1
-    terms, gain, state, outs = refs[:count], refs[count], refs[count + 1 : count + 7], refs[count + 7 :]
-    grad = total(terms)
-    scaled = grad[0] * gain_column(gain, 1)
+    terms_e, terms_s, refs = refs[:count], refs[count : 2 * count], refs[2 * count :]
+    gain, state, outs = refs[0], refs[1:7], refs[7:]
+    scaled = total(terms_e) * gain_column(gain, 1)
     adam_into(outs[:4], [r[...] for r in state[:3]], scaled, 0.05, 0.1)
-    adam_into(outs[4:], [r[...] for r in state[3:]], grad[1], 0.025, 0.1)
+    adam_into(outs[4:], [r[...] for r in state[3:]], total(terms_s), 0.025, 0.1)
 
 
 def attention_update_kernel(count, place_ref, *refs):
@@ -338,10 +320,11 @@
 
 
 def prepare_kernel(place_ref, *refs):
-    whole, first, second = refs[5:8]
-    local, sems = refs[8:13], refs[13]
+    whole, first, second, x_row, c_row = refs[7:12]
+    local, sems = refs[12:17], refs[17]
+    rows = [pltpu.make_async_copy(refs[5 + k].at[place_ref[2]], (x_row, c_row)[k], sems.at[5 + k]) for k in range(2)]
     copies = [pltpu.make_async_copy(refs[k], local[k], sems.at[k]) for k in range(5)]
-    for copy in copies:
+    for copy in copies + rows:
         copy.start()
     for copy in copies:
         copy.wait()
@@ -356,6 +339,8 @@
     second[:, cols:] = shrink[...].astype(BF)
     whole[:, :512] = first[...]
     whole[:, 512:] = second[...]
+    for copy in rows:
+        copy.wait()
 
 
 def put_kernel(messages, place_ref, *refs):
@@ -483,13 +468,15 @@
     where = jnp.stack([dp_at // 2, dp_at % 2, mp_at]).astype(jnp.int32)
 
     masters = [gains_master, attend_master, mixing_master.T, expand_master, shrink_master.T]
-    whole, first, second = call(
+    whole, first, second, x_row, c_row = call(
         prepare_kernel,
-        [struct((rows, 512 + 2 * cols), BF), struct((rows, 512), BF), struct((rows, 2 * cols), BF)],
-        masters,
+        [struct((rows, 512 + 2 * cols), BF), struct((rows, 512), BF), struct((rows, 2 * cols), BF)]
+        + [struct((length, width), BF)] * 2,
+        masters + [blocks, upstream],
         where,
-        scratch=[pltpu.VMEM(a.shape, F32) for a in masters] + [pltpu.SemaphoreType.DMA((5,))],
-        outside=range(5),
+        scratch=[pltpu.VMEM(a.shape, F32) for a in masters] + [pltpu.SemaphoreType.DMA((7,))],
+        outside=range(7),
+
         limit=60,
         moved=2 << 20,
     )
@@ -497,8 +484,9 @@
     sibling = over_core(whole)
     column_one = gather_column(first, sibling[:, :512], count)
     column_two = gather_column(second, sibling[:, 512:], count)
-    near_one, near_two = gather_near(column_one), gather_near(column_two)
-    far_one = gather_far(after(near_one, column_two), core)
+    near_one = gather_near(column_one)
+    near_two = gather_near(after(column_two, near_one))
+    far_one = gather_far(near_one, core)
     sib_far_one = over_core(far_one)
     tiles = length // TILE
     half = count * rows
@@ -510,97 +498,90 @@
             struct((8, tiles, 3 * TILE, TILE), BF),
             struct((width, 2048), BF),
         ],
-        [blocks, block_segment, column_one, near_one, over_core(near_one), far_one, sib_far_one],
+        [x_row, block_segment, column_one, near_one, over_core(near_one), far_one, sib_far_one],
         where,
-        scratch=[pltpu.VMEM((length, width), BF), *[pltpu.VMEM((512, length), BF)] * 2, pltpu.SemaphoreType.DMA],
-        outside=(0,),
+        scratch=[pltpu.VMEM((512, length), BF)] * 2,
         flops=6 * 10**9,
         moved=12 << 20,
         trans=10**6,
     )
-    far_two = gather_far(after(near_two, h), core)
+    far_two = gather_far(near_two, core)
+    sib_far_two = over_core(after(far_two, h))
     pair = struct((2, 2, half, cols), BF)
-    far_own, far_sib, g, dz, w_feed, u_near, c_near = call(
+    *far_grads, g, dz, w_feed, u_near, c_near, row = call(
         functools.partial(feed_kernel, count, rows),
         [
-            pair,
-            pair,
+            *[struct((2, half, cols), BF)] * 4,
             *[struct((length, 4 * cols), BF)] * 2,
             struct((width, 8 * cols), BF),
             *[struct((half, length), BF)] * 2,
+            struct((length, width), BF),
         ],
-        [h, upstream, column_two, near_two, over_core(near_two), far_two, over_core(far_two)],
+        [h, c_row, column_two, near_two, over_core(near_two), far_two, sib_far_two],
         where,
-        scratch=[
-            pltpu.VMEM((length, width), BF),
-            *[pltpu.VMEM((width, length), BF)] * 2,
-            *[pltpu.VMEM((half, length), BF)] * 2,
-            pltpu.SemaphoreType.DMA,
-        ],
-        outside=(1,),
+        scratch=[*[pltpu.VMEM((width, length), BF)] * 2, *[pltpu.VMEM((half, length), BF)] * 2],
         flops=4 * 10**9,
         moved=12 << 20,
         trans=10**6,
     )
-    send = add(far_own, over_core(far_sib))
-    g = after(g, send)
-    near_own, near_sib, row, dh, gain_two = call(
+    send_x = [add(far_grads[k], over_core(far_grads[k + 1])) for k in (0, 2)]
+    g = after(g, send_x)
+    near_own, near_sib, dh, gain_two = call(
         feed_rest_kernel,
         [
             pair,
             pair,
-            struct((length, width), BF),
             struct((length, width), F32),
             struct((8, width), F32),
         ],
-        [h, g, dz, w_feed, u_near, c_near, upstream],
+        [h, g, dz, w_feed, u_near, c_near, c_row],
         where,
-        scratch=[pltpu.VMEM((length, width), BF), pltpu.SemaphoreType.DMA],
-        outside=(6,),
         flops=4 * 10**9,
         moved=12 << 20,
     )
-    far = over_x(send)
+    far = [over_x(value) for value in send_x]
     row_sib, row_across = over_core(row), over_y(row)
     one = struct((2, half + 16, 512), BF)
     bg, row_low, *grads_one = call(
         functools.partial(attention_back_kernel, count, rows),
         [struct((length, width), F32), struct((length, width), BF), one, one, one, one],
-        [blocks, dh, q, k, v, o, probs, weights, gain_two],
+        [x_row, dh, q, k, v, o, probs, weights, gain_two],
         where,
         scratch=[
-            pltpu.VMEM((length, width), BF),
             *[pltpu.VMEM((width, length), BF)] * 2,
             *[pltpu.VMEM((half, length), BF)] * 2,
             pltpu.VMEM((length, 512), BF),
             *[pltpu.VMEM((512, length), BF)] * 2,
             pltpu.VMEM((2, tiles, 3 * TILE, TILE), BF),
             pltpu.VMEM((length, 1536), BF),
-            pltpu.SemaphoreType.DMA,
         ],
-        outside=(0,),
         flops=8 * 10**9,
         moved=12 << 20,
     )
-    bg, row_low, grads_one = after((bg, row_low, grads_one), row_across)
+    bg, row_low = after((bg, row_low), row_across)
+    low_sib, low_across = over_core(row_low), over_y(row_low)
+    grads_one = after(grads_one, far[1])
     result = put(BF, [row, row_sib], 0, where)
     result = put(result, [row_across, over_core(row_across)], 2, where)
     send_one = scatter_start(grads_one)
     far_one = over_x(send_one)
-    low_sib, low_across = over_core(row_low), over_y(row_low)
     low_far = over_core(after(low_across, far_one))
     bg = put(F32, [bg, low_sib], 0, where)
     blocks_grad = put(bg, [low_across, low_far], 2, where)
 
     got = over_core(near_sib)
-    units = [
-        add(*[part[:, :, k * rows : (k + 1) * rows] for part in (near_own, got, far)]) for k in range(count)
-    ]
-    units = [over_z(unit, k) if k else unit for k, unit in enumerate(units)]
     kept_one, send_one_y = scatter_next(grads_one, far_one)
-    units = after(units, far_one, result)
-    send = add(*[unit[:, 1] for unit in units])
-    terms_two = [unit[:, 0] for unit in units] + [over_y(send)]
+    sums = []
+    for k in (1, 0):
+        kept, send = [add(near_own[k, y], got[k, y], far[k][y]) for y in range(2)]
+        if k == 0:
+            send = after(send, low_across)
+        sums.append(add(kept, over_y(send)))
+    sums = sums[::-1]
+    sums[0] = after(sums[0], result)
+    terms_two = []
+    for value in sums:
+        terms_two += [value[:rows]] + [over_z(value[k * rows : (k + 1) * rows], k) for k in range(1, count)]
     sum_one = add(kept_one, over_y(send_one_y))
     parts = [jnp.concatenate([sum_one[k * rows : (k + 1) * rows], sum_one[half:]], axis=0) for k in range(count)]
     terms_one = [over_z(part, k) if k else part for k, part in enumerate(parts)]

time: 153 us -> 149 us (0.974)
  waiting for transfers between devices: 60.1 us -> 52.4 us
  starting transfers between devices: 41.3 us -> 45.9 us
    ppermute x8 -> x11, waiting for transfers between devices: 13.9 us -> 6.21 us  [over_z(): return lax.ppermute(value, 'dp', [(i, (i + 2 * k) % n) for i in range(n)])]
    ppermute x2 -> x3, waiting for transfers between devices: 0.6 us -> 6.77 us  [over_x(): return lax.ppermute(value, 'dp', [(i, i ^ 1) for i in range(n)])]
    ppermute x15 -> x16, waiting for transfers between devices: 10.4 us -> 4.37 us  [over_core(): return lax.ppermute(value, 'mp', [(i, i ^ 1) for i in range(4)])]
    ppermute x8 -> x11, starting transfers between devices: 18.7 us -> 23.4 us  [over_z(): return lax.ppermute(value, 'dp', [(i, (i + 2 * k) % n) for i in range(n)])]
    ppermute x4 -> x5, waiting for transfers between devices: 13.7 us -> 11.8 us  [over_y(): return lax.ppermute(value, 'mp', [(i, i ^ 2) for i in range(4)])]
    ppermute x6, starting transfers between devices: 11.6 us -> 9.71 us  [two_ways(): lax.ppermute(value, ('dp', 'mp'), [(source, dp * 4 + mp) for source, (dp,...]
    ppermute x6, waiting for transfers between devices: 21.5 us -> 23.2 us  [two_ways(): lax.ppermute(value, ('dp', 'mp'), [(source, dp * 4 + mp) for source, (dp,...]
    ppermute x2 -> x3, starting transfers between devices: 2.14 us -> 3.75 us  [over_x(): return lax.ppermute(value, 'dp', [(i, i ^ 1) for i in range(n)])]
  transfers between devices with their start and end apart: 35 -> 41, of which waited for: 15 -> 13; matrix products, arithmetic and copies ran while one was open for 3% -> 3% of each run, Pallas kernels for 21% -> 20%
where the time goes in v2:
time: 149 us
  waiting for transfers between devices  52.4 us (35%)
  starting transfers between devices  45.9 us (31%)
  Pallas kernels  42.3 us (28%)
  other arithmetic  3.58 us (2%)
  local copies, waits for them, and re-layouts  3.13 us (2%)
    pallas_call x7, Pallas kernels, call(): pl.pallas_call(body, out_shape=outs, in_specs=[pl.BlockSpec(memory_space=...  35.3 us
    ppermute x11, starting transfers between devices, over_z(): return lax.ppermute(value, 'dp', [(i, (i + 2 * k) % n) for i in range(n)])  23.4 us
    ppermute x6, waiting for transfers between devices, two_ways(): lax.ppermute(value, ('dp', 'mp'), [(source, dp * 4 + mp) for source, (dp,...  23.2 us
    ppermute x5, waiting for transfers between devices, over_y(): return lax.ppermute(value, 'mp', [(i, i ^ 2) for i in range(4)])  11.8 us
    ppermute x6, starting transfers between devices, two_ways(): lax.ppermute(value, ('dp', 'mp'), [(source, dp * 4 + mp) for source, (dp,...  9.71 us
    pallas_call x4, Pallas kernels, put(): pl.pallas_call(functools.partial(put_kernel, len(messages)), out_shape=st...  7.07 us
    ppermute x3, waiting for transfers between devices, over_x(): return lax.ppermute(value, 'dp', [(i, i ^ 1) for i in range(n)])  6.77 us
    ppermute x5, starting transfers between devices, over_y(): return lax.ppermute(value, 'mp', [(i, i ^ 2) for i in range(4)])  6.28 us
  transfers between devices with their start and end apart: 41, of which 13 were waited for; matrix products, arithmetic and copies ran while one was open for 3% of the time, Pallas kernels for 20%

profile of v2, /device:TPU:0, one launch (start us, length us, event | category | flops | bytes accessed | tf_op | source)
XLA Modules:
  0.0 148.8 jit_solution(1543837812055118199)
XLA Ops:
  1.3 3.2 %shard_map.345 = (bf16[64,1536]{1,0:T(8,128)(2,1)}, bf16[64,512]{1,0:T(8,128)(2,1)}, bf16[64,1024]{1,0:T(8,128)(2,1)}, bf16[512,512]{1,0:T(8,128)(2,1)}, bf16[512,512]{1,0:T(8,128)(2,1)}) custom-call(s32[3]{0:T(128)} %pad_add_fusion.place_ref, f32[2,64]{1,0:T(2,128)} %refs_4_.1, f32[3,64,128]{2,1,0:T(8,128)} %refs_7_.1, f32[64,128]{1,0:T(8,128)} %bitcast.58, ...), custom_call_target="tpu_custom_call" | custom-call | bytes 2097152 | tf_op jit(solution)/shard_map/pallas_call | solution.py:39
  4.5 4.1 %collective-permute-start.1 = (bf16[64,512]{1,0:T(8,128)(2,1)}, bf16[64,512]{1,0:T(8,128)(2,1)S(1)}, u32[]{:S(2)}, u32[]{:S(2)}) collective-permute-start(bf16[64,512]{1,0:T(8,128)(2,1)} %get-tuple-element.91), channel_id=1, source_target_pairs={{0,16},{4,20},{8,24},{12,28},{16,0},{20,4},{24,8},{28,12},{1,17},{... | collective-permute-start | bytes 196616 | tf_op jit(solution)/shard_map/ppermute | solution.py:366
  8.7 0.8 constant_dynamic-update-slice_fusion.4
  9.5 0.9 constant_dynamic-update-slice_fusion.9
  10.5 0.9 pad_maximum_fusion.3
  11.3 1.9 %collective-permute-start.2 = (bf16[128,512]{1,0:T(8,128)(2,1)S(1)}, bf16[128,512]{1,0:T(8,128)(2,1)S(1)}, u32[]{:S(2)}, u32[]{:S(2)}) collective-permute-start(bf16[128,512]{1,0:T(8,128)(2,1)S(1)} %pad_maximum_fusion.3), channel_id=1, source_target_pairs={{0,8},{1,25},{2,10},{3,27},{4,12},{5,29},{6,14},{7,31},{8,16},{9,1... | collective-permute-start | bytes 393224 | tf_op jit(solution)/shard_map/ppermute | solution.py:380
  13.2 0.9 pad_maximum_fusion.1
  14.2 1.6 %collective-permute-start.9 = (bf16[128,1024]{1,0:T(8,128)(2,1)S(1)}, bf16[128,1024]{1,0:T(8,128)(2,1)S(1)}, u32[]{:S(2)}, u32[]{:S(2)}) collective-permute-start(bf16[128,1024]{1,0:T(8,128)(2,1)S(1)} %pad_maximum_fusion.1), channel_id=1, source_target_pairs={{0,8},{1,25},{2,10},{3,27},{4,12},{5,29},{6,14},{7,31},{8,16},{9,1... | collective-permute-start | bytes 786440 | tf_op jit(solution)/shard_map/ppermute | solution.py:380
  15.8 3.8 %collective-permute-done.2 = bf16[128,512]{1,0:T(8,128)(2,1)S(1)} collective-permute-done((bf16[128,512]{1,0:T(8,128)(2,1)S(1)}, bf16[128,512]{1,0:T(8,128)(2,1)S(1)}, u32[]{:S(2)}, u32[]{:S(2)}) %collective-permute-start.2) | collective-permute-done | bytes 131104 | tf_op jit(solution)/shard_map/ppermute | solution.py:380
  19.8 1.4 collective-permute-done.3
  21.1 2.0 %collective-permute-start.4 = (bf16[512,512]{1,0:T(8,128)(2,1)S(1)}, bf16[512,512]{1,0:T(8,128)(2,1)S(1)}, u32[]{:S(2)}, u32[]{:S(2)}) collective-permute-start(bf16[512,512]{1,0:T(8,128)(2,1)S(1)} %constant_dynamic-update-slice_fusion.refs_0_), channel_id=1, source_target_pairs={{0,4},{1,3},{2,6},{3,1},{4,0},{5,7},{6,2},{7,5},{8,12},{9,11},{10,... | collective-permute-start | bytes 1572872 | tf_op jit(solution)/shard_map/ppermute | solution.py:380
  23.1 2.1 %collective-permute-done.9 = bf16[128,1024]{1,0:T(8,128)(2,1)S(1)} collective-permute-done((bf16[128,1024]{1,0:T(8,128)(2,1)S(1)}, bf16[128,1024]{1,0:T(8,128)(2,1)S(1)}, u32[]{:S(2)}, u32[]{:S(2)}) %collective-permute-start.9) | collective-permute-done | bytes 262176 | tf_op jit(solution)/shard_map/ppermute | solution.py:380
  25.6 1.4 collective-permute-done.10
  27.0 3.3 %collective-permute-done.4.refs_1_ = bf16[512,512]{1,0:T(8,128)(2,1)S(1)} collective-permute-done((bf16[512,512]{1,0:T(8,128)(2,1)S(1)}, bf16[512,512]{1,0:T(8,128)(2,1)S(1)}, u32[]{:S(2)}, u32[]{:S(2)}) %collective-permute-start.4) | collective-permute-done | bytes 524320 | tf_op jit(solution)/shard_map/ppermute | solution.py:380
  30.4 1.9 %collective-permute-start.11 = (bf16[512,1024]{1,0:T(8,128)(2,1)S(1)}, bf16[512,1024]{1,0:T(8,128)(2,1)S(1)}, u32[]{:S(2)}, u32[]{:S(2)}) collective-permute-start(bf16[512,1024]{1,0:T(8,128)(2,1)S(1)} %constant_dynamic-update-slice_fusion.5.refs_0_), channel_id=1, source_target_pairs={{0,4},{1,3},{2,6},{3,1},{4,0},{5,7},{6,2},{7,5},{8,12},{9,11},{10,... | collective-permute-start | bytes 3145736 | tf_op jit(solution)/shard_map/ppermute | solution.py:380
  32.3 1.6 %collective-permute-start.6 = (bf16[512,256]{1,0:T(8,128)(2,1)S(1)}, bf16[512,256]{1,0:T(8,128)(2,1)S(1)}, u32[]{:S(2)}, u32[]{:S(2)}) collective-permute-start(bf16[512,256]{1,0:T(8,128)(2,1)S(1)} %constant_dynamic-slice_fusion.1), channel_id=1, source_target_pairs={{0,2},{1,5},{2,0},{3,7},{4,6},{5,1},{6,4},{7,3},{8,10},{9,13},{10,... | collective-permute-start | bytes 786440 | tf_op jit(solution)/shard_map/ppermute | solution.py:380
  33.9 7.7 %collective-permute-done.6.refs_3_ = bf16[512,256]{1,0:T(8,128)(2,1)S(1)} collective-permute-done((bf16[512,256]{1,0:T(8,128)(2,1)S(1)}, bf16[512,256]{1,0:T(8,128)(2,1)S(1)}, u32[]{:S(2)}, u32[]{:S(2)}) %collective-permute-start.6) | collective-permute-done | bytes 262176 | tf_op jit(solution)/shard_map/ppermute | solution.py:380
  41.7 6.3 %collective-permute-done.11.refs_1_ = bf16[512,1024]{1,0:T(8,128)(2,1)S(1)} collective-permute-done((bf16[512,1024]{1,0:T(8,128)(2,1)S(1)}, bf16[512,1024]{1,0:T(8,128)(2,1)S(1)}, u32[]{:S(2)}, u32[]{:S(2)}) %collective-permute-start.11) | collective-permute-done | bytes 1048608 | tf_op jit(solution)/shard_map/ppermute | solution.py:380
  48.0 0.7 collective-permute-start.13
  48.8 1.0 copy-done.16
  49.8 8.6 %shard_map.346 = (f32[512,512]{1,0:T(8,128)S(1)}, bf16[512,512]{1,0:T(8,128)(2,1)S(1)}, bf16[512,512]{1,0:T(8,128)(2,1)S(1)}, bf16[512,512]{1,0:T(8,128)(2,1)S(1...) custom-call(s32[3]{0:T(128)S(1)} %copy-done.12, ...), custom_call_target="tpu_custom_call" | custom-call | flops 6000000000 | bytes 12582912 | tf_op jit(solution)/shard_map/pallas_call | solution.py:39
  59.0 1.5 %collective-permute-done.14.refs_4_ = bf16[512,512]{1,0:T(8,128)(2,1)S(1)} collective-permute-done((bf16[512,512]{1,0:T(8,128)(2,1)S(1)}, bf16[512,512]{1,0:T(8,128)(2,1)S(1)}, u32[]{:S(2)}, u32[]{:S(2)}) %collective-permute-start.14) | collective-permute-done | bytes 524320 | tf_op jit(solution)/shard_map/ppermute | solution.py:374
  60.5 7.8 %shard_map.347 = (bf16[2,256,512]{2,1,0:T(8,128)(2,1)S(1)}, bf16[2,256,512]{2,1,0:T(8,128)(2,1)S(1)}, bf16[2,256,512]{2,1,0:T(8,128)(2,1)S(1)}, bf16[2,256,512]{...) custom-call(s32[3]{0:T(128)S(1)} %copy-done.12, ...), custom_call_target="tpu_custom_call" | custom-call | flops 4000000000 | bytes 12582912 | tf_op jit(solution)/shard_map/pallas_call | solution.py:39
  68.9 1.4 collective-permute-start.16
  70.5 1.9 %collective-permute-start.22 = (bf16[2,256,512]{2,1,0:T(8,128)(2,1)S(1)}, bf16[2,256,512]{2,1,0:T(8,128)(2,1)S(1)}, u32[]{:S(2)}, u32[]{:S(2)}) collective-permute-start(bf16[2,256,512]{2,1,0:T(8,128)(2,1)S(1)} %add_convert_fusion.1), channel_id=1, source_target_pairs={{0,4},{4,0},{8,12},{12,8},{16,20},{20,16},{24,28},{28,24},{1,5},{5... | collective-permute-start | bytes 1572872 | tf_op jit(solution)/shard_map/ppermute | solution.py:361
  72.5 3.2 %shard_map.350 = (bf16[2,2,256,512]{3,2,1,0:T(8,128)(2,1)S(1)}, bf16[2,2,256,512]{3,2,1,0:T(8,128)(2,1)S(1)}, f32[512,512]{1,0:T(8,128)S(1)}, f32[8,512]{1,0:T(8,128)S(1)}) custom-call(s32[3]{0:T(128)S(1)} %copy-done.12, f32[512,512]{1,0:T(8,128)S(1)} %get-tuple-element.93.h_ref, bf16[512,2048]{1,0:T(8,128)(2,1)S(1)} %get-tuple-element.104.g_ref, ...), custom_call_target="tpu_custom_call" | custom-call | flops 4000000000 | bytes 12582912 | tf_op jit(solution)/shard_map/pallas_call | solution.py:39
  75.8 9.3 %shard_map.351 = (f32[512,512]{1,0:T(8,128)S(1)}, bf16[512,512]{1,0:T(8,128)(2,1)S(1)}, bf16[2,272,512]{2,1,0:T(8,128)(2,1)S(1)}, bf16[2,272,512]{2,1,0:T(8,128)...) custom-call(s32[3]{0:T(128)S(1)} %copy-done.12, bf16[512,512]{1,0:T(8,128)(2,1)S(1)} %copy-done.17, ...), custom_call_target="tpu_custom_call" | custom-call | flops 8000000000 | bytes 12582912 | tf_op jit(solution)/shard_map/pallas_call | solution.py:39
  86.2 0.8 collective-permute-start.32
  86.9 1.5 %collective-permute-start.21 = (bf16[512,512]{1,0:T(8,128)(2,1)S(1)}, bf16[512,512]{1,0:T(8,128)(2,1)S(1)}, u32[]{:S(2)}, u32[]{:S(2)}) collective-permute-start(bf16[512,512]{1,0:T(8,128)(2,1)S(1)} %get-tuple-element.120), channel_id=1, source_target_pairs={{0,2},{1,3},{2,0},{3,1},{4,6},{5,7},{6,4},{7,5},{8,10},{9,11},{10,... | collective-permute-start | bytes 1572872 | tf_op jit(solution)/shard_map/ppermute | solution.py:370
  88.7 1.1 collective-permute-start.37
  89.9 1.1 collective-permute-start.24
  91.0 1.6 %shard_map.348.refs_0_ = bf16[4,512,512]{2,1,0:T(8,128)(2,1)} custom-call(s32[3]{0:T(128)S(1)} %copy-done.12, bf16[512,512]{1,0:T(8,128)(2,1)S(1)} %get-tuple-element.98.refs_0_, bf16[512,512]{1,0:T(8,128)(2,1)S(1)} %collective-permute-done.15.refs_1_), custom_call_target="tpu_custom_call" | custom-call | bytes 4194304 | tf_op jit(solution)/shard_map/pallas_call | solution.py:426
  92.6 1.6 %shard_map.349 = bf16[4,512,512]{2,1,0:T(8,128)(2,1)} custom-call(s32[3]{0:T(128)S(1)} %copy-done.12, bf16[4,512,512]{2,1,0:T(8,128)(2,1)} %shard_map.348.refs_0_, bf16[512,512]{1,0:T(8,128)(2,1)S(1)} %collective-permute-done.16.refs_1_, bf16[512,512]{1,0:T(8,128)(2,1)S(1)} %collective-permute-done.17.refs_2_), custom_call_target="tpu_custom_call", output_to_operand_aliasing={{}: (1, {})} | custom-call | bytes 4194304 | tf_op jit(solution)/shard_map/pallas_call | solution.py:426
  94.2 6.8 %collective-permute-done.32 = bf16[2,256,512]{2,1,0:T(8,128)(2,1)S(1)} collective-permute-done((bf16[2,256,512]{2,1,0:T(8,128)(2,1)S(1)}, bf16[2,256,512]{2,1,0:T(8,128)(2,1)S(1)}, u32[]{:S(2)}, u32[]{:S(2)}) %collective-permute-start.32) | collective-permute-done | bytes 524320 | tf_op jit(solution)/shard_map/ppermute | solution.py:361
  100.9 5.7 %collective-permute-done.37 = bf16[256,512]{1,0:T(8,128)(2,1)S(1)} collective-permute-done((bf16[256,512]{1,0:T(8,128)(2,1)S(1)}, bf16[256,512]{1,0:T(8,128)(2,1)S(1)}, u32[]{:S(2)}, u32[]{:S(2)}) %collective-permute-start.37) | collective-permute-done | bytes 262176 | tf_op jit(solution)/shard_map/ppermute | solution.py:370
  106.9 1.6 %collective-permute-start.33 = (bf16[256,512]{1,0:T(8,128)(2,1)S(1)}, bf16[256,512]{1,0:T(8,128)(2,1)S(1)}, u32[]{:S(2)}, u32[]{:S(2)}) collective-permute-start(bf16[256,512]{1,0:T(8,128)(2,1)S(1)} %get-tuple-element.132), channel_id=1, source_target_pairs={{0,2},{1,3},{2,0},{3,1},{4,6},{5,7},{6,4},{7,5},{8,10},{9,11},{10,... | collective-permute-start | bytes 786440 | tf_op jit(solution)/shard_map/ppermute | solution.py:370
  108.5 6.5 %collective-permute-start.40 = (bf16[64,512]{1,0:T(8,128)(2,1)S(1)}, bf16[64,512]{1,0:T(8,128)(2,1)S(1)}, u32[]{:S(2)}, u32[]{:S(2)}) collective-permute-start(bf16[64,512]{1,0:T(8,128)(2,1)S(1)} %get-tuple-element.163), channel_id=1, source_target_pairs={{0,24},{4,28},{8,0},{12,4},{16,8},{20,12},{24,16},{28,20},{1,25},{... | collective-permute-start | bytes 196616 | tf_op jit(solution)/shard_map/ppermute | solution.py:366
  115.0 1.2 collective-permute-start.38
  117.1 6.1 %collective-permute-done.27 = bf16[272,512]{1,0:T(8,128)(2,1)S(1)} collective-permute-done((bf16[272,512]{1,0:T(8,128)(2,1)S(1)}, bf16[272,512]{1,0:T(8,128)(2,1)S(1)}, u32[]{:S(2)}, u32[]{:S(2)}) %collective-permute-start.27) | collective-permute-done | bytes 278560 | tf_op jit(solution)/shard_map/ppermute | solution.py:370
  123.5 4.6 %collective-permute-start.36 = (bf16[64,512]{1,0:T(8,128)(2,1)S(1)}, bf16[64,512]{1,0:T(8,128)(2,1)S(1)}, u32[]{:S(2)}, u32[]{:S(2)}) collective-permute-start(bf16[64,512]{1,0:T(8,128)(2,1)S(1)} %get-tuple-element.167), channel_id=1, source_target_pairs={{0,24},{4,28},{8,0},{12,4},{16,8},{20,12},{24,16},{28,20},{1,25},{... | collective-permute-start | bytes 196616 | tf_op jit(solution)/shard_map/ppermute | solution.py:366
  128.2 3.0 %collective-permute-start.29 = (bf16[80,512]{1,0:T(8,128)(2,1)S(1)}, bf16[80,512]{1,0:T(8,128)(2,1)S(1)}, u32[]{:S(2)}, u32[]{:S(2)}) collective-permute-start(bf16[80,512]{1,0:T(8,128)(2,1)S(1)} %get-tuple-element.175), channel_id=1, source_target_pairs={{0,16},{4,20},{8,24},{12,28},{16,0},{20,4},{24,8},{28,12},{1,17},{... | collective-permute-start | bytes 245768 | tf_op jit(solution)/shard_map/ppermute | solution.py:366
  131.2 3.8 %collective-permute-start.30 = (bf16[80,512]{1,0:T(8,128)(2,1)S(1)}, bf16[80,512]{1,0:T(8,128)(2,1)S(1)}, u32[]{:S(2)}, u32[]{:S(2)}) collective-permute-start(bf16[80,512]{1,0:T(8,128)(2,1)S(1)} %concatenate.42), channel_id=1, source_target_pairs={{0,24},{4,28},{8,0},{12,4},{16,8},{20,12},{24,16},{28,20},{1,25},{... | collective-permute-start | bytes 245768 | tf_op jit(solution)/shard_map/ppermute | solution.py:366
  135.0 2.1 %collective-permute-done.35.refs_2_ = bf16[64,512]{1,0:T(8,128)(2,1)S(1)} collective-permute-done((bf16[64,512]{1,0:T(8,128)(2,1)S(1)}, bf16[64,512]{1,0:T(8,128)(2,1)S(1)}, u32[]{:S(2)}, u32[]{:S(2)}) %collective-permute-start.35) | collective-permute-done | bytes 65568 | tf_op jit(solution)/shard_map/ppermute | solution.py:366
  137.2 2.0 %shard_map.352.refs_0_ = f32[4,512,512]{2,1,0:T(8,128)} custom-call(s32[3]{0:T(128)S(1)} %copy-done.12, f32[512,512]{1,0:T(8,128)S(1)} %get-tuple-element.119.refs_0_, bf16[512,512]{1,0:T(8,128)(2,1)S(1)} %collective-permute-done.20.refs_1_), custom_call_target="tpu_custom_call" | custom-call | bytes 4194304 | tf_op jit(solution)/shard_map/pallas_call | solution.py:426
  139.1 4.1 %collective-permute-done.34.refs_1_ = bf16[64,512]{1,0:T(8,128)(2,1)S(1)} collective-permute-done((bf16[64,512]{1,0:T(8,128)(2,1)S(1)}, bf16[64,512]{1,0:T(8,128)(2,1)S(1)}, u32[]{:S(2)}, u32[]{:S(2)}) %collective-permute-start.34) | collective-permute-done | bytes 65568 | tf_op jit(solution)/shard_map/ppermute | solution.py:366
  143.3 1.7 %shard_map.354 = (f32[64,512]{1,0:T(8,128)}, f32[64,512]{1,0:T(8,128)}, f32[64,512]{1,0:T(8,128)}, bf16[64,512]{1,0:T(8,128)(2,1)}, f32[64,512]{1,0:T(8,128)}, /...) custom-call(s32[3]{0:T(128)S(1)} %copy-done.12, bf16[64,512]{1,0:T(8,128)(2,1)S(1)} %get-tuple-element.170.refs_0_, ...), custom_call_target="tpu_custom_call" | custom-call | bytes 3145728 | tf_op jit(solution)/shard_map/pallas_call | solution.py:39
  145.1 2.0 %shard_map.353 = f32[4,512,512]{2,1,0:T(8,128)} custom-call(s32[3]{0:T(128)S(1)} %copy-done.12, f32[4,512,512]{2,1,0:T(8,128)} %shard_map.352.refs_0_, bf16[512,512]{1,0:T(8,128)(2,1)S(1)} %collective-permute-done.21.refs_1_, bf16[512,512]{1,0:T(8,128)(2,1)S(1)} %collective-permute-done.25.refs_2_), custom_call_target="tpu_custom_call", output_to_operand_aliasing={{}: (1, {})} | custom-call | bytes 4194304 | tf_op jit(solution)/shard_map/pallas_call | solution.py:426
  147.1 1.5 shard_map.355
  (116 shorter events, 5.7 us)
Async XLA Ops:
  4.5 11.3 %collective-permute-start.1 = (bf16[64,512]{1,0:T(8,128)(2,1)}, bf16[64,512]{1,0:T(8,128)(2,1)S(1)}, u32[]{:S(2)}, u32[]{:S(2)}) collective-permute-start(bf16[64,512]{1,0:T(8,128)(2,1)} %get-tuple-element.91), channel_id=1, source_target_pairs={{0,16},{4,20},{8,24},{12,28},{16,0},{20,4},{24,8},{28,12},{1,17},{... | collective-permute-start | bytes 196616 | tf_op jit(solution)/shard_map/ppermute | solution.py:366
  8.6 14.5 %collective-permute-start.8 = (bf16[64,1024]{1,0:T(8,128)(2,1)}, bf16[64,1024]{1,0:T(8,128)(2,1)S(1)}, u32[]{:S(2)}, u32[]{:S(2)}) collective-permute-start(bf16[64,1024]{1,0:T(8,128)(2,1)} %get-tuple-element.95), channel_id=1, source_target_pairs={{0,16},{4,20},{8,24},{12,28},{16,0},{20,4},{24,8},{28,12},{1,17},{... | collective-permute-start | bytes 393224 | tf_op jit(solution)/shard_map/ppermute | solution.py:366
  8.7 1.8 %collective-permute-start = (bf16[64,1536]{1,0:T(8,128)(2,1)}, bf16[64,1536]{1,0:T(8,128)(2,1)S(1)}, u32[]{:S(2)}, u32[]{:S(2)}) collective-permute-start(bf16[64,1536]{1,0:T(8,128)(2,1)} %get-tuple-element.92), channel_id=1, source_target_pairs={{0,1},{1,0},{2,3},{3,2},{4,5},{5,4},{6,7},{7,6},{8,9},{9,8},{10,11... | collective-permute-start | bytes 589832 | tf_op jit(solution)/shard_map/ppermute | solution.py:374
  11.3 8.3 %collective-permute-start.2 = (bf16[128,512]{1,0:T(8,128)(2,1)S(1)}, bf16[128,512]{1,0:T(8,128)(2,1)S(1)}, u32[]{:S(2)}, u32[]{:S(2)}) collective-permute-start(bf16[128,512]{1,0:T(8,128)(2,1)S(1)} %pad_maximum_fusion.3), channel_id=1, source_target_pairs={{0,8},{1,25},{2,10},{3,27},{4,12},{5,29},{6,14},{7,31},{8,16},{9,1... | collective-permute-start | bytes 393224 | tf_op jit(solution)/shard_map/ppermute | solution.py:380
  14.2 11.0 %collective-permute-start.9 = (bf16[128,1024]{1,0:T(8,128)(2,1)S(1)}, bf16[128,1024]{1,0:T(8,128)(2,1)S(1)}, u32[]{:S(2)}, u32[]{:S(2)}) collective-permute-start(bf16[128,1024]{1,0:T(8,128)(2,1)S(1)} %pad_maximum_fusion.1), channel_id=1, source_target_pairs={{0,8},{1,25},{2,10},{3,27},{4,12},{5,29},{6,14},{7,31},{8,16},{9,1... | collective-permute-start | bytes 786440 | tf_op jit(solution)/shard_map/ppermute | solution.py:380
  19.6 1.5 %collective-permute-start.3 = (bf16[192,512]{1,0:T(8,128)(2,1)S(1)}, bf16[192,512]{1,0:T(8,128)(2,1)S(1)}, u32[]{:S(2)}, u32[]{:S(2)}) collective-permute-start(bf16[192,512]{1,0:T(8,128)(2,1)S(1)} %pad_maximum_fusion.2), channel_id=1, source_target_pairs={{0,1},{1,0},{2,3},{3,2},{4,5},{5,4},{6,7},{7,6},{8,9},{9,8},{10,11... | collective-permute-start | bytes 589832 | tf_op jit(solution)/shard_map/ppermute | solution.py:374
  19.7 29.0 %copy-start.12 = (s32[3]{0:T(128)S(1)}, s32[3]{0:T(128)}, u32[]{:S(2)}) copy-start(s32[3]{0:T(128)} %pad_add_fusion.place_ref) | copy-start | bytes 40
  19.7 29.0 %copy-start.19 = (s32[4,512]{1,0:T(4,128)S(1)}, s32[4,512]{1,0:T(4,128)}, u32[]{:S(2)}) copy-start(s32[4,512]{1,0:T(4,128)} %seg_ref.1) | copy-start | bytes 24580
  21.1 9.2 %collective-permute-start.4 = (bf16[512,512]{1,0:T(8,128)(2,1)S(1)}, bf16[512,512]{1,0:T(8,128)(2,1)S(1)}, u32[]{:S(2)}, u32[]{:S(2)}) collective-permute-start(bf16[512,512]{1,0:T(8,128)(2,1)S(1)} %constant_dynamic-update-slice_fusion.refs_0_), channel_id=1, source_target_pairs={{0,4},{1,3},{2,6},{3,1},{4,0},{5,7},{6,2},{7,5},{8,12},{9,11},{10,... | collective-permute-start | bytes 1572872 | tf_op jit(solution)/shard_map/ppermute | solution.py:380
  25.2 1.8 %collective-permute-start.10 = (bf16[192,1024]{1,0:T(8,128)(2,1)S(1)}, bf16[192,1024]{1,0:T(8,128)(2,1)S(1)}, u32[]{:S(2)}, u32[]{:S(2)}) collective-permute-start(bf16[192,1024]{1,0:T(8,128)(2,1)S(1)} %pad_maximum_fusion), channel_id=1, source_target_pairs={{0,1},{1,0},{2,3},{3,2},{4,5},{5,4},{6,7},{7,6},{8,9},{9,8},{10,11... | collective-permute-start | bytes 1179656 | tf_op jit(solution)/shard_map/ppermute | solution.py:374
  30.4 17.6 %collective-permute-start.11 = (bf16[512,1024]{1,0:T(8,128)(2,1)S(1)}, bf16[512,1024]{1,0:T(8,128)(2,1)S(1)}, u32[]{:S(2)}, u32[]{:S(2)}) collective-permute-start(bf16[512,1024]{1,0:T(8,128)(2,1)S(1)} %constant_dynamic-update-slice_fusion.5.refs_0_), channel_id=1, source_target_pairs={{0,4},{1,3},{2,6},{3,1},{4,0},{5,7},{6,2},{7,5},{8,12},{9,11},{10,... | collective-permute-start | bytes 3145736 | tf_op jit(solution)/shard_map/ppermute | solution.py:380
  32.3 9.3 %collective-permute-start.6 = (bf16[512,256]{1,0:T(8,128)(2,1)S(1)}, bf16[512,256]{1,0:T(8,128)(2,1)S(1)}, u32[]{:S(2)}, u32[]{:S(2)}) collective-permute-start(bf16[512,256]{1,0:T(8,128)(2,1)S(1)} %constant_dynamic-slice_fusion.1), channel_id=1, source_target_pairs={{0,2},{1,5},{2,0},{3,7},{4,6},{5,1},{6,4},{7,3},{8,10},{9,13},{10,... | collective-permute-start | bytes 786440 | tf_op jit(solution)/shard_map/ppermute | solution.py:380
  33.9 14.8 %collective-permute-start.5 = (bf16[512,512]{1,0:T(8,128)(2,1)S(1)}, bf16[512,512]{1,0:T(8,128)(2,1)}, u32[]{:S(2)}, u32[]{:S(2)}) collective-permute-start(bf16[512,512]{1,0:T(8,128)(2,1)S(1)} %collective-permute-done.4.refs_1_), channel_id=1, source_target_pairs={{0,1},{1,0},{2,3},{3,2},{4,5},{5,4},{6,7},{7,6},{8,9},{9,8},{10,11... | collective-permute-start | bytes 1572872 | tf_op jit(solution)/shard_map/ppermute | solution.py:374
  41.7 7.1 %collective-permute-start.7 = (bf16[512,256]{1,0:T(8,128)(2,1)S(1)}, bf16[512,256]{1,0:T(8,128)(2,1)}, u32[]{:S(2)}, u32[]{:S(2)}) collective-permute-start(bf16[512,256]{1,0:T(8,128)(2,1)S(1)} %collective-permute-done.6.refs_3_), channel_id=1, source_target_pairs={{0,1},{1,0},{2,3},{3,2},{4,5},{5,4},{6,7},{7,6},{8,9},{9,8},{10,11... | collective-permute-start | bytes 786440 | tf_op jit(solution)/shard_map/ppermute | solution.py:374
  48.0 10.4 %collective-permute-start.13 = (bf16[512,512]{1,0:T(8,128)(2,1)S(1)}, bf16[512,512]{1,0:T(8,128)(2,1)S(1)}, u32[]{:S(2)}, u32[]{:S(2)}) collective-permute-start(bf16[512,512]{1,0:T(8,128)(2,1)S(1)} %constant_dynamic-slice_fusion), channel_id=1, source_target_pairs={{0,2},{1,5},{2,0},{3,7},{4,6},{5,1},{6,4},{7,3},{8,10},{9,13},{10,... | collective-permute-start | bytes 1572872 | tf_op jit(solution)/shard_map/ppermute | solution.py:380
  48.7 10.3 %collective-permute-start.12 = (bf16[512,1024]{1,0:T(8,128)(2,1)S(1)}, bf16[512,1024]{1,0:T(8,128)(2,1)S(1)}, u32[]{:S(2)}, u32[]{:S(2)}) collective-permute-start(bf16[512,1024]{1,0:T(8,128)(2,1)S(1)} %collective-permute-done.11.refs_1_), channel_id=1, source_target_pairs={{0,1},{1,0},{2,3},{3,2},{4,5},{5,4},{6,7},{7,6},{8,9},{9,8},{10,11... | collective-permute-start | bytes 3145736 | tf_op jit(solution)/shard_map/ppermute | solution.py:374
  49.8 10.7 %copy-start.18 = (bf16[512,512]{1,0:T(8,128)(2,1)S(1)}, bf16[512,512]{1,0:T(8,128)(2,1)}, u32[]{:S(2)}) copy-start(bf16[512,512]{1,0:T(8,128)(2,1)} %get-tuple-element.94.c_row) | copy-start | bytes 1572868
  58.4 2.1 %collective-permute-start.14 = (bf16[512,512]{1,0:T(8,128)(2,1)S(1)}, bf16[512,512]{1,0:T(8,128)(2,1)S(1)}, u32[]{:S(2)}, u32[]{:S(2)}) collective-permute-start(bf16[512,512]{1,0:T(8,128)(2,1)S(1)} %collective-permute-done.13.refs_3_), channel_id=1, source_target_pairs={{0,1},{1,0},{2,3},{3,2},{4,5},{5,4},{6,7},{7,6},{8,9},{9,8},{10,11... | collective-permute-start | bytes 1572872 | tf_op jit(solution)/shard_map/ppermute | solution.py:374
  68.3 2.0 %collective-permute-start.19 = (bf16[2,256,512]{2,1,0:T(8,128)(2,1)S(1)}, bf16[2,256,512]{2,1,0:T(8,128)(2,1)S(1)}, u32[]{:S(2)}, u32[]{:S(2)}) collective-permute-start(bf16[2,256,512]{2,1,0:T(8,128)(2,1)S(1)} %get-tuple-element.103), channel_id=1, source_target_pairs={{0,1},{1,0},{2,3},{3,2},{4,5},{5,4},{6,7},{7,6},{8,9},{9,8},{10,11... | collective-permute-start | bytes 1572872 | tf_op jit(solution)/shard_map/ppermute | solution.py:374
  68.7 3.6 %collective-permute-start.18 = (bf16[2,256,512]{2,1,0:T(8,128)(2,1)S(1)}, bf16[2,256,512]{2,1,0:T(8,128)(2,1)S(1)}, u32[]{:S(2)}, u32[]{:S(2)}) collective-permute-start(bf16[2,256,512]{2,1,0:T(8,128)(2,1)S(1)} %get-tuple-element.101), channel_id=1, source_target_pairs={{0,1},{1,0},{2,3},{3,2},{4,5},{5,4},{6,7},{7,6},{8,9},{9,8},{10,11... | collective-permute-start | bytes 1572872 | tf_op jit(solution)/shard_map/ppermute | solution.py:374
  68.9 16.9 %collective-permute-start.16 = (bf16[512,512]{1,0:T(8,128)(2,1)S(1)}, bf16[512,512]{1,0:T(8,128)(2,1)S(1)}, u32[]{:S(2)}, u32[]{:S(2)}) collective-permute-start(bf16[512,512]{1,0:T(8,128)(2,1)S(1)} %get-tuple-element.98.refs_0_), channel_id=1, source_target_pairs={{0,2},{1,3},{2,0},{3,1},{4,6},{5,7},{6,4},{7,5},{8,10},{9,11},{10,... | collective-permute-start | bytes 1572872 | tf_op jit(solution)/shard_map/ppermute | solution.py:370
  70.5 14.6 %collective-permute-start.22 = (bf16[2,256,512]{2,1,0:T(8,128)(2,1)S(1)}, bf16[2,256,512]{2,1,0:T(8,128)(2,1)S(1)}, u32[]{:S(2)}, u32[]{:S(2)}) collective-permute-start(bf16[2,256,512]{2,1,0:T(8,128)(2,1)S(1)} %add_convert_fusion.1), channel_id=1, source_target_pairs={{0,4},{4,0},{8,12},{12,8},{16,20},{20,16},{24,28},{28,24},{1,5},{5... | collective-permute-start | bytes 1572872 | tf_op jit(solution)/shard_map/ppermute | solution.py:361
  75.7 11.2 %collective-permute-start.31 = (bf16[2,2,256,512]{3,2,1,0:T(8,128)(2,1)S(1)}, bf16[2,2,256,512]{3,2,1,0:T(8,128)(2,1)S(1)}, u32[]{:S(2)}, u32[]{:S(2)}) collective-permute-start(bf16[2,2,256,512]{3,2,1,0:T(8,128)(2,1)S(1)} %get-tuple-element.131), channel_id=1, source_target_pairs={{0,1},{1,0},{2,3},{3,2},{4,5},{5,4},{6,7},{7,6},{8,9},{9,8},{10,11... | collective-permute-start | bytes 3145736 | tf_op jit(solution)/shard_map/ppermute | solution.py:374
  85.1 3.6 %collective-permute-start.23 = (bf16[2,272,512]{2,1,0:T(8,128)(2,1)S(1)}, bf16[2,272,512]{2,1,0:T(8,128)(2,1)S(1)}, u32[]{:S(2)}, u32[]{:S(2)}) collective-permute-start(bf16[2,272,512]{2,1,0:T(8,128)(2,1)S(1)} %get-tuple-element.126), channel_id=1, source_target_pairs={{0,1},{1,0},{2,3},{3,2},{4,5},{5,4},{6,7},{7,6},{8,9},{9,8},{10,11... | collective-permute-start | bytes 1671176 | tf_op jit(solution)/shard_map/ppermute | solution.py:374
  85.7 2.9 %collective-permute-start.15 = (bf16[512,512]{1,0:T(8,128)(2,1)S(1)}, bf16[512,512]{1,0:T(8,128)(2,1)S(1)}, u32[]{:S(2)}, u32[]{:S(2)}) collective-permute-start(bf16[512,512]{1,0:T(8,128)(2,1)S(1)} %get-tuple-element.98.refs_0_), channel_id=1, source_target_pairs={{0,1},{1,0},{2,3},{3,2},{4,5},{5,4},{6,7},{7,6},{8,9},{9,8},{10,11... | collective-permute-start | bytes 1572872 | tf_op jit(solution)/shard_map/ppermute | solution.py:374
  85.7 4.2 %collective-permute-start.17 = (bf16[512,512]{1,0:T(8,128)(2,1)S(1)}, bf16[512,512]{1,0:T(8,128)(2,1)S(1)}, u32[]{:S(2)}, u32[]{:S(2)}) collective-permute-start(bf16[512,512]{1,0:T(8,128)(2,1)S(1)} %collective-permute-done.16.refs_1_), channel_id=1, source_target_pairs={{0,1},{1,0},{2,3},{3,2},{4,5},{5,4},{6,7},{7,6},{8,9},{9,8},{10,11... | collective-permute-start | bytes 1572872 | tf_op jit(solution)/shard_map/ppermute | solution.py:374
  86.2 14.8 %collective-permute-start.32 = (bf16[2,256,512]{2,1,0:T(8,128)(2,1)S(1)}, bf16[2,256,512]{2,1,0:T(8,128)(2,1)S(1)}, u32[]{:S(2)}, u32[]{:S(2)}) collective-permute-start(bf16[2,256,512]{2,1,0:T(8,128)(2,1)S(1)} %add_convert_fusion.2), channel_id=1, source_target_pairs={{0,4},{4,0},{8,12},{12,8},{16,20},{20,16},{24,28},{28,24},{1,5},{5... | collective-permute-start | bytes 1572872 | tf_op jit(solution)/shard_map/ppermute | solution.py:361
  86.9 19.9 %collective-permute-start.21 = (bf16[512,512]{1,0:T(8,128)(2,1)S(1)}, bf16[512,512]{1,0:T(8,128)(2,1)S(1)}, u32[]{:S(2)}, u32[]{:S(2)}) collective-permute-start(bf16[512,512]{1,0:T(8,128)(2,1)S(1)} %get-tuple-element.120), channel_id=1, source_target_pairs={{0,2},{1,3},{2,0},{3,1},{4,6},{5,7},{6,4},{7,5},{8,10},{9,11},{10,... | collective-permute-start | bytes 1572872 | tf_op jit(solution)/shard_map/ppermute | solution.py:370
  88.6 26.4 %collective-permute-start.26 = (bf16[2,272,512]{2,1,0:T(8,128)(2,1)S(1)}, bf16[2,272,512]{2,1,0:T(8,128)(2,1)S(1)}, u32[]{:S(2)}, u32[]{:S(2)}) collective-permute-start(bf16[2,272,512]{2,1,0:T(8,128)(2,1)S(1)} %get-tuple-element.129), channel_id=1, source_target_pairs={{0,1},{1,0},{2,3},{3,2},{4,5},{5,4},{6,7},{7,6},{8,9},{9,8},{10,11... | collective-permute-start | bytes 1671176 | tf_op jit(solution)/shard_map/ppermute | solution.py:374
  88.7 17.9 %collective-permute-start.37 = (bf16[256,512]{1,0:T(8,128)(2,1)S(1)}, bf16[256,512]{1,0:T(8,128)(2,1)S(1)}, u32[]{:S(2)}, u32[]{:S(2)}) collective-permute-start(bf16[256,512]{1,0:T(8,128)(2,1)S(1)} %fusion.1), channel_id=1, source_target_pairs={{0,2},{1,3},{2,0},{3,1},{4,6},{5,7},{6,4},{7,5},{8,10},{9,11},{10,... | collective-permute-start | bytes 786440 | tf_op jit(solution)/shard_map/ppermute | solution.py:370
  89.9 25.1 %collective-permute-start.24 = (bf16[2,272,512]{2,1,0:T(8,128)(2,1)S(1)}, bf16[2,272,512]{2,1,0:T(8,128)(2,1)S(1)}, u32[]{:S(2)}, u32[]{:S(2)}) collective-permute-start(bf16[2,272,512]{2,1,0:T(8,128)(2,1)S(1)} %add_convert_fusion), channel_id=1, source_target_pairs={{0,4},{4,0},{8,12},{12,8},{16,20},{20,16},{24,28},{28,24},{1,5},{5... | collective-permute-start | bytes 1671176 | tf_op jit(solution)/shard_map/ppermute | solution.py:361
  100.9 22.5 %collective-permute-start.20 = (bf16[512,512]{1,0:T(8,128)(2,1)S(1)}, bf16[512,512]{1,0:T(8,128)(2,1)S(1)}, u32[]{:S(2)}, u32[]{:S(2)}) collective-permute-start(bf16[512,512]{1,0:T(8,128)(2,1)S(1)} %get-tuple-element.120), channel_id=1, source_target_pairs={{0,1},{1,0},{2,3},{3,2},{4,5},{5,4},{6,7},{7,6},{8,9},{9,8},{10,11... | collective-permute-start | bytes 1572872 | tf_op jit(solution)/shard_map/ppermute | solution.py:374
  106.9 9.5 %collective-permute-start.33 = (bf16[256,512]{1,0:T(8,128)(2,1)S(1)}, bf16[256,512]{1,0:T(8,128)(2,1)S(1)}, u32[]{:S(2)}, u32[]{:S(2)}) collective-permute-start(bf16[256,512]{1,0:T(8,128)(2,1)S(1)} %get-tuple-element.132), channel_id=1, source_target_pairs={{0,2},{1,3},{2,0},{3,1},{4,6},{5,7},{6,4},{7,5},{8,10},{9,11},{10,... | collective-permute-start | bytes 786440 | tf_op jit(solution)/shard_map/ppermute | solution.py:370
  108.5 19.6 %collective-permute-start.40 = (bf16[64,512]{1,0:T(8,128)(2,1)S(1)}, bf16[64,512]{1,0:T(8,128)(2,1)S(1)}, u32[]{:S(2)}, u32[]{:S(2)}) collective-permute-start(bf16[64,512]{1,0:T(8,128)(2,1)S(1)} %get-tuple-element.163), channel_id=1, source_target_pairs={{0,24},{4,28},{8,0},{12,4},{16,8},{20,12},{24,16},{28,20},{1,25},{... | collective-permute-start | bytes 196616 | tf_op jit(solution)/shard_map/ppermute | solution.py:366
  115.0 13.1 %collective-permute-start.39 = (bf16[64,512]{1,0:T(8,128)(2,1)S(1)}, bf16[64,512]{1,0:T(8,128)(2,1)S(1)}, u32[]{:S(2)}, u32[]{:S(2)}) collective-permute-start(bf16[64,512]{1,0:T(8,128)(2,1)S(1)} %get-tuple-element.164), channel_id=1, source_target_pairs={{0,16},{4,20},{8,24},{12,28},{16,0},{20,4},{24,8},{28,12},{1,17},{... | collective-permute-start | bytes 196616 | tf_op jit(solution)/shard_map/ppermute | solution.py:366
  115.0 16.1 %collective-permute-start.38 = (bf16[64,512]{1,0:T(8,128)(2,1)S(1)}, bf16[64,512]{1,0:T(8,128)(2,1)S(1)}, u32[]{:S(2)}, u32[]{:S(2)}) collective-permute-start(bf16[64,512]{1,0:T(8,128)(2,1)S(1)} %get-tuple-element.165), channel_id=1, source_target_pairs={{0,8},{4,12},{8,16},{12,20},{16,24},{20,28},{24,0},{28,4},{1,9},{5... | collective-permute-start | bytes 196616 | tf_op jit(solution)/shard_map/ppermute | solution.py:366
  116.3 6.9 %collective-permute-start.27 = (bf16[272,512]{1,0:T(8,128)(2,1)S(1)}, bf16[272,512]{1,0:T(8,128)(2,1)S(1)}, u32[]{:S(2)}, u32[]{:S(2)}) collective-permute-start(bf16[272,512]{1,0:T(8,128)(2,1)S(1)} %fusion.6), channel_id=1, source_target_pairs={{0,2},{1,3},{2,0},{3,1},{4,6},{5,7},{6,4},{7,5},{8,10},{9,11},{10,... | collective-permute-start | bytes 835592 | tf_op jit(solution)/shard_map/ppermute | solution.py:370
  123.3 21.8 %collective-permute-start.25 = (bf16[512,512]{1,0:T(8,128)(2,1)S(1)}, bf16[512,512]{1,0:T(8,128)(2,1)S(1)}, u32[]{:S(2)}, u32[]{:S(2)}) collective-permute-start(bf16[512,512]{1,0:T(8,128)(2,1)S(1)} %collective-permute-done.21.refs_1_), channel_id=1, source_target_pairs={{0,1},{1,0},{2,3},{3,2},{4,5},{5,4},{6,7},{7,6},{8,9},{9,8},{10,11... | collective-permute-start | bytes 1572872 | tf_op jit(solution)/shard_map/ppermute | solution.py:374
  123.5 7.7 %collective-permute-start.36 = (bf16[64,512]{1,0:T(8,128)(2,1)S(1)}, bf16[64,512]{1,0:T(8,128)(2,1)S(1)}, u32[]{:S(2)}, u32[]{:S(2)}) collective-permute-start(bf16[64,512]{1,0:T(8,128)(2,1)S(1)} %get-tuple-element.167), channel_id=1, source_target_pairs={{0,24},{4,28},{8,0},{12,4},{16,8},{20,12},{24,16},{28,20},{1,25},{... | collective-permute-start | bytes 196616 | tf_op jit(solution)/shard_map/ppermute | solution.py:366
  128.1 9.0 %collective-permute-start.35 = (bf16[64,512]{1,0:T(8,128)(2,1)S(1)}, bf16[64,512]{1,0:T(8,128)(2,1)S(1)}, u32[]{:S(2)}, u32[]{:S(2)}) collective-permute-start(bf16[64,512]{1,0:T(8,128)(2,1)S(1)} %get-tuple-element.168), channel_id=1, source_target_pairs={{0,16},{4,20},{8,24},{12,28},{16,0},{20,4},{24,8},{28,12},{1,17},{... | collective-permute-start | bytes 196616 | tf_op jit(solution)/shard_map/ppermute | solution.py:366
  128.2 18.9 %collective-permute-start.29 = (bf16[80,512]{1,0:T(8,128)(2,1)S(1)}, bf16[80,512]{1,0:T(8,128)(2,1)S(1)}, u32[]{:S(2)}, u32[]{:S(2)}) collective-permute-start(bf16[80,512]{1,0:T(8,128)(2,1)S(1)} %get-tuple-element.175), channel_id=1, source_target_pairs={{0,16},{4,20},{8,24},{12,28},{16,0},{20,4},{24,8},{28,12},{1,17},{... | collective-permute-start | bytes 245768 | tf_op jit(solution)/shard_map/ppermute | solution.py:366
  131.1 15.9 %collective-permute-start.28 = (bf16[80,512]{1,0:T(8,128)(2,1)S(1)}, bf16[80,512]{1,0:T(8,128)(2,1)S(1)}, u32[]{:S(2)}, u32[]{:S(2)}) collective-permute-start(bf16[80,512]{1,0:T(8,128)(2,1)S(1)} %get-tuple-element.176), channel_id=1, source_target_pairs={{0,8},{4,12},{8,16},{12,20},{16,24},{20,28},{24,0},{28,4},{1,9},{5... | collective-permute-start | bytes 245768 | tf_op jit(solution)/shard_map/ppermute | solution.py:366
  131.2 15.9 %collective-permute-start.30 = (bf16[80,512]{1,0:T(8,128)(2,1)S(1)}, bf16[80,512]{1,0:T(8,128)(2,1)S(1)}, u32[]{:S(2)}, u32[]{:S(2)}) collective-permute-start(bf16[80,512]{1,0:T(8,128)(2,1)S(1)} %concatenate.42), channel_id=1, source_target_pairs={{0,24},{4,28},{8,0},{12,4},{16,8},{20,12},{24,16},{28,20},{1,25},{... | collective-permute-start | bytes 245768 | tf_op jit(solution)/shard_map/ppermute | solution.py:366
  137.1 6.2 %copy-start.5 = (f32[64,512]{1,0:T(8,128)S(1)}, f32[64,512]{1,0:T(8,128)}, u32[]{:S(2)}) copy-start(f32[64,512]{1,0:T(8,128)} %refs_11_.1) | copy-start | bytes 393220
  137.1 6.2 %copy-start.6 = (f32[512,64]{0,1:T(8,128)S(1)}, f32[512,64]{0,1:T(8,128)}, u32[]{:S(2)}) copy-start(f32[512,64]{0,1:T(8,128)} %param.31) | copy-start | bytes 393220
  137.1 6.2 %copy-start.7 = (f32[512,64]{0,1:T(8,128)S(1)}, f32[512,64]{0,1:T(8,128)}, u32[]{:S(2)}) copy-start(f32[512,64]{0,1:T(8,128)} %param.32) | copy-start | bytes 393220
  137.1 6.2 %copy-start.13 = (f32[2,64]{1,0:T(2,128)S(1)}, f32[2,64]{1,0:T(2,128)}, u32[]{:S(2)}) copy-start(f32[2,64]{1,0:T(2,128)} %refs_4_.1) | copy-start | bytes 1540
  137.1 6.1 %collective-permute-start.34 = (bf16[64,512]{1,0:T(8,128)(2,1)S(1)}, bf16[64,512]{1,0:T(8,128)(2,1)S(1)}, u32[]{:S(2)}, u32[]{:S(2)}) collective-permute-start(bf16[64,512]{1,0:T(8,128)(2,1)S(1)} %get-tuple-element.169), channel_id=1, source_target_pairs={{0,8},{4,12},{8,16},{12,20},{16,24},{20,28},{24,0},{28,4},{1,9},{5... | collective-permute-start | bytes 196616 | tf_op jit(solution)/shard_map/ppermute | solution.py:366
  (13 other events, 39.4 us)

commit v3 on v2

--- a/solution.py
+++ b/solution.py
@@ -561,13 +561,11 @@
     bg, row_low = after((bg, row_low), row_across)
     low_sib, low_across = over_core(row_low), over_y(row_low)
     grads_one = after(grads_one, far[1])
-    result = put(BF, [row, row_sib], 0, where)
-    result = put(result, [row_across, over_core(row_across)], 2, where)
+    result = put(BF, [row, row_sib, row_across, over_core(row_across)], 0, where)
     send_one = scatter_start(grads_one)
     far_one = over_x(send_one)
     low_far = over_core(after(low_across, far_one))
-    bg = put(F32, [bg, low_sib], 0, where)
-    blocks_grad = put(bg, [low_across, low_far], 2, where)
+    blocks_grad = put(F32, [bg, low_sib, low_across, low_far], 0, where)
 
     got = over_core(near_sib)
     kept_one, send_one_y = scatter_next(grads_one, far_one)
@@ -593,7 +591,7 @@
         functools.partial(feed_update_kernel, count),
         quad((rows, cols)) * 2,
         [
-            *terms_two,
+            *after(terms_two, blocks_grad),
             gains_master,
             expand_master,
             expand_first,

time: 149 us -> 146 us (0.980)
  waiting for transfers between devices: 52.4 us -> 50.8 us
  Pallas kernels: 42.3 us -> 40.7 us
    ppermute x11, waiting for transfers between devices: 6.21 us -> 3.87 us  [over_z(): return lax.ppermute(value, 'dp', [(i, (i + 2 * k) % n) for i in range(n)])]
    pallas_call x4 -> x2, Pallas kernels: 7.07 us -> 5.42 us  [put(): pl.pallas_call(functools.partial(put_kernel, len(messages)), out_shape=st...]
  transfers between devices with their start and end apart: 41 -> 41, of which waited for: 13 -> 12; matrix products, arithmetic and copies ran while one was open for 3% -> 3% of each run, Pallas kernels for 20% -> 19%
where the time goes in v3:
time: 146 us
  waiting for transfers between devices  50.8 us (35%)
  starting transfers between devices  46.4 us (32%)
  Pallas kernels  40.7 us (28%)
  other arithmetic  3.59 us (2%)
  local copies, waits for them, and re-layouts  3.14 us (2%)
  between operations  1.46 us (1%)
    pallas_call x7, Pallas kernels, call(): pl.pallas_call(body, out_shape=outs, in_specs=[pl.BlockSpec(memory_space=...  35.3 us
    ppermute x11, starting transfers between devices, over_z(): return lax.ppermute(value, 'dp', [(i, (i + 2 * k) % n) for i in range(n)])  23.9 us
    ppermute x6, waiting for transfers between devices, two_ways(): lax.ppermute(value, ('dp', 'mp'), [(source, dp * 4 + mp) for source, (dp,...  23.2 us
    ppermute x5, waiting for transfers between devices, over_y(): return lax.ppermute(value, 'mp', [(i, i ^ 2) for i in range(4)])  11.8 us
    ppermute x6, starting transfers between devices, two_ways(): lax.ppermute(value, ('dp', 'mp'), [(source, dp * 4 + mp) for source, (dp,...  9.71 us
    ppermute x3, waiting for transfers between devices, over_x(): return lax.ppermute(value, 'dp', [(i, i ^ 1) for i in range(n)])  7.51 us
    ppermute x5, starting transfers between devices, over_y(): return lax.ppermute(value, 'mp', [(i, i ^ 2) for i in range(4)])  6.28 us
    pallas_call x2, Pallas kernels, put(): pl.pallas_call(functools.partial(put_kernel, len(messages)), out_shape=st...  5.42 us
  transfers between devices with their start and end apart: 41, of which 12 were waited for; matrix products, arithmetic and copies ran while one was open for 3% of the time, Pallas kernels for 19%

profile of v3, /device:TPU:0, one launch (start us, length us, event | category | flops | bytes accessed | tf_op | source)
XLA Modules:
  0.0 146.0 jit_solution(17988553475705793510)
XLA Ops:
  1.3 3.2 %shard_map.345 = (bf16[64,1536]{1,0:T(8,128)(2,1)}, bf16[64,512]{1,0:T(8,128)(2,1)}, bf16[64,1024]{1,0:T(8,128)(2,1)}, bf16[512,512]{1,0:T(8,128)(2,1)}, bf16[512,512]{1,0:T(8,128)(2,1)}) custom-call(s32[3]{0:T(128)} %pad_add_fusion.place_ref, f32[2,64]{1,0:T(2,128)} %refs_4_.1, f32[3,64,128]{2,1,0:T(8,128)} %refs_7_.1, f32[64,128]{1,0:T(8,128)} %bitcast.58, ...), custom_call_target="tpu_custom_call" | custom-call | bytes 2097152 | tf_op jit(solution)/shard_map/pallas_call | solution.py:39
  4.5 4.1 %collective-permute-start.1 = (bf16[64,512]{1,0:T(8,128)(2,1)}, bf16[64,512]{1,0:T(8,128)(2,1)S(1)}, u32[]{:S(2)}, u32[]{:S(2)}) collective-permute-start(bf16[64,512]{1,0:T(8,128)(2,1)} %get-tuple-element.99), channel_id=1, source_target_pairs={{0,16},{4,20},{8,24},{12,28},{16,0},{20,4},{24,8},{28,12},{1,17},{... | collective-permute-start | bytes 196616 | tf_op jit(solution)/shard_map/ppermute | solution.py:366
  8.7 0.8 constant_dynamic-update-slice_fusion.4
  9.5 0.9 constant_dynamic-update-slice_fusion.9
  10.5 0.9 pad_maximum_fusion.3
  11.3 1.9 %collective-permute-start.2 = (bf16[128,512]{1,0:T(8,128)(2,1)S(1)}, bf16[128,512]{1,0:T(8,128)(2,1)S(1)}, u32[]{:S(2)}, u32[]{:S(2)}) collective-permute-start(bf16[128,512]{1,0:T(8,128)(2,1)S(1)} %pad_maximum_fusion.3), channel_id=1, source_target_pairs={{0,8},{1,25},{2,10},{3,27},{4,12},{5,29},{6,14},{7,31},{8,16},{9,1... | collective-permute-start | bytes 393224 | tf_op jit(solution)/shard_map/ppermute | solution.py:380
  13.2 0.9 pad_maximum_fusion.1
  14.2 1.6 %collective-permute-start.9 = (bf16[128,1024]{1,0:T(8,128)(2,1)S(1)}, bf16[128,1024]{1,0:T(8,128)(2,1)S(1)}, u32[]{:S(2)}, u32[]{:S(2)}) collective-permute-start(bf16[128,1024]{1,0:T(8,128)(2,1)S(1)} %pad_maximum_fusion.1), channel_id=1, source_target_pairs={{0,8},{1,25},{2,10},{3,27},{4,12},{5,29},{6,14},{7,31},{8,16},{9,1... | collective-permute-start | bytes 786440 | tf_op jit(solution)/shard_map/ppermute | solution.py:380
  15.8 3.8 %collective-permute-done.2 = bf16[128,512]{1,0:T(8,128)(2,1)S(1)} collective-permute-done((bf16[128,512]{1,0:T(8,128)(2,1)S(1)}, bf16[128,512]{1,0:T(8,128)(2,1)S(1)}, u32[]{:S(2)}, u32[]{:S(2)}) %collective-permute-start.2) | collective-permute-done | bytes 131104 | tf_op jit(solution)/shard_map/ppermute | solution.py:380
  19.8 1.4 collective-permute-done.3
  21.1 2.0 %collective-permute-start.4 = (bf16[512,512]{1,0:T(8,128)(2,1)S(1)}, bf16[512,512]{1,0:T(8,128)(2,1)S(1)}, u32[]{:S(2)}, u32[]{:S(2)}) collective-permute-start(bf16[512,512]{1,0:T(8,128)(2,1)S(1)} %constant_dynamic-update-slice_fusion.refs_0_), channel_id=1, source_target_pairs={{0,4},{1,3},{2,6},{3,1},{4,0},{5,7},{6,2},{7,5},{8,12},{9,11},{10,... | collective-permute-start | bytes 1572872 | tf_op jit(solution)/shard_map/ppermute | solution.py:380
  23.1 2.1 %collective-permute-done.9 = bf16[128,1024]{1,0:T(8,128)(2,1)S(1)} collective-permute-done((bf16[128,1024]{1,0:T(8,128)(2,1)S(1)}, bf16[128,1024]{1,0:T(8,128)(2,1)S(1)}, u32[]{:S(2)}, u32[]{:S(2)}) %collective-permute-start.9) | collective-permute-done | bytes 262176 | tf_op jit(solution)/shard_map/ppermute | solution.py:380
  25.6 1.4 collective-permute-done.10
  27.0 3.3 %collective-permute-done.4.refs_1_ = bf16[512,512]{1,0:T(8,128)(2,1)S(1)} collective-permute-done((bf16[512,512]{1,0:T(8,128)(2,1)S(1)}, bf16[512,512]{1,0:T(8,128)(2,1)S(1)}, u32[]{:S(2)}, u32[]{:S(2)}) %collective-permute-start.4) | collective-permute-done | bytes 524320 | tf_op jit(solution)/shard_map/ppermute | solution.py:380
  30.4 1.9 %collective-permute-start.11 = (bf16[512,1024]{1,0:T(8,128)(2,1)S(1)}, bf16[512,1024]{1,0:T(8,128)(2,1)S(1)}, u32[]{:S(2)}, u32[]{:S(2)}) collective-permute-start(bf16[512,1024]{1,0:T(8,128)(2,1)S(1)} %constant_dynamic-update-slice_fusion.5.refs_0_), channel_id=1, source_target_pairs={{0,4},{1,3},{2,6},{3,1},{4,0},{5,7},{6,2},{7,5},{8,12},{9,11},{10,... | collective-permute-start | bytes 3145736 | tf_op jit(solution)/shard_map/ppermute | solution.py:380
  32.3 1.6 %collective-permute-start.6 = (bf16[512,256]{1,0:T(8,128)(2,1)S(1)}, bf16[512,256]{1,0:T(8,128)(2,1)S(1)}, u32[]{:S(2)}, u32[]{:S(2)}) collective-permute-start(bf16[512,256]{1,0:T(8,128)(2,1)S(1)} %constant_dynamic-slice_fusion.1), channel_id=1, source_target_pairs={{0,2},{1,5},{2,0},{3,7},{4,6},{5,1},{6,4},{7,3},{8,10},{9,13},{10,... | collective-permute-start | bytes 786440 | tf_op jit(solution)/shard_map/ppermute | solution.py:380
  33.9 7.7 %collective-permute-done.6.refs_3_ = bf16[512,256]{1,0:T(8,128)(2,1)S(1)} collective-permute-done((bf16[512,256]{1,0:T(8,128)(2,1)S(1)}, bf16[512,256]{1,0:T(8,128)(2,1)S(1)}, u32[]{:S(2)}, u32[]{:S(2)}) %collective-permute-start.6) | collective-permute-done | bytes 262176 | tf_op jit(solution)/shard_map/ppermute | solution.py:380
  41.7 6.3 %collective-permute-done.11.refs_1_ = bf16[512,1024]{1,0:T(8,128)(2,1)S(1)} collective-permute-done((bf16[512,1024]{1,0:T(8,128)(2,1)S(1)}, bf16[512,1024]{1,0:T(8,128)(2,1)S(1)}, u32[]{:S(2)}, u32[]{:S(2)}) %collective-permute-start.11) | collective-permute-done | bytes 1048608 | tf_op jit(solution)/shard_map/ppermute | solution.py:380
  48.0 0.7 collective-permute-start.13
  48.8 1.0 copy-done.16
  49.8 8.6 %shard_map.346 = (f32[512,512]{1,0:T(8,128)S(1)}, bf16[512,512]{1,0:T(8,128)(2,1)S(1)}, bf16[512,512]{1,0:T(8,128)(2,1)S(1)}, bf16[512,512]{1,0:T(8,128)(2,1)S(1...) custom-call(s32[3]{0:T(128)S(1)} %copy-done.12, ...), custom_call_target="tpu_custom_call" | custom-call | flops 6000000000 | bytes 12582912 | tf_op jit(solution)/shard_map/pallas_call | solution.py:39
  59.0 1.5 %collective-permute-done.14.refs_4_ = bf16[512,512]{1,0:T(8,128)(2,1)S(1)} collective-permute-done((bf16[512,512]{1,0:T(8,128)(2,1)S(1)}, bf16[512,512]{1,0:T(8,128)(2,1)S(1)}, u32[]{:S(2)}, u32[]{:S(2)}) %collective-permute-start.14) | collective-permute-done | bytes 524320 | tf_op jit(solution)/shard_map/ppermute | solution.py:374
  60.5 7.8 %shard_map.347 = (bf16[2,256,512]{2,1,0:T(8,128)(2,1)S(1)}, bf16[2,256,512]{2,1,0:T(8,128)(2,1)S(1)}, bf16[2,256,512]{2,1,0:T(8,128)(2,1)S(1)}, bf16[2,256,512]{...) custom-call(s32[3]{0:T(128)S(1)} %copy-done.12, ...), custom_call_target="tpu_custom_call" | custom-call | flops 4000000000 | bytes 12582912 | tf_op jit(solution)/shard_map/pallas_call | solution.py:39
  68.9 1.4 collective-permute-start.16
  70.5 1.9 %collective-permute-start.22 = (bf16[2,256,512]{2,1,0:T(8,128)(2,1)S(1)}, bf16[2,256,512]{2,1,0:T(8,128)(2,1)S(1)}, u32[]{:S(2)}, u32[]{:S(2)}) collective-permute-start(bf16[2,256,512]{2,1,0:T(8,128)(2,1)S(1)} %add_convert_fusion.1), channel_id=1, source_target_pairs={{0,4},{4,0},{8,12},{12,8},{16,20},{20,16},{24,28},{28,24},{1,5},{5... | collective-permute-start | bytes 1572872 | tf_op jit(solution)/shard_map/ppermute | solution.py:361
  72.5 3.2 %shard_map.349 = (bf16[2,2,256,512]{3,2,1,0:T(8,128)(2,1)S(1)}, bf16[2,2,256,512]{3,2,1,0:T(8,128)(2,1)S(1)}, f32[512,512]{1,0:T(8,128)S(1)}, f32[8,512]{1,0:T(8,128)S(1)}) custom-call(s32[3]{0:T(128)S(1)} %copy-done.12, f32[512,512]{1,0:T(8,128)S(1)} %get-tuple-element.101.h_ref, bf16[512,2048]{1,0:T(8,128)(2,1)S(1)} %get-tuple-element.112.g_ref, ...), custom_call_target="tpu_custom_call" | custom-call | flops 4000000000 | bytes 12582912 | tf_op jit(solution)/shard_map/pallas_call | solution.py:39
  75.8 9.3 %shard_map.350 = (f32[512,512]{1,0:T(8,128)S(1)}, bf16[512,512]{1,0:T(8,128)(2,1)S(1)}, bf16[2,272,512]{2,1,0:T(8,128)(2,1)S(1)}, bf16[2,272,512]{2,1,0:T(8,128)...) custom-call(s32[3]{0:T(128)S(1)} %copy-done.12, bf16[512,512]{1,0:T(8,128)(2,1)S(1)} %copy-done.17, ...), custom_call_target="tpu_custom_call" | custom-call | flops 8000000000 | bytes 12582912 | tf_op jit(solution)/shard_map/pallas_call | solution.py:39
  86.2 0.8 collective-permute-start.32
  86.9 1.5 %collective-permute-start.21 = (bf16[512,512]{1,0:T(8,128)(2,1)S(1)}, bf16[512,512]{1,0:T(8,128)(2,1)S(1)}, u32[]{:S(2)}, u32[]{:S(2)}) collective-permute-start(bf16[512,512]{1,0:T(8,128)(2,1)S(1)} %get-tuple-element.128), channel_id=1, source_target_pairs={{0,2},{1,3},{2,0},{3,1},{4,6},{5,7},{6,4},{7,5},{8,10},{9,11},{10,... | collective-permute-start | bytes 1572872 | tf_op jit(solution)/shard_map/ppermute | solution.py:370
  88.7 1.1 collective-permute-start.37
  89.9 1.1 collective-permute-start.24
  91.0 2.4 %shard_map.348 = bf16[4,512,512]{2,1,0:T(8,128)(2,1)} custom-call(s32[3]{0:T(128)S(1)} %copy-done.12, bf16[512,512]{1,0:T(8,128)(2,1)S(1)} %get-tuple-element.106.refs_0_, bf16[512,512]{1,0:T(8,128)(2,1)S(1)} %collective-permute-done.15.refs_1_, bf16[512,512]{1,0:T(8,128)(2,1)S(1)} %collective-permute-done.16.refs_2_, ...), custom_call_target="tpu_custom_call" | custom-call | bytes 4194304 | tf_op jit(solution)/shard_map/pallas_call | solution.py:426
  93.4 7.5 %collective-permute-done.32 = bf16[2,256,512]{2,1,0:T(8,128)(2,1)S(1)} collective-permute-done((bf16[2,256,512]{2,1,0:T(8,128)(2,1)S(1)}, bf16[2,256,512]{2,1,0:T(8,128)(2,1)S(1)}, u32[]{:S(2)}, u32[]{:S(2)}) %collective-permute-start.32) | collective-permute-done | bytes 524320 | tf_op jit(solution)/shard_map/ppermute | solution.py:361
  100.9 5.7 %collective-permute-done.37 = bf16[256,512]{1,0:T(8,128)(2,1)S(1)} collective-permute-done((bf16[256,512]{1,0:T(8,128)(2,1)S(1)}, bf16[256,512]{1,0:T(8,128)(2,1)S(1)}, u32[]{:S(2)}, u32[]{:S(2)}) %collective-permute-start.37) | collective-permute-done | bytes 262176 | tf_op jit(solution)/shard_map/ppermute | solution.py:370
  106.9 1.6 %collective-permute-start.33 = (bf16[256,512]{1,0:T(8,128)(2,1)S(1)}, bf16[256,512]{1,0:T(8,128)(2,1)S(1)}, u32[]{:S(2)}, u32[]{:S(2)}) collective-permute-start(bf16[256,512]{1,0:T(8,128)(2,1)S(1)} %get-tuple-element.140), channel_id=1, source_target_pairs={{0,2},{1,3},{2,0},{3,1},{4,6},{5,7},{6,4},{7,5},{8,10},{9,11},{10,... | collective-permute-start | bytes 786440 | tf_op jit(solution)/shard_map/ppermute | solution.py:370
  108.5 6.5 %collective-permute-start.40 = (bf16[64,512]{1,0:T(8,128)(2,1)S(1)}, bf16[64,512]{1,0:T(8,128)(2,1)S(1)}, u32[]{:S(2)}, u32[]{:S(2)}) collective-permute-start(bf16[64,512]{1,0:T(8,128)(2,1)S(1)} %get-tuple-element.179), channel_id=1, source_target_pairs={{0,24},{4,28},{8,0},{12,4},{16,8},{20,12},{24,16},{28,20},{1,25},{... | collective-permute-start | bytes 196616 | tf_op jit(solution)/shard_map/ppermute | solution.py:366
  115.0 1.2 collective-permute-start.38
  116.3 0.6 collective-permute-start.27
  117.1 6.1 %collective-permute-done.27 = bf16[272,512]{1,0:T(8,128)(2,1)S(1)} collective-permute-done((bf16[272,512]{1,0:T(8,128)(2,1)S(1)}, bf16[272,512]{1,0:T(8,128)(2,1)S(1)}, u32[]{:S(2)}, u32[]{:S(2)}) %collective-permute-start.27) | collective-permute-done | bytes 278560 | tf_op jit(solution)/shard_map/ppermute | solution.py:370
  123.5 4.6 %collective-permute-start.36 = (bf16[64,512]{1,0:T(8,128)(2,1)S(1)}, bf16[64,512]{1,0:T(8,128)(2,1)S(1)}, u32[]{:S(2)}, u32[]{:S(2)}) collective-permute-start(bf16[64,512]{1,0:T(8,128)(2,1)S(1)} %get-tuple-element.183), channel_id=1, source_target_pairs={{0,24},{4,28},{8,0},{12,4},{16,8},{20,12},{24,16},{28,20},{1,25},{... | collective-permute-start | bytes 196616 | tf_op jit(solution)/shard_map/ppermute | solution.py:366
  128.2 1.2 collective-permute-start.28
  129.4 2.7 %collective-permute-start.30 = (bf16[80,512]{1,0:T(8,128)(2,1)S(1)}, bf16[80,512]{1,0:T(8,128)(2,1)S(1)}, u32[]{:S(2)}, u32[]{:S(2)}) collective-permute-start(bf16[80,512]{1,0:T(8,128)(2,1)S(1)} %concatenate.42), channel_id=1, source_target_pairs={{0,24},{4,28},{8,0},{12,4},{16,8},{20,12},{24,16},{28,20},{1,25},{... | collective-permute-start | bytes 245768 | tf_op jit(solution)/shard_map/ppermute | solution.py:366
  132.1 1.1 collective-permute-start.35
  133.3 2.3 %collective-permute-start.34 = (bf16[64,512]{1,0:T(8,128)(2,1)S(1)}, bf16[64,512]{1,0:T(8,128)(2,1)S(1)}, u32[]{:S(2)}, u32[]{:S(2)}) collective-permute-start(bf16[64,512]{1,0:T(8,128)(2,1)S(1)} %get-tuple-element.185), channel_id=1, source_target_pairs={{0,8},{4,12},{8,16},{12,20},{16,24},{20,28},{24,0},{28,4},{1,9},{5... | collective-permute-start | bytes 196616 | tf_op jit(solution)/shard_map/ppermute | solution.py:366
  135.7 3.0 %shard_map.351 = f32[4,512,512]{2,1,0:T(8,128)} custom-call(s32[3]{0:T(128)S(1)} %copy-done.12, f32[512,512]{1,0:T(8,128)S(1)} %get-tuple-element.127.refs_0_, bf16[512,512]{1,0:T(8,128)(2,1)S(1)} %collective-permute-done.20.refs_1_, bf16[512,512]{1,0:T(8,128)(2,1)S(1)} %collective-permute-done.21.refs_2_, bf16[512,512]{1,0:T(8,128)(2,1)S(1)} %collective-permute-done.25.refs_3_), custom_call_target="tpu_custom_call" | custom-call | bytes 4194304 | tf_op jit(solution)/shard_map/pallas_call | solution.py:426
  138.7 3.8 %collective-permute-done.35.refs_2_ = bf16[64,512]{1,0:T(8,128)(2,1)S(1)} collective-permute-done((bf16[64,512]{1,0:T(8,128)(2,1)S(1)}, bf16[64,512]{1,0:T(8,128)(2,1)S(1)}, u32[]{:S(2)}, u32[]{:S(2)}) %collective-permute-start.35) | collective-permute-done | bytes 65568 | tf_op jit(solution)/shard_map/ppermute | solution.py:366
  142.6 1.7 %shard_map.352 = (f32[64,512]{1,0:T(8,128)}, f32[64,512]{1,0:T(8,128)}, f32[64,512]{1,0:T(8,128)}, bf16[64,512]{1,0:T(8,128)(2,1)}, f32[64,512]{1,0:T(8,128)}, /...) custom-call(s32[3]{0:T(128)S(1)} %copy-done.12, bf16[64,512]{1,0:T(8,128)(2,1)S(1)} %get-tuple-element.142.refs_0_, ...), custom_call_target="tpu_custom_call" | custom-call | bytes 3145728 | tf_op jit(solution)/shard_map/pallas_call | solution.py:39
  144.4 1.5 %shard_map.353 = (f32[3,64,128]{2,1,0:T(8,128)}, f32[3,64,128]{2,1,0:T(8,128)}, f32[3,64,128]{2,1,0:T(8,128)}, bf16[3,64,128]{2,1,0:T(8,128)(2,1)}, f32[64,128]{...) custom-call(s32[3]{0:T(128)S(1)} %copy-done.12, ...), custom_call_target="tpu_custom_call" | custom-call | bytes 3145728 | tf_op jit(solution)/shard_map/pallas_call | solution.py:39
  (114 shorter events, 5.1 us)
Async XLA Ops:
  4.5 11.3 %collective-permute-start.1 = (bf16[64,512]{1,0:T(8,128)(2,1)}, bf16[64,512]{1,0:T(8,128)(2,1)S(1)}, u32[]{:S(2)}, u32[]{:S(2)}) collective-permute-start(bf16[64,512]{1,0:T(8,128)(2,1)} %get-tuple-element.99), channel_id=1, source_target_pairs={{0,16},{4,20},{8,24},{12,28},{16,0},{20,4},{24,8},{28,12},{1,17},{... | collective-permute-start | bytes 196616 | tf_op jit(solution)/shard_map/ppermute | solution.py:366
  8.6 14.5 %collective-permute-start.8 = (bf16[64,1024]{1,0:T(8,128)(2,1)}, bf16[64,1024]{1,0:T(8,128)(2,1)S(1)}, u32[]{:S(2)}, u32[]{:S(2)}) collective-permute-start(bf16[64,1024]{1,0:T(8,128)(2,1)} %get-tuple-element.103), channel_id=1, source_target_pairs={{0,16},{4,20},{8,24},{12,28},{16,0},{20,4},{24,8},{28,12},{1,17},{... | collective-permute-start | bytes 393224 | tf_op jit(solution)/shard_map/ppermute | solution.py:366
  8.7 1.8 %collective-permute-start = (bf16[64,1536]{1,0:T(8,128)(2,1)}, bf16[64,1536]{1,0:T(8,128)(2,1)S(1)}, u32[]{:S(2)}, u32[]{:S(2)}) collective-permute-start(bf16[64,1536]{1,0:T(8,128)(2,1)} %get-tuple-element.100), channel_id=1, source_target_pairs={{0,1},{1,0},{2,3},{3,2},{4,5},{5,4},{6,7},{7,6},{8,9},{9,8},{10,11... | collective-permute-start | bytes 589832 | tf_op jit(solution)/shard_map/ppermute | solution.py:374
  11.3 8.3 %collective-permute-start.2 = (bf16[128,512]{1,0:T(8,128)(2,1)S(1)}, bf16[128,512]{1,0:T(8,128)(2,1)S(1)}, u32[]{:S(2)}, u32[]{:S(2)}) collective-permute-start(bf16[128,512]{1,0:T(8,128)(2,1)S(1)} %pad_maximum_fusion.3), channel_id=1, source_target_pairs={{0,8},{1,25},{2,10},{3,27},{4,12},{5,29},{6,14},{7,31},{8,16},{9,1... | collective-permute-start | bytes 393224 | tf_op jit(solution)/shard_map/ppermute | solution.py:380
  14.2 11.0 %collective-permute-start.9 = (bf16[128,1024]{1,0:T(8,128)(2,1)S(1)}, bf16[128,1024]{1,0:T(8,128)(2,1)S(1)}, u32[]{:S(2)}, u32[]{:S(2)}) collective-permute-start(bf16[128,1024]{1,0:T(8,128)(2,1)S(1)} %pad_maximum_fusion.1), channel_id=1, source_target_pairs={{0,8},{1,25},{2,10},{3,27},{4,12},{5,29},{6,14},{7,31},{8,16},{9,1... | collective-permute-start | bytes 786440 | tf_op jit(solution)/shard_map/ppermute | solution.py:380
  19.6 1.5 %collective-permute-start.3 = (bf16[192,512]{1,0:T(8,128)(2,1)S(1)}, bf16[192,512]{1,0:T(8,128)(2,1)S(1)}, u32[]{:S(2)}, u32[]{:S(2)}) collective-permute-start(bf16[192,512]{1,0:T(8,128)(2,1)S(1)} %pad_maximum_fusion.2), channel_id=1, source_target_pairs={{0,1},{1,0},{2,3},{3,2},{4,5},{5,4},{6,7},{7,6},{8,9},{9,8},{10,11... | collective-permute-start | bytes 589832 | tf_op jit(solution)/shard_map/ppermute | solution.py:374
  19.7 29.0 %copy-start.12 = (s32[3]{0:T(128)S(1)}, s32[3]{0:T(128)}, u32[]{:S(2)}) copy-start(s32[3]{0:T(128)} %pad_add_fusion.place_ref) | copy-start | bytes 40
  19.7 29.0 %copy-start.19 = (s32[4,512]{1,0:T(4,128)S(1)}, s32[4,512]{1,0:T(4,128)}, u32[]{:S(2)}) copy-start(s32[4,512]{1,0:T(4,128)} %seg_ref.1) | copy-start | bytes 24580
  21.1 9.2 %collective-permute-start.4 = (bf16[512,512]{1,0:T(8,128)(2,1)S(1)}, bf16[512,512]{1,0:T(8,128)(2,1)S(1)}, u32[]{:S(2)}, u32[]{:S(2)}) collective-permute-start(bf16[512,512]{1,0:T(8,128)(2,1)S(1)} %constant_dynamic-update-slice_fusion.refs_0_), channel_id=1, source_target_pairs={{0,4},{1,3},{2,6},{3,1},{4,0},{5,7},{6,2},{7,5},{8,12},{9,11},{10,... | collective-permute-start | bytes 1572872 | tf_op jit(solution)/shard_map/ppermute | solution.py:380
  25.2 1.8 %collective-permute-start.10 = (bf16[192,1024]{1,0:T(8,128)(2,1)S(1)}, bf16[192,1024]{1,0:T(8,128)(2,1)S(1)}, u32[]{:S(2)}, u32[]{:S(2)}) collective-permute-start(bf16[192,1024]{1,0:T(8,128)(2,1)S(1)} %pad_maximum_fusion), channel_id=1, source_target_pairs={{0,1},{1,0},{2,3},{3,2},{4,5},{5,4},{6,7},{7,6},{8,9},{9,8},{10,11... | collective-permute-start | bytes 1179656 | tf_op jit(solution)/shard_map/ppermute | solution.py:374
  30.4 17.6 %collective-permute-start.11 = (bf16[512,1024]{1,0:T(8,128)(2,1)S(1)}, bf16[512,1024]{1,0:T(8,128)(2,1)S(1)}, u32[]{:S(2)}, u32[]{:S(2)}) collective-permute-start(bf16[512,1024]{1,0:T(8,128)(2,1)S(1)} %constant_dynamic-update-slice_fusion.5.refs_0_), channel_id=1, source_target_pairs={{0,4},{1,3},{2,6},{3,1},{4,0},{5,7},{6,2},{7,5},{8,12},{9,11},{10,... | collective-permute-start | bytes 3145736 | tf_op jit(solution)/shard_map/ppermute | solution.py:380
  32.3 9.3 %collective-permute-start.6 = (bf16[512,256]{1,0:T(8,128)(2,1)S(1)}, bf16[512,256]{1,0:T(8,128)(2,1)S(1)}, u32[]{:S(2)}, u32[]{:S(2)}) collective-permute-start(bf16[512,256]{1,0:T(8,128)(2,1)S(1)} %constant_dynamic-slice_fusion.1), channel_id=1, source_target_pairs={{0,2},{1,5},{2,0},{3,7},{4,6},{5,1},{6,4},{7,3},{8,10},{9,13},{10,... | collective-permute-start | bytes 786440 | tf_op jit(solution)/shard_map/ppermute | solution.py:380
  33.9 14.8 %collective-permute-start.5 = (bf16[512,512]{1,0:T(8,128)(2,1)S(1)}, bf16[512,512]{1,0:T(8,128)(2,1)}, u32[]{:S(2)}, u32[]{:S(2)}) collective-permute-start(bf16[512,512]{1,0:T(8,128)(2,1)S(1)} %collective-permute-done.4.refs_1_), channel_id=1, source_target_pairs={{0,1},{1,0},{2,3},{3,2},{4,5},{5,4},{6,7},{7,6},{8,9},{9,8},{10,11... | collective-permute-start | bytes 1572872 | tf_op jit(solution)/shard_map/ppermute | solution.py:374
  41.7 7.1 %collective-permute-start.7 = (bf16[512,256]{1,0:T(8,128)(2,1)S(1)}, bf16[512,256]{1,0:T(8,128)(2,1)}, u32[]{:S(2)}, u32[]{:S(2)}) collective-permute-start(bf16[512,256]{1,0:T(8,128)(2,1)S(1)} %collective-permute-done.6.refs_3_), channel_id=1, source_target_pairs={{0,1},{1,0},{2,3},{3,2},{4,5},{5,4},{6,7},{7,6},{8,9},{9,8},{10,11... | collective-permute-start | bytes 786440 | tf_op jit(solution)/shard_map/ppermute | solution.py:374
  48.0 10.4 %collective-permute-start.13 = (bf16[512,512]{1,0:T(8,128)(2,1)S(1)}, bf16[512,512]{1,0:T(8,128)(2,1)S(1)}, u32[]{:S(2)}, u32[]{:S(2)}) collective-permute-start(bf16[512,512]{1,0:T(8,128)(2,1)S(1)} %constant_dynamic-slice_fusion), channel_id=1, source_target_pairs={{0,2},{1,5},{2,0},{3,7},{4,6},{5,1},{6,4},{7,3},{8,10},{9,13},{10,... | collective-permute-start | bytes 1572872 | tf_op jit(solution)/shard_map/ppermute | solution.py:380
  48.7 10.3 %collective-permute-start.12 = (bf16[512,1024]{1,0:T(8,128)(2,1)S(1)}, bf16[512,1024]{1,0:T(8,128)(2,1)S(1)}, u32[]{:S(2)}, u32[]{:S(2)}) collective-permute-start(bf16[512,1024]{1,0:T(8,128)(2,1)S(1)} %collective-permute-done.11.refs_1_), channel_id=1, source_target_pairs={{0,1},{1,0},{2,3},{3,2},{4,5},{5,4},{6,7},{7,6},{8,9},{9,8},{10,11... | collective-permute-start | bytes 3145736 | tf_op jit(solution)/shard_map/ppermute | solution.py:374
  58.4 2.1 %collective-permute-start.14 = (bf16[512,512]{1,0:T(8,128)(2,1)S(1)}, bf16[512,512]{1,0:T(8,128)(2,1)S(1)}, u32[]{:S(2)}, u32[]{:S(2)}) collective-permute-start(bf16[512,512]{1,0:T(8,128)(2,1)S(1)} %collective-permute-done.13.refs_3_), channel_id=1, source_target_pairs={{0,1},{1,0},{2,3},{3,2},{4,5},{5,4},{6,7},{7,6},{8,9},{9,8},{10,11... | collective-permute-start | bytes 1572872 | tf_op jit(solution)/shard_map/ppermute | solution.py:374
  68.3 2.0 %collective-permute-start.19 = (bf16[2,256,512]{2,1,0:T(8,128)(2,1)S(1)}, bf16[2,256,512]{2,1,0:T(8,128)(2,1)S(1)}, u32[]{:S(2)}, u32[]{:S(2)}) collective-permute-start(bf16[2,256,512]{2,1,0:T(8,128)(2,1)S(1)} %get-tuple-element.111), channel_id=1, source_target_pairs={{0,1},{1,0},{2,3},{3,2},{4,5},{5,4},{6,7},{7,6},{8,9},{9,8},{10,11... | collective-permute-start | bytes 1572872 | tf_op jit(solution)/shard_map/ppermute | solution.py:374
  68.7 3.6 %collective-permute-start.18 = (bf16[2,256,512]{2,1,0:T(8,128)(2,1)S(1)}, bf16[2,256,512]{2,1,0:T(8,128)(2,1)S(1)}, u32[]{:S(2)}, u32[]{:S(2)}) collective-permute-start(bf16[2,256,512]{2,1,0:T(8,128)(2,1)S(1)} %get-tuple-element.109), channel_id=1, source_target_pairs={{0,1},{1,0},{2,3},{3,2},{4,5},{5,4},{6,7},{7,6},{8,9},{9,8},{10,11... | collective-permute-start | bytes 1572872 | tf_op jit(solution)/shard_map/ppermute | solution.py:374
  68.9 16.9 %collective-permute-start.16 = (bf16[512,512]{1,0:T(8,128)(2,1)S(1)}, bf16[512,512]{1,0:T(8,128)(2,1)S(1)}, u32[]{:S(2)}, u32[]{:S(2)}) collective-permute-start(bf16[512,512]{1,0:T(8,128)(2,1)S(1)} %get-tuple-element.106.refs_0_), channel_id=1, source_target_pairs={{0,2},{1,3},{2,0},{3,1},{4,6},{5,7},{6,4},{7,5},{8,10},{9,11},{10,... | collective-permute-start | bytes 1572872 | tf_op jit(solution)/shard_map/ppermute | solution.py:370
  70.5 14.6 %collective-permute-start.22 = (bf16[2,256,512]{2,1,0:T(8,128)(2,1)S(1)}, bf16[2,256,512]{2,1,0:T(8,128)(2,1)S(1)}, u32[]{:S(2)}, u32[]{:S(2)}) collective-permute-start(bf16[2,256,512]{2,1,0:T(8,128)(2,1)S(1)} %add_convert_fusion.1), channel_id=1, source_target_pairs={{0,4},{4,0},{8,12},{12,8},{16,20},{20,16},{24,28},{28,24},{1,5},{5... | collective-permute-start | bytes 1572872 | tf_op jit(solution)/shard_map/ppermute | solution.py:361
  75.7 11.2 %collective-permute-start.31 = (bf16[2,2,256,512]{3,2,1,0:T(8,128)(2,1)S(1)}, bf16[2,2,256,512]{3,2,1,0:T(8,128)(2,1)S(1)}, u32[]{:S(2)}, u32[]{:S(2)}) collective-permute-start(bf16[2,2,256,512]{3,2,1,0:T(8,128)(2,1)S(1)} %get-tuple-element.139), channel_id=1, source_target_pairs={{0,1},{1,0},{2,3},{3,2},{4,5},{5,4},{6,7},{7,6},{8,9},{9,8},{10,11... | collective-permute-start | bytes 3145736 | tf_op jit(solution)/shard_map/ppermute | solution.py:374
  85.1 3.6 %collective-permute-start.23 = (bf16[2,272,512]{2,1,0:T(8,128)(2,1)S(1)}, bf16[2,272,512]{2,1,0:T(8,128)(2,1)S(1)}, u32[]{:S(2)}, u32[]{:S(2)}) collective-permute-start(bf16[2,272,512]{2,1,0:T(8,128)(2,1)S(1)} %get-tuple-element.134), channel_id=1, source_target_pairs={{0,1},{1,0},{2,3},{3,2},{4,5},{5,4},{6,7},{7,6},{8,9},{9,8},{10,11... | collective-permute-start | bytes 1671176 | tf_op jit(solution)/shard_map/ppermute | solution.py:374
  85.7 2.9 %collective-permute-start.15 = (bf16[512,512]{1,0:T(8,128)(2,1)S(1)}, bf16[512,512]{1,0:T(8,128)(2,1)S(1)}, u32[]{:S(2)}, u32[]{:S(2)}) collective-permute-start(bf16[512,512]{1,0:T(8,128)(2,1)S(1)} %get-tuple-element.106.refs_0_), channel_id=1, source_target_pairs={{0,1},{1,0},{2,3},{3,2},{4,5},{5,4},{6,7},{7,6},{8,9},{9,8},{10,11... | collective-permute-start | bytes 1572872 | tf_op jit(solution)/shard_map/ppermute | solution.py:374
  85.7 4.2 %collective-permute-start.17 = (bf16[512,512]{1,0:T(8,128)(2,1)S(1)}, bf16[512,512]{1,0:T(8,128)(2,1)S(1)}, u32[]{:S(2)}, u32[]{:S(2)}) collective-permute-start(bf16[512,512]{1,0:T(8,128)(2,1)S(1)} %collective-permute-done.16.refs_2_), channel_id=1, source_target_pairs={{0,1},{1,0},{2,3},{3,2},{4,5},{5,4},{6,7},{7,6},{8,9},{9,8},{10,11... | collective-permute-start | bytes 1572872 | tf_op jit(solution)/shard_map/ppermute | solution.py:374
  86.2 14.8 %collective-permute-start.32 = (bf16[2,256,512]{2,1,0:T(8,128)(2,1)S(1)}, bf16[2,256,512]{2,1,0:T(8,128)(2,1)S(1)}, u32[]{:S(2)}, u32[]{:S(2)}) collective-permute-start(bf16[2,256,512]{2,1,0:T(8,128)(2,1)S(1)} %add_convert_fusion.2), channel_id=1, source_target_pairs={{0,4},{4,0},{8,12},{12,8},{16,20},{20,16},{24,28},{28,24},{1,5},{5... | collective-permute-start | bytes 1572872 | tf_op jit(solution)/shard_map/ppermute | solution.py:361
  86.9 19.9 %collective-permute-start.21 = (bf16[512,512]{1,0:T(8,128)(2,1)S(1)}, bf16[512,512]{1,0:T(8,128)(2,1)S(1)}, u32[]{:S(2)}, u32[]{:S(2)}) collective-permute-start(bf16[512,512]{1,0:T(8,128)(2,1)S(1)} %get-tuple-element.128), channel_id=1, source_target_pairs={{0,2},{1,3},{2,0},{3,1},{4,6},{5,7},{6,4},{7,5},{8,10},{9,11},{10,... | collective-permute-start | bytes 1572872 | tf_op jit(solution)/shard_map/ppermute | solution.py:370
  88.6 26.4 %collective-permute-start.26 = (bf16[2,272,512]{2,1,0:T(8,128)(2,1)S(1)}, bf16[2,272,512]{2,1,0:T(8,128)(2,1)S(1)}, u32[]{:S(2)}, u32[]{:S(2)}) collective-permute-start(bf16[2,272,512]{2,1,0:T(8,128)(2,1)S(1)} %get-tuple-element.137), channel_id=1, source_target_pairs={{0,1},{1,0},{2,3},{3,2},{4,5},{5,4},{6,7},{7,6},{8,9},{9,8},{10,11... | collective-permute-start | bytes 1671176 | tf_op jit(solution)/shard_map/ppermute | solution.py:374
  88.7 17.9 %collective-permute-start.37 = (bf16[256,512]{1,0:T(8,128)(2,1)S(1)}, bf16[256,512]{1,0:T(8,128)(2,1)S(1)}, u32[]{:S(2)}, u32[]{:S(2)}) collective-permute-start(bf16[256,512]{1,0:T(8,128)(2,1)S(1)} %fusion.1), channel_id=1, source_target_pairs={{0,2},{1,3},{2,0},{3,1},{4,6},{5,7},{6,4},{7,5},{8,10},{9,11},{10,... | collective-permute-start | bytes 786440 | tf_op jit(solution)/shard_map/ppermute | solution.py:370
  89.9 25.1 %collective-permute-start.24 = (bf16[2,272,512]{2,1,0:T(8,128)(2,1)S(1)}, bf16[2,272,512]{2,1,0:T(8,128)(2,1)S(1)}, u32[]{:S(2)}, u32[]{:S(2)}) collective-permute-start(bf16[2,272,512]{2,1,0:T(8,128)(2,1)S(1)} %add_convert_fusion), channel_id=1, source_target_pairs={{0,4},{4,0},{8,12},{12,8},{16,20},{20,16},{24,28},{28,24},{1,5},{5... | collective-permute-start | bytes 1671176 | tf_op jit(solution)/shard_map/ppermute | solution.py:361
  100.9 22.5 %collective-permute-start.20 = (bf16[512,512]{1,0:T(8,128)(2,1)S(1)}, bf16[512,512]{1,0:T(8,128)(2,1)S(1)}, u32[]{:S(2)}, u32[]{:S(2)}) collective-permute-start(bf16[512,512]{1,0:T(8,128)(2,1)S(1)} %get-tuple-element.128), channel_id=1, source_target_pairs={{0,1},{1,0},{2,3},{3,2},{4,5},{5,4},{6,7},{7,6},{8,9},{9,8},{10,11... | collective-permute-start | bytes 1572872 | tf_op jit(solution)/shard_map/ppermute | solution.py:374
  106.9 9.5 %collective-permute-start.33 = (bf16[256,512]{1,0:T(8,128)(2,1)S(1)}, bf16[256,512]{1,0:T(8,128)(2,1)S(1)}, u32[]{:S(2)}, u32[]{:S(2)}) collective-permute-start(bf16[256,512]{1,0:T(8,128)(2,1)S(1)} %get-tuple-element.140), channel_id=1, source_target_pairs={{0,2},{1,3},{2,0},{3,1},{4,6},{5,7},{6,4},{7,5},{8,10},{9,11},{10,... | collective-permute-start | bytes 786440 | tf_op jit(solution)/shard_map/ppermute | solution.py:370
  108.5 19.7 %collective-permute-start.40 = (bf16[64,512]{1,0:T(8,128)(2,1)S(1)}, bf16[64,512]{1,0:T(8,128)(2,1)S(1)}, u32[]{:S(2)}, u32[]{:S(2)}) collective-permute-start(bf16[64,512]{1,0:T(8,128)(2,1)S(1)} %get-tuple-element.179), channel_id=1, source_target_pairs={{0,24},{4,28},{8,0},{12,4},{16,8},{20,12},{24,16},{28,20},{1,25},{... | collective-permute-start | bytes 196616 | tf_op jit(solution)/shard_map/ppermute | solution.py:366
  115.0 13.2 %collective-permute-start.39 = (bf16[64,512]{1,0:T(8,128)(2,1)S(1)}, bf16[64,512]{1,0:T(8,128)(2,1)S(1)}, u32[]{:S(2)}, u32[]{:S(2)}) collective-permute-start(bf16[64,512]{1,0:T(8,128)(2,1)S(1)} %get-tuple-element.180), channel_id=1, source_target_pairs={{0,16},{4,20},{8,24},{12,28},{16,0},{20,4},{24,8},{28,12},{1,17},{... | collective-permute-start | bytes 196616 | tf_op jit(solution)/shard_map/ppermute | solution.py:366
  115.0 14.4 %collective-permute-start.38 = (bf16[64,512]{1,0:T(8,128)(2,1)S(1)}, bf16[64,512]{1,0:T(8,128)(2,1)S(1)}, u32[]{:S(2)}, u32[]{:S(2)}) collective-permute-start(bf16[64,512]{1,0:T(8,128)(2,1)S(1)} %get-tuple-element.181), channel_id=1, source_target_pairs={{0,8},{4,12},{8,16},{12,20},{16,24},{20,28},{24,0},{28,4},{1,9},{5... | collective-permute-start | bytes 196616 | tf_op jit(solution)/shard_map/ppermute | solution.py:366
  116.3 6.9 %collective-permute-start.27 = (bf16[272,512]{1,0:T(8,128)(2,1)S(1)}, bf16[272,512]{1,0:T(8,128)(2,1)S(1)}, u32[]{:S(2)}, u32[]{:S(2)}) collective-permute-start(bf16[272,512]{1,0:T(8,128)(2,1)S(1)} %fusion.6), channel_id=1, source_target_pairs={{0,2},{1,3},{2,0},{3,1},{4,6},{5,7},{6,4},{7,5},{8,10},{9,11},{10,... | collective-permute-start | bytes 835592 | tf_op jit(solution)/shard_map/ppermute | solution.py:370
  123.3 9.9 %collective-permute-start.25 = (bf16[512,512]{1,0:T(8,128)(2,1)S(1)}, bf16[512,512]{1,0:T(8,128)(2,1)S(1)}, u32[]{:S(2)}, u32[]{:S(2)}) collective-permute-start(bf16[512,512]{1,0:T(8,128)(2,1)S(1)} %collective-permute-done.21.refs_2_), channel_id=1, source_target_pairs={{0,1},{1,0},{2,3},{3,2},{4,5},{5,4},{6,7},{7,6},{8,9},{9,8},{10,11... | collective-permute-start | bytes 1572872 | tf_op jit(solution)/shard_map/ppermute | solution.py:374
  123.5 8.7 %collective-permute-start.36 = (bf16[64,512]{1,0:T(8,128)(2,1)S(1)}, bf16[64,512]{1,0:T(8,128)(2,1)S(1)}, u32[]{:S(2)}, u32[]{:S(2)}) collective-permute-start(bf16[64,512]{1,0:T(8,128)(2,1)S(1)} %get-tuple-element.183), channel_id=1, source_target_pairs={{0,24},{4,28},{8,0},{12,4},{16,8},{20,12},{24,16},{28,20},{1,25},{... | collective-permute-start | bytes 196616 | tf_op jit(solution)/shard_map/ppermute | solution.py:366
  128.1 16.1 %collective-permute-start.29 = (bf16[80,512]{1,0:T(8,128)(2,1)S(1)}, bf16[80,512]{1,0:T(8,128)(2,1)S(1)}, u32[]{:S(2)}, u32[]{:S(2)}) collective-permute-start(bf16[80,512]{1,0:T(8,128)(2,1)S(1)} %get-tuple-element.191), channel_id=1, source_target_pairs={{0,16},{4,20},{8,24},{12,28},{16,0},{20,4},{24,8},{28,12},{1,17},{... | collective-permute-start | bytes 245768 | tf_op jit(solution)/shard_map/ppermute | solution.py:366
  128.2 16.0 %collective-permute-start.28 = (bf16[80,512]{1,0:T(8,128)(2,1)S(1)}, bf16[80,512]{1,0:T(8,128)(2,1)S(1)}, u32[]{:S(2)}, u32[]{:S(2)}) collective-permute-start(bf16[80,512]{1,0:T(8,128)(2,1)S(1)} %get-tuple-element.192), channel_id=1, source_target_pairs={{0,8},{4,12},{8,16},{12,20},{16,24},{20,28},{24,0},{28,4},{1,9},{5... | collective-permute-start | bytes 245768 | tf_op jit(solution)/shard_map/ppermute | solution.py:366
  129.4 14.9 %collective-permute-start.30 = (bf16[80,512]{1,0:T(8,128)(2,1)S(1)}, bf16[80,512]{1,0:T(8,128)(2,1)S(1)}, u32[]{:S(2)}, u32[]{:S(2)}) collective-permute-start(bf16[80,512]{1,0:T(8,128)(2,1)S(1)} %concatenate.42), channel_id=1, source_target_pairs={{0,24},{4,28},{8,0},{12,4},{16,8},{20,12},{24,16},{28,20},{1,25},{... | collective-permute-start | bytes 245768 | tf_op jit(solution)/shard_map/ppermute | solution.py:366
  132.1 10.4 %collective-permute-start.35 = (bf16[64,512]{1,0:T(8,128)(2,1)S(1)}, bf16[64,512]{1,0:T(8,128)(2,1)S(1)}, u32[]{:S(2)}, u32[]{:S(2)}) collective-permute-start(bf16[64,512]{1,0:T(8,128)(2,1)S(1)} %get-tuple-element.184), channel_id=1, source_target_pairs={{0,16},{4,20},{8,24},{12,28},{16,0},{20,4},{24,8},{28,12},{1,17},{... | collective-permute-start | bytes 196616 | tf_op jit(solution)/shard_map/ppermute | solution.py:366
  133.2 11.1 %copy-start.2 = (f32[3,64,128]{2,1,0:T(8,128)S(1)}, f32[3,64,128]{2,1,0:T(8,128)}, u32[]{:S(2)}) copy-start(f32[3,64,128]{2,1,0:T(8,128)} %refs_7_.1) | copy-start | bytes 294916
  133.3 11.1 %copy-start.3 = (f32[128,64]{0,1:T(8,128)S(1)}, f32[128,64]{0,1:T(8,128)}, u32[]{:S(2)}) copy-start(f32[128,64]{0,1:T(8,128)} %param.24) | copy-start | bytes 98308
  133.3 11.1 %copy-start.8 = (f32[3,64,128]{2,1,0:T(8,128)S(1)}, f32[3,64,128]{2,1,0:T(8,128)}, u32[]{:S(2)}) copy-start(f32[3,64,128]{2,1,0:T(8,128)} %refs_8_.3) | copy-start | bytes 294916
  133.3 11.1 %copy-start.9 = (f32[3,64,128]{2,1,0:T(8,128)S(1)}, f32[3,64,128]{2,1,0:T(8,128)}, u32[]{:S(2)}) copy-start(f32[3,64,128]{2,1,0:T(8,128)} %refs_9_.3) | copy-start | bytes 294916
  133.3 11.1 %copy-start.10 = (f32[128,64]{0,1:T(8,128)S(1)}, f32[128,64]{0,1:T(8,128)}, u32[]{:S(2)}) copy-start(f32[128,64]{0,1:T(8,128)} %param.25) | copy-start | bytes 98308
  133.3 9.2 %collective-permute-start.34 = (bf16[64,512]{1,0:T(8,128)(2,1)S(1)}, bf16[64,512]{1,0:T(8,128)(2,1)S(1)}, u32[]{:S(2)}, u32[]{:S(2)}) collective-permute-start(bf16[64,512]{1,0:T(8,128)(2,1)S(1)} %get-tuple-element.185), channel_id=1, source_target_pairs={{0,8},{4,12},{8,16},{12,20},{16,24},{20,28},{24,0},{28,4},{1,9},{5... | collective-permute-start | bytes 196616 | tf_op jit(solution)/shard_map/ppermute | solution.py:366
  (13 other events, 113.6 us)
